TPU v7x, 128 devices: a whole 4x4x4 slice. The times are simulated.
128 devices in a mesh: tensor: 2 (over core), dp: 4 (over x), context: 16 (over z, y).
Axes of the slice: x: 4, y: 4, z: 4, core: 2. Of those that a mesh axis runs over, the one named last changes fastest.
Arguments:
- hidden_in: bfloat16 [16384, 1024], P(('dp', 'context'), 'tensor'), may hold values from -6 to 6
- segment_ids: int32 [16384], P(('dp', 'context')), may hold values from 0 to 2, as said below
- norm_gain: float32 [1024], replicated, may hold values from 0.25 to 1.75
- in_weight: bfloat16 [1024, 2, 2048], P(None, None, 'tensor'), may hold values from -0.1875 to 0.1875
- bc_weight: bfloat16 [1024, 2, 128], replicated, may hold values from -0.1875 to 0.1875
- step_weight: bfloat16 [1024, 32], P(None, 'tensor'), may hold values from -0.1875 to 0.1875
- conv_weight: float32 [4, 2048], P(None, 'tensor'), may hold values from -3 to 3
- conv_bias: float32 [2048], P('tensor'), may hold values from -3 to 3
- bc_conv_weight: float32 [4, 2, 128], replicated, may hold values from -3 to 3
- bc_conv_bias: float32 [2, 128], replicated, may hold values from -3 to 3
- step_bias: float32 [32], replicated, may hold values from -6.5 to -2.5
- decay_log: float32 [32], P('tensor'), may hold values from -1.5 to 2.5
- skip_gain: float32 [32], P('tensor'), may hold values from 0.5 to 2
- gate_gain: float32 [2048], P('tensor'), may hold values from 0.25 to 1.75
- out_weight: bfloat16 [2048, 1024], P('tensor'), may hold values from -0.125 to 0.125
- out_grad: bfloat16 [16384, 1024], P(('dp', 'context'), 'tensor'), may hold values from -6 to 6
Outputs:
- hidden_out: bfloat16 [16384, 1024], P(('dp', 'context'), 'tensor')
- hidden_grad: bfloat16 [16384, 1024], P(('dp', 'context'), 'tensor')
- grad_norm_gain: float32 [1024], P('tensor')
- grad_in_weight: float32 [1024, 2, 2048], P(None, None, 'tensor')
- grad_bc_weight: float32 [1024, 2, 128], P('tensor')
- grad_step_weight: float32 [1024, 32], P(None, 'tensor')
- grad_conv_weight: float32 [4, 2048], P(None, 'tensor')
- grad_conv_bias: float32 [2048], P('tensor')
- grad_bc_conv_weight: float32 [4, 2, 128], replicated
- grad_bc_conv_bias: float32 [2, 128], replicated
- grad_step_bias: float32 [32], P('tensor')
- grad_decay_log: float32 [32], P('tensor')
- grad_skip_gain: float32 [32], P('tensor')
- grad_gate_gain: float32 [2048], P('tensor')
- grad_out_weight: float32 [2048, 1024], P('tensor')
Inputs may be any that keep to these rules, and one draw needn't show every extreme that they name: `segment_ids`: each group of 4096 tokens (one index of dp) holds three documents with ids 0, 1, 2 in order, never falling; the first and the last are each 1 to 128 tokens long, so the middle one starts in the group's first context piece and ends in its last.
All inputs are finite; a program needn't handle non-finite values.
Results may differ from a plain program's by a relative error of at most 0.013.
Values may be sent and summed in bfloat16 or wider, within the bound.
No kernel may reach another device: no remote copies, remote signals or barrier semaphores. Data moves between devices by JAX's collectives and lax.ppermute only.
A program may use at most 128 MiB of HBM per device.

v0:
```python
import jax
import jax.numpy as jnp
from jax import lax
from jax.experimental import pallas as pl
from jax.experimental.pallas import tpu as pltpu
from jax.sharding import Mesh
from jax.sharding import PartitionSpec as P

D = 1024
HEAD = 64
STATE = 128
INNER = 2048
ROWS = 256
HEADS = 16
LOCAL = 1024
HALO = 16
EXT = ROWS + HALO
LANES = 128
PAIRS = LOCAL // LANES
CHUNK = 80
DEVICES = 64
CONTEXT = ("context_0", "context_1")
EVERYONE = ("dp", "context_0", "context_1")
EPSILON = 1e-05
f32 = jnp.float32
bf16 = jnp.bfloat16
HIGHEST = lax.Precision.HIGHEST


def mm(a, b):
    return lax.dot_general(a, b, (((1,), (0,)), ((), ())), preferred_element_type=f32)


def nt(a, b):
    return lax.dot_general(a, b, (((1,), (1,)), ((), ())), preferred_element_type=f32)


def tn(a, b):
    return lax.dot_general(a, b, (((0,), (0,)), ((), ())), preferred_element_type=f32)


def exact(a, b):
    return lax.dot_general(
        a, b, (((1,), (0,)), ((), ())), precision=HIGHEST, preferred_element_type=f32
    )


def whole(shape):
    return pl.BlockSpec(shape, lambda i: (0,) * len(shape), pipeline_mode=pl.Buffered(1))


def kernel_call(body, outs, args, scratch=(), flops=0, vmem=56):
    return pl.pallas_call(
        body,
        grid=(1,),
        out_shape=[jax.ShapeDtypeStruct(shape, kind) for shape, kind in outs],
        in_specs=[whole(a.shape) for a in args],
        out_specs=[whole(shape) for shape, _ in outs],
        scratch_shapes=list(scratch),
        compiler_params=pltpu.CompilerParams(vmem_limit_bytes=vmem * 1024 * 1024),
        cost_estimate=pl.CostEstimate(
            flops=flops,
            bytes_accessed=0,
            transcendentals=0,
        ),
    )(*args)


def lane_index(shape):
    return lax.broadcasted_iota(jnp.int32, shape, 1)


def row_index(shape):
    return lax.broadcasted_iota(jnp.int32, shape, 0)


def spread_pair(columns, pair):
    rows = columns.shape[0]
    first = jnp.broadcast_to(columns[:, 2 * pair : 2 * pair + 1], (rows, LANES))
    second = jnp.broadcast_to(columns[:, 2 * pair + 1 : 2 * pair + 2], (rows, LANES))
    return jnp.where(lane_index((rows, LANES)) < HEAD, first, second)


def pair_mask(documents, seg_row):
    shape = (ROWS, ROWS)
    causal = row_index(shape) >= lane_index(shape)
    columns = jnp.concatenate([documents, documents], axis=1)
    return jnp.where((columns == seg_row) & causal, 0.0, -1e30).astype(f32)


def decay_block(cum, cum_t, head, bias):
    return jnp.exp(cum[:, head : head + 1] - cum_t[head : head + 1, :] + bias)


def document_before():
    piece = lax.axis_index("context_0") * 4 + lax.axis_index("context_1")
    return jnp.where(piece > 0, 2.0, 0.0).astype(f32)


def documents_of(seg_ref):
    seg_row = seg_ref[...].astype(f32) + 1.0
    return seg_row, jnp.broadcast_to(seg_row, (LANES, ROWS)).T


def tap_masks_of(documents, ext_ref):
    ext_ref[:8, :] = jnp.full((8, LANES), document_before(), f32)
    ext_ref[8:, :] = documents
    return [(ext_ref[5 + k : 5 + k + ROWS, :] == documents).astype(f32) for k in range(3)]


def end_decay(cum, documents):
    last = (documents == documents[ROWS - 1 : ROWS, :]).astype(f32)
    return jnp.exp(cum[ROWS - 1 : ROWS, :] - cum) * last


def entry_decay(cum, documents):
    return jnp.exp(cum) * (documents == document_before()).astype(f32)


def to_lanes(values):
    rows, count = values.shape
    return jnp.concatenate([values, jnp.zeros((rows, LANES - count), f32)], axis=1)


def front_body(
    hidden_ref,
    halo_ref,
    gain_ref,
    win_ref,
    wbc_ref,
    wst_ref,
    taps_ref,
    bias_ref,
    bc_taps_ref,
    bc_bias_ref,
    seg_ref,
    step_bias_ref,
    decay_log_ref,
    normed_ref,
    joined_ref,
    pre_ref,
    gate_ref,
    b_ref,
    c_ref,
    step_ref,
    cum_ref,
    sig_ref,
    decay_ref,
    state_ref,
    ext_ref,
    wide_ref,
):
    gain = gain_ref[...]
    for source, start, rows in ((halo_ref, 0, HALO), (hidden_ref, HALO, ROWS)):
        values = source[...].astype(f32)
        scale = lax.rsqrt(jnp.sum(values * values, axis=1, keepdims=True) / D + EPSILON)
        normed_ref[start : start + rows, :] = (values * scale * gain).astype(bf16)
    normed_ext = normed_ref[...]
    normed = normed_ref[HALO:, :]
    joined_ref[:, :LOCAL] = mm(normed_ext, win_ref[:, :LOCAL])
    joined_ref[:, LOCAL:] = mm(normed_ext, wbc_ref[...])
    gate_ref[...] = mm(normed, win_ref[:, LOCAL:])
    wide_ref[...] = jnp.zeros_like(wide_ref)
    wide_ref[:, :HEADS] = wst_ref[...]
    both = step_bias_ref[...]
    first = lax.axis_index("tensor") == 0
    local_bias = jnp.where(first, both[:, :HEADS], both[:, HEADS:])
    raw = mm(normed, wide_ref[...]) + to_lanes(local_bias)
    step = jnp.maximum(raw, 0.0) + jnp.log1p(jnp.exp(-jnp.abs(raw)))
    decay = step * to_lanes(-jnp.exp(decay_log_ref[...]))
    tri = (row_index((ROWS, ROWS)) >= lane_index((ROWS, ROWS))).astype(f32)
    cum = exact(tri, decay)
    step_ref[...] = step
    cum_ref[...] = cum
    sig_ref[...] = jax.nn.sigmoid(raw)
    decay_ref[...] = decay
    _, documents = documents_of(seg_ref)
    tap_masks = tap_masks_of(documents, ext_ref)

    def conv(at, taps, bias):
        lanes = slice(at, at + LANES)
        total = jnp.broadcast_to(bias, (ROWS, LANES))
        for k in range(4):
            part = joined_ref[HALO - 3 + k : HALO - 3 + k + ROWS, lanes] * taps[k : k + 1]
            total = total + (part * tap_masks[k] if k < 3 else part)
        pre_ref[:, lanes] = total
        return total * jax.nn.sigmoid(total)

    b_low = conv(LOCAL, bc_taps_ref[:, :STATE], bc_bias_ref[:, :STATE]).astype(bf16)
    c_low = conv(LOCAL + STATE, bc_taps_ref[:, STATE:], bc_bias_ref[:, STATE:]).astype(bf16)
    b_ref[...] = b_low
    c_ref[...] = c_low
    gains = jnp.exp(cum[ROWS - 1 : ROWS, :])
    ended = step * end_decay(cum, documents)
    for pair in range(PAIRS):
        lanes = slice(pair * LANES, (pair + 1) * LANES)
        x = conv(pair * LANES, taps_ref[:, lanes], bias_ref[:, lanes])
        state = tn((x * spread_pair(ended, pair)).astype(bf16), b_low).astype(bf16)
        for side in range(2):
            head = 2 * pair + side
            state_ref[head, :HEAD, :] = state[side * HEAD : (side + 1) * HEAD, :]
            state_ref[head, HEAD:, :] = jnp.broadcast_to(
                gains[:, head : head + 1], (CHUNK - HEAD, STATE)
            ).astype(bf16)


def within_body(pre_ref, step_ref, cum_ref, b_ref, c_ref, seg_ref, skip_ref, within_ref):
    seg_row, documents = documents_of(seg_ref)
    products = nt(c_ref[...], b_ref[...])
    bias = pair_mask(documents, seg_row)
    step = step_ref[...]
    cum = cum_ref[...]
    cum_t = cum.T
    skip = skip_ref[...]
    first_half = lane_index((ROWS, LANES)) < HEAD
    for pair in range(PAIRS):
        lanes = slice(pair * LANES, (pair + 1) * LANES)
        pre = pre_ref[:, lanes]
        x = pre * jax.nn.sigmoid(pre)
        xs_low = (x * spread_pair(step, pair)).astype(bf16)
        sums = []
        for head in (2 * pair, 2 * pair + 1):
            block = (decay_block(cum, cum_t, head, bias) * products).astype(bf16)
            sums.append(mm(block, xs_low))
        within_ref[:, lanes] = (
            jnp.where(first_half, sums[0], sums[1]) + spread_pair(skip, pair) * x
        )


def scan_body(pieces_ref, start_ref):
    state = jnp.zeros((HEAD, STATE), f32)
    for k in range(16):
        start_ref[k] = state.astype(bf16)
        if k < 15:
            gain = pieces_ref[k, HEAD : HEAD + 16, :].astype(f32)[0:1, :]
            state = state * gain + pieces_ref[k, :HEAD, :].astype(f32)


def scan_back_body(pieces_ref, grads_ref, adjoint_ref):
    state = jnp.zeros((HEAD, STATE), f32)
    for k in reversed(range(16)):
        adjoint_ref[k] = state.astype(bf16)
        if k > 0:
            gain = pieces_ref[k, HEAD : HEAD + 16, :].astype(f32)[0:1, :]
            state = state * gain + grads_ref[k].astype(f32)


def mixed_body(
    within_ref, start_ref, c_ref, cum_ref, seg_ref, gate_ref, dg_ref, gain_ref, mixed_ref, sums_ref
):
    entry = entry_decay(cum_ref[...], documents_of(seg_ref)[1])
    c_low = c_ref[...]
    squares = jnp.zeros((ROWS, LANES), f32)
    dots = jnp.zeros((ROWS, LANES), f32)
    for pair in range(PAIRS):
        lanes = slice(pair * LANES, (pair + 1) * LANES)
        carried = nt(c_low, start_ref[lanes, :])
        mixed = within_ref[:, lanes] + spread_pair(entry, pair) * carried
        mixed_ref[:, lanes] = mixed
        gate = gate_ref[:, lanes]
        gated = mixed * (gate * jax.nn.sigmoid(gate))
        squares = squares + gated * gated
        dots = dots + gated * gain_ref[:, lanes] * dg_ref[:, lanes]
    lane = lane_index((ROWS, LANES))
    sums_ref[...] = jnp.where(
        lane == 0,
        jnp.sum(squares, axis=1, keepdims=True),
        jnp.where(lane == 1, jnp.sum(dots, axis=1, keepdims=True), 0.0),
    )


def gate_body(
    sums_ref,
    other_ref,
    mixed_ref,
    gate_ref,
    dg_ref,
    gain_ref,
    c_ref,
    cum_ref,
    seg_ref,
    gnorm_ref,
    d_mixed_ref,
    d_gate_ref,
    grad_gain_ref,
    d_start_ref,
):
    sums = sums_ref[...] + other_ref[...]
    rate = lax.rsqrt(sums[:, 0:1] / INNER + EPSILON)
    back = rate * rate * rate * sums[:, 1:2] / INNER
    rate = jnp.broadcast_to(rate, (ROWS, LANES))
    back = jnp.broadcast_to(back, (ROWS, LANES))
    entry = entry_decay(cum_ref[...], documents_of(seg_ref)[1])
    c_low = c_ref[...]
    for pair in range(PAIRS):
        lanes = slice(pair * LANES, (pair + 1) * LANES)
        mixed = mixed_ref[:, lanes]
        gate = gate_ref[:, lanes]
        gain = gain_ref[:, lanes]
        dg = dg_ref[:, lanes]
        sig = jax.nn.sigmoid(gate)
        silu = gate * sig
        gated = mixed * silu
        scaled = gated * rate
        gnorm_ref[:, lanes] = (scaled * gain).astype(bf16)
        grad_gain_ref[:, lanes] = jnp.sum(dg * scaled, axis=0, keepdims=True)
        d_gated = rate * gain * dg - gated * back
        d_mixed = d_gated * silu
        d_mixed_ref[:, lanes] = d_mixed
        d_gate_ref[:, lanes] = (d_gated * mixed * (sig + silu * (1.0 - sig))).astype(bf16)
        d_state = tn((d_mixed * spread_pair(entry, pair)).astype(bf16), c_low).astype(bf16)
        for side in range(2):
            d_start_ref[2 * pair + side] = d_state[side * HEAD : (side + 1) * HEAD, :]


def head_sums(values, pair):
    shape = (LANES, LANES)
    into = lane_index(shape) == 2 * pair + (row_index(shape) >= HEAD).astype(jnp.int32)
    into = into.astype(bf16)
    high = values.astype(bf16)
    low = (values - high.astype(f32)).astype(bf16)
    return mm(high, into) + mm(low, into)


def conv_back(d_pre, joined_ref, source, lanes, taps, masks, pad_ref, into):
    total = None
    sums = []
    for k in range(4):
        joined = joined_ref[HALO - 3 + k : HALO - 3 + k + ROWS, source]
        part = d_pre * masks[k] if k < 3 else d_pre
        sums.append(jnp.sum(part * joined, axis=0, keepdims=True))
        pad_ref[k, 24 : 24 + ROWS, :] = part * taps[k : k + 1]
        moved = pad_ref[k, 24 - 13 - k : 24 - 13 - k + EXT, :]
        total = moved if total is None else total + moved
    sums.append(jnp.sum(d_pre, axis=0, keepdims=True))
    into[:, lanes] = jnp.concatenate(sums + [jnp.zeros((3, LANES), f32)], axis=0)
    return total


def back_body(
    d_mixed_ref,
    pre_ref,
    joined_ref,
    within_ref,
    start_ref,
    adjoint_ref,
    b_ref,
    c_ref,
    step_ref,
    cum_ref,
    sig_ref,
    decay_ref,
    seg_ref,
    decay_log_ref,
    skip_ref,
    taps_ref,
    d_bc_ref,
    d_ext_ref,
    d_step_ref,
    conv_ref,
    skip_grad_ref,
    small_ref,
    ext_ref,
    pad_ref,
):
    seg_row, documents = documents_of(seg_ref)
    tap_masks = tap_masks_of(documents, ext_ref)
    pad_ref[...] = jnp.zeros_like(pad_ref)
    skips = skip_ref[...]
    cum = cum_ref[...]
    cum_t = cum.T
    step = step_ref[...]
    b_low = b_ref[...]
    c_low = c_ref[...]
    products = nt(c_low, b_low)
    bias = pair_mask(documents, seg_row)
    end = end_decay(cum, documents)
    entry = entry_decay(cum, documents)
    gains = jnp.exp(cum[ROWS - 1 : ROWS, :])
    first_half = lane_index((ROWS, LANES)) < HEAD
    lane = lane_index((1, LANES))
    d_products = jnp.zeros((ROWS, ROWS), f32)
    d_b = jnp.zeros((ROWS, STATE), f32)
    d_c = jnp.zeros((ROWS, STATE), f32)
    d_cum = jnp.zeros((ROWS, LANES), f32)
    d_step = jnp.zeros((ROWS, LANES), f32)
    d_last = jnp.zeros((8, LANES), f32)
    d_whole = jnp.zeros((1, LANES), f32)
    for pair in range(PAIRS):
        lanes = slice(pair * LANES, (pair + 1) * LANES)
        pre = pre_ref[:, lanes]
        sig = jax.nn.sigmoid(pre)
        x = pre * sig
        steps = spread_pair(step, pair)
        ends = spread_pair(end, pair)
        entries = spread_pair(entry, pair)
        skip = spread_pair(skips, pair)
        xs = x * steps
        xs_low = xs.astype(bf16)
        d_mixed = d_mixed_ref[:, lanes]
        dy_low = d_mixed.astype(bf16)
        zero = jnp.zeros_like(dy_low)
        parts = []
        for side in range(2):
            head = 2 * pair + side
            own = jnp.where(first_half if side == 0 else ~first_half, dy_low, zero)
            decays = decay_block(cum, cum_t, head, bias)
            d_products = d_products + decays * nt(own, xs_low)
            parts.append(tn((decays * products).astype(bf16), dy_low))
        d_xs = jnp.where(first_half, parts[0], parts[1])
        within = within_ref[:, lanes] - skip * x
        through = dy_low.astype(f32) * within - xs_low.astype(f32) * d_xs
        start_low = start_ref[lanes, :]
        adjoint_low = adjoint_ref[lanes, :]
        d_ended = nt(b_low, adjoint_low) * ends
        d_b = d_b + mm((xs * ends).astype(bf16), adjoint_low)
        at_end = xs * d_ended
        carried = nt(c_low, start_low) * entries
        d_c = d_c + mm((d_mixed * entries).astype(bf16), start_low)
        d_cum = d_cum + head_sums(through + d_mixed * carried - at_end, pair)
        d_xs = d_xs + d_ended
        d_step = d_step + head_sums(x * d_xs, pair)
        end_sum = jnp.sum(at_end, axis=0, keepdims=True)
        d_last = d_last + head_sums(jnp.broadcast_to(end_sum, (8, LANES)), pair)
        meeting = start_low.astype(f32) * adjoint_low.astype(f32)
        for side in range(2):
            whole = jnp.sum(
                jnp.sum(meeting[side * HEAD : (side + 1) * HEAD, :], axis=0, keepdims=True),
                axis=1,
                keepdims=True,
            )
            d_whole = d_whole + jnp.where(lane == 2 * pair + side, whole, 0.0)
        skip_grad_ref[:, lanes] = jnp.sum(d_mixed * x, axis=0, keepdims=True)
        d_pre = (steps * d_xs + skip * d_mixed) * (sig + x * (1.0 - sig))
        d_ext_ref[:, lanes] = conv_back(
            d_pre, joined_ref, lanes, lanes, taps_ref[:, lanes], tap_masks, pad_ref, conv_ref
        ).astype(bf16)
    d_products = d_products.astype(bf16)
    d_bc_ref[:, :STATE] = (d_b + tn(d_products, c_low)).astype(bf16)
    d_bc_ref[:, STATE:] = (d_c + mm(d_products, b_low)).astype(bf16)
    tri = (row_index((ROWS, ROWS)) <= lane_index((ROWS, ROWS))).astype(f32)
    d_decay = exact(tri, d_cum) + (d_last[0:1, :] + gains * d_whole)
    d_raw = (d_step + d_decay * to_lanes(-jnp.exp(decay_log_ref[...]))) * sig_ref[...]
    d_step_ref[...] = d_raw.astype(bf16)
    small_ref[...] = jnp.concatenate(
        [
            jnp.sum(d_raw, axis=0, keepdims=True),
            jnp.sum(d_decay * decay_ref[...], axis=0, keepdims=True),
            jnp.zeros((6, LANES), f32),
        ],
        axis=0,
    )


def bc_back_body(
    own_ref, other_ref, pre_ref, joined_ref, seg_ref, taps_ref, d_ext_ref, conv_ref, ext_ref, pad_ref
):
    _, documents = documents_of(seg_ref)
    tap_masks = tap_masks_of(documents, ext_ref)
    pad_ref[...] = jnp.zeros_like(pad_ref)
    for half in range(2):
        lanes = slice(half * LANES, (half + 1) * LANES)
        source = slice(LOCAL + half * LANES, LOCAL + (half + 1) * LANES)
        pre = pre_ref[:, source]
        sig = jax.nn.sigmoid(pre)
        d_act = own_ref[:, lanes].astype(f32) + other_ref[:, lanes].astype(f32)
        d_pre = d_act * (sig + pre * sig * (1.0 - sig))
        d_ext_ref[:, lanes] = conv_back(
            d_pre, joined_ref, source, lanes, taps_ref[:, lanes], tap_masks, pad_ref, conv_ref
        ).astype(bf16)


def terms_body(dx_ref, dz_ref, dst_ref, dbc_ref, win_ref, wst_ref, wbc_ref, out_ref):
    first = lax.axis_index("tensor") == 0
    dbc = dbc_ref[...]
    wbc = wbc_ref[...]
    half = jnp.where(first, dbc[:, :STATE], dbc[:, STATE:])
    weights = jnp.where(first, wbc[:, :STATE], wbc[:, STATE:])
    both = nt(dx_ref[...], win_ref[:, :LOCAL]) + nt(half, weights)
    out_ref[:HALO, :] = both[:HALO, :].astype(bf16)
    own = nt(dz_ref[...], win_ref[:, LOCAL:]) + nt(dst_ref[:, :HEADS], wst_ref[...])
    out_ref[HALO:, :] = (both[HALO:, :] + own).astype(bf16)


def hidden_body(
    hidden_ref, terms_ref, other_ref, returned_ref, gain_ref, out_grad_ref, grad_ref, gain_grad_ref
):
    values = hidden_ref[...].astype(f32)
    scale = lax.rsqrt(jnp.sum(values * values, axis=1, keepdims=True) / D + EPSILON)
    d_normed = terms_ref[HALO:, :].astype(f32) + other_ref[HALO:, :].astype(f32)
    tail = jnp.concatenate(
        [jnp.zeros((ROWS - HALO, D), f32), returned_ref[...].astype(f32)], axis=0
    )
    d_normed = d_normed + tail
    first = lax.axis_index("tensor") == 0
    half = D // 2
    grads = jnp.sum(d_normed * values * scale, axis=0, keepdims=True)
    gain_grad_ref[...] = jnp.where(first, grads[:, :half], grads[:, half:])
    scaled = d_normed * gain_ref[...]
    dots = jnp.sum(values * scaled, axis=1, keepdims=True)
    result = scale * scaled - values * (scale * scale * scale * dots / D)
    own = jnp.where(first, result[:, :half], result[:, half:])
    grad_ref[...] = (out_grad_ref[...].astype(f32) + own).astype(bf16)


def bundle_body(
    normed_ref,
    dx_ref,
    dbc_ref,
    dst_ref,
    conv_ref,
    bc_conv_ref,
    gate_gain_ref,
    norm_gain_ref,
    skip_ref,
    small_ref,
    bundle_ref,
):
    half = D // 2
    bundle_ref[:, :LOCAL] = tn(normed_ref[...], dx_ref[...]).astype(bf16)
    first = lax.axis_index("tensor") == 0
    share = jnp.where(first, normed_ref[:, :half], normed_ref[:, half:])
    bundle_ref[:half, LOCAL:] = tn(share, dbc_ref[...]).astype(bf16)
    steps = tn(dst_ref[...], normed_ref[HALO:, :])
    for part in range(4):
        at = half + part * HEADS
        bundle_ref[at : at + HEADS, LOCAL:] = steps[:HEADS, part * 256 : part * 256 + 256].astype(bf16)
    row = half + 4 * HEADS
    pieces = []
    for part in range(4):
        pieces.append(conv_ref[:, part * 256 : part * 256 + 256])
    pieces.append(bc_conv_ref[...])
    lone = [gate_gain_ref[:, part * 256 : part * 256 + 256] for part in range(4)]
    lone += [norm_gain_ref[:, part * 256 : part * 256 + 256] for part in range(2)]
    lone += [jnp.concatenate([small_ref[0:1, :], small_ref[1:2, :]], axis=1)]
    lone += [jnp.zeros((1, 256), f32)]
    pieces.append(jnp.concatenate(lone, axis=0))
    skips = skip_ref[...]
    pieces.append(
        jnp.concatenate(
            [skips[:, part * 256 : part * 256 + 256] for part in range(4)]
            + [jnp.zeros((4, 256), f32)],
            axis=0,
        )
    )
    pieces.append(jnp.zeros((8, 256), f32))
    bundle_ref[row : row + 64, LOCAL:] = jnp.concatenate(pieces, axis=0).astype(bf16)
    bundle_ref[row + 64 :, LOCAL:] = jnp.zeros((half - 4 * HEADS - 64, 256), bf16)


def total_body(received_ref, out_ref):
    total = jnp.zeros(received_ref.shape[1:], f32)
    for k in range(DEVICES):
        total = total + received_ref[k].astype(f32)
    total = total.astype(bf16)
    for k in range(DEVICES):
        out_ref[k] = total


def few_body(
    final_ref,
    bc_ref,
    step_ref,
    conv_ref,
    conv_bias_ref,
    bc_conv_ref,
    bc_conv_bias_ref,
    gate_gain_ref,
    norm_gain_ref,
    skip_ref,
    step_bias_ref,
    decay_log_ref,
):
    half = D // 2
    grads = final_ref[:half, LOCAL:].astype(f32)
    bc_ref[:, 0, :] = grads[:, :STATE]
    bc_ref[:, 1, :] = grads[:, STATE:]
    rest = final_ref[half : half + 128, LOCAL:].astype(f32)
    steps = jnp.concatenate([rest[part * HEADS : (part + 1) * HEADS] for part in range(4)], axis=1)
    steps = jnp.concatenate([steps, jnp.zeros((LANES - HEADS, D), f32)], axis=0)
    step_ref[...] = steps.T[:, :HEADS]
    conv = jnp.concatenate([rest[64 + part * 8 : 72 + part * 8] for part in range(4)], axis=1)
    conv_ref[...] = conv[:4]
    conv_bias_ref[...] = conv[4:5]
    bc = rest[96:104]
    for side in range(2):
        lanes = slice(side * STATE, (side + 1) * STATE)
        bc_conv_ref[:, side, :] = bc[:4, lanes]
        bc_conv_bias_ref[side : side + 1, :] = bc[4:5, lanes]
    lone = rest[104:112]
    gate_gain_ref[...] = jnp.concatenate([lone[part : part + 1] for part in range(4)], axis=1)
    norm_gain_ref[...] = jnp.concatenate([lone[part : part + 1] for part in range(4, 6)], axis=1)
    step_bias_ref[...] = lone[6:7, :HEADS]
    decay_log_ref[...] = lone[6:7, LANES : LANES + HEADS]
    skips = rest[112:116]
    total = jnp.zeros((1, LANES), f32)
    lane = lane_index((1, LANES))
    for head in range(HEADS):
        at = (head % 4) * HEAD
        own = jnp.sum(
            skips[head // 4 : head // 4 + 1, at : at + HEAD], axis=1, keepdims=True
        )
        total = total + jnp.where(lane == head, own, 0.0)
    skip_ref[...] = total[:, :HEADS]


def large_body(final_ref, gate_ref, grad_in_ref):
    grad_in_ref[:, 0, :] = final_ref[:, :LOCAL].astype(f32)
    grad_in_ref[:, 1, :] = gate_ref[...]


def swapped(values):
    return lax.ppermute(values, "tensor", [(0, 1), (1, 0)])


def shards(
    hidden_in,
    segment_ids,
    norm_gain,
    in_weight,
    bc_weight,
    step_weight,
    conv_weight,
    conv_bias,
    bc_conv_weight,
    bc_conv_bias,
    step_bias,
    decay_log,
    skip_gain,
    gate_gain,
    out_weight,
    out_grad,
):
    side = lax.axis_index("tensor")
    width = hidden_in.shape[1]
    gathered = lax.all_gather(hidden_in, "tensor", axis=1, tiled=True)
    halo = lax.ppermute(gathered[ROWS - HALO :], CONTEXT, [(i, i + 1) for i in range(15)])
    cotangent = lax.all_gather(out_grad, "tensor", axis=1, tiled=True)
    win = in_weight.reshape(D, 2 * LOCAL)
    wbc = bc_weight.reshape(D, 2 * STATE)
    bc_taps = bc_conv_weight.reshape(4, 2 * STATE)
    segs = segment_ids[None]
    skip = skip_gain[None]
    gain_row = gate_gain[None]
    dg = nt(cotangent, out_weight)
    ext_scratch = pltpu.VMEM((ROWS + 8, LANES), f32)
    pad_scratch = pltpu.VMEM((4, ROWS + 48, LANES), f32)
    (
        normed_ext,
        joined,
        pre,
        gate,
        b_low,
        c_low,
        step,
        cum,
        sig,
        decay,
        state,
    ) = kernel_call(
        front_body,
        [
            ((EXT, D), bf16),
            ((EXT, LOCAL + 2 * STATE), f32),
            ((ROWS, LOCAL + 2 * STATE), f32),
            ((ROWS, LOCAL), f32),
            ((ROWS, STATE), bf16),
            ((ROWS, STATE), bf16),
            ((ROWS, LANES), f32),
            ((ROWS, LANES), f32),
            ((ROWS, LANES), f32),
            ((ROWS, LANES), f32),
            ((HEADS, CHUNK, STATE), bf16),
        ],
        (
            gathered,
            halo,
            norm_gain[None],
            win,
            wbc,
            step_weight,
            conv_weight,
            conv_bias[None],
            bc_taps,
            bc_conv_bias.reshape(1, 2 * STATE),
            segs,
            step_bias[None],
            decay_log[None],
        ),
        scratch=[ext_scratch, pltpu.VMEM((D, LANES), bf16)],
    )
    pieces = lax.all_to_all(state, CONTEXT, 0, 0, tiled=True)
    (within,) = kernel_call(
        within_body,
        [((ROWS, LOCAL), f32)],
        (pre, step, cum, b_low, c_low, segs, skip),
    )
    (starts,) = kernel_call(scan_body, [((16, HEAD, STATE), bf16)], (pieces,))
    start = lax.all_to_all(starts, CONTEXT, 0, 0, tiled=True).reshape(LOCAL, STATE)
    mixed, sums = kernel_call(
        mixed_body,
        [((ROWS, LOCAL), f32), ((ROWS, LANES), f32)],
        (within, start, c_low, cum, segs, gate, dg, gain_row),
    )
    gnorm, d_mixed, d_gate, grad_gate_gain, d_start = kernel_call(
        gate_body,
        [
            ((ROWS, LOCAL), bf16),
            ((ROWS, LOCAL), f32),
            ((ROWS, LOCAL), bf16),
            ((1, LOCAL), f32),
            ((HEADS, HEAD, STATE), bf16),
        ],
        (sums, swapped(sums), mixed, gate, dg, gain_row, c_low, cum, segs),
    )
    normed = normed_ext[HALO:]
    grad_out, grad_gate, d_start = lax.optimization_barrier(
        (tn(gnorm, cotangent), tn(normed, d_gate), d_start)
    )
    grad_out, grad_gate = lax.psum((grad_out, grad_gate), EVERYONE)
    received = lax.all_to_all(d_start, CONTEXT, 0, 0, tiled=True)
    (adjoints,) = kernel_call(
        scan_back_body, [((16, HEAD, STATE), bf16)], (pieces, received)
    )
    adjoint = lax.all_to_all(adjoints, CONTEXT, 0, 0, tiled=True).reshape(LOCAL, STATE)
    out_terms = mm(gnorm, out_weight).astype(bf16)
    kept = lax.dynamic_slice_in_dim(out_terms, side * width, width, 1)
    given = lax.dynamic_slice_in_dim(out_terms, (1 - side) * width, width, 1)
    hidden_out = (
        hidden_in.astype(f32) + kept.astype(f32) + swapped(given).astype(f32)
    ).astype(bf16)
    d_bc, d_ext, d_step, conv_grads, skip_grads, small = kernel_call(
        back_body,
        [
            ((ROWS, 2 * STATE), bf16),
            ((EXT, LOCAL), bf16),
            ((ROWS, LANES), bf16),
            ((8, LOCAL), f32),
            ((1, LOCAL), f32),
            ((8, LANES), f32),
        ],
        (
            d_mixed,
            pre,
            joined,
            within,
            start,
            adjoint,
            b_low,
            c_low,
            step,
            cum,
            sig,
            decay,
            segs,
            decay_log[None],
            skip,
            conv_weight,
        ),
        scratch=[ext_scratch, pad_scratch],
    )
    d_bc_ext, bc_conv_grads = kernel_call(
        bc_back_body,
        [((EXT, 2 * STATE), bf16), ((8, 2 * STATE), f32)],
        (d_bc, swapped(d_bc), pre, joined, segs, bc_taps),
        scratch=[ext_scratch, pad_scratch],
    )
    (terms,) = kernel_call(
        terms_body,
        [((EXT, D), bf16)],
        (d_ext, d_gate, d_step, d_bc_ext, win, step_weight, wbc),
    )
    other_terms = swapped(terms)
    halo_terms = (terms[:HALO].astype(f32) + other_terms[:HALO].astype(f32)).astype(bf16)
    returned = lax.ppermute(halo_terms, CONTEXT, [(i + 1, i) for i in range(15)])
    hidden_grad, grad_norm = kernel_call(
        hidden_body,
        [((ROWS, width), bf16), ((1, width), f32)],
        (gathered, terms, other_terms, returned, norm_gain[None], out_grad),
    )
    (bundle,) = kernel_call(
        bundle_body,
        [((D, LOCAL + 256), bf16)],
        (
            normed_ext,
            d_ext,
            d_bc_ext,
            d_step,
            conv_grads,
            bc_conv_grads,
            grad_gate_gain,
            grad_norm,
            skip_grads,
            small,
        ),
    )
    scattered = lax.all_to_all(
        bundle.reshape(DEVICES, 16, LOCAL + 256), EVERYONE, 0, 0, tiled=True
    )
    (spread,) = kernel_call(total_body, [(scattered.shape, bf16)], (scattered,))
    final = lax.all_to_all(spread, EVERYONE, 0, 0, tiled=True).reshape(D, LOCAL + 256)
    half = D // 2
    (
        grad_bc,
        grad_step,
        grad_conv,
        grad_conv_bias,
        grad_bc_conv,
        grad_bc_conv_bias,
        total_gate_gain,
        total_norm_gain,
        grad_skip,
        grad_step_bias,
        grad_decay_log,
    ) = kernel_call(
        few_body,
        [
            ((half, 2, STATE), f32),
            ((D, HEADS), f32),
            ((4, LOCAL), f32),
            ((1, LOCAL), f32),
            ((4, 2, STATE), f32),
            ((2, STATE), f32),
            ((1, LOCAL), f32),
            ((1, half), f32),
            ((1, HEADS), f32),
            ((1, HEADS), f32),
            ((1, HEADS), f32),
        ],
        (final,),
    )
    (grad_in,) = kernel_call(large_body, [((D, 2, LOCAL), f32)], (final, grad_gate))
    return (
        hidden_out,
        hidden_grad,
        total_norm_gain[0],
        grad_in,
        grad_bc,
        grad_step,
        grad_conv,
        grad_conv_bias[0],
        grad_bc_conv,
        grad_bc_conv_bias,
        grad_step_bias[0],
        grad_decay_log[0],
        grad_skip[0],
        total_gate_gain[0],
        grad_out,
    )


def solution(mesh):
    torus = Mesh(
        mesh.devices.reshape(mesh.shape["tensor"], mesh.shape["dp"], 4, 4),
        ("tensor", "dp", "context_0", "context_1"),
    )
    rows = ("dp", "context_0", "context_1")
    in_specs = (
        P(rows, "tensor"),
        P(rows),
        P(),
        P(None, None, "tensor"),
        P(),
        P(None, "tensor"),
        P(None, "tensor"),
        P("tensor"),
        P(),
        P(),
        P(),
        P("tensor"),
        P("tensor"),
        P("tensor"),
        P("tensor", None),
        P(rows, "tensor"),
    )
    out_specs = (
        P(rows, "tensor"),
        P(rows, "tensor"),
        P("tensor"),
        P(None, None, "tensor"),
        P("tensor", None, None),
        P(None, "tensor"),
        P(None, "tensor"),
        P("tensor"),
        P(),
        P(),
        P("tensor"),
        P("tensor"),
        P("tensor"),
        P("tensor"),
        P("tensor", None),
    )
    return jax.shard_map(
        shards, mesh=torus, in_specs=in_specs, out_specs=out_specs, check_vma=False
    )
```

profile of v0, /device:TPU:1, one launch (start us, length us, event | category | flops | bytes accessed | tf_op | source)
XLA Modules:
  0.0 302.5 jit_solution(16643095383494441212)
XLA Ops:
  7.2 3.6 %all_gather.6.hidden_ref = bf16[256,1024]{1,0:T(8,128)(2,1)S(1)} all-gather(bf16[256,512]{1,0:T(8,128)(2,1)} %param.16), channel_id=1, replica_groups=mesh['tensor'=2,'dp'=4,'context_0'=4,'context_1'=4] {'tensor'}, dimensions={1}, use_global_device_ids=true | all-gather | bytes 786432 | tf_op jit(solution)/shard_map/all_gather | solution.py:636
  10.8 3.3 %collective-permute-start = (bf16[16,1024]{1,0:T(8,128)(2,1)S(1)}, bf16[16,1024]{1,0:T(8,128)(2,1)S(1)}, u32[]{:S(2)}, u32[]{:S(2)}) collective-permute-start(bf16[16,1024]{1,0:T(8,128)(2,1)S(1)} %slice.16), channel_id=1, source_target_pairs={{0,1},{1,2},{2,3},{3,4},{4,5},{5,6},{6,7},{7,8},{8,9},{9,10},{10,1... | collective-permute-start | bytes 98312 | tf_op jit(solution)/shard_map/ppermute | solution.py:637
  14.1 5.7 %copy.34 = bf16[128,8,2,1024]{3,1,2,0:T(8,128)(2,1)} copy(bf16[128,8,2,1024]{3,2,1,0:T(2,128)(2,1)} %bitcast.40) | data formatting | bytes 8388608
  19.8 0.9 copy.39
  20.7 0.8 copy.31.wst_ref
  22.7 7.6 %shard_map.271 = (bf16[272,1024]{1,0:T(8,128)(2,1)}, f32[272,1280]{1,0:T(8,128)}, f32[256,1280]{1,0:T(8,128)}, f32[256,1024]{1,0:T(8,128)}, bf16[256,128]{1,0:T(...) custom-call(bf16[256,1024]{1,0:T(8,128)(2,1)} %copy-done.1, ...), custom_call_target="tpu_custom_call" | custom-call | tf_op jit(solution)/shard_map/pallas_call | solution.py:53
  30.3 7.5 %all-to-all-start = ((bf16[16,80,128]{2,1,0:T(8,128)(2,1)}), bf16[16,80,128]{2,1,0:T(8,128)(2,1)S(1)}, u32[]{:S(2)}, u32[]{:S(2)}) async-start(bf16[16,80,128]{2,1,0:T(8,128)(2,1)} %get-tuple-element.62), calls=%async_computation | async-start | bytes 655360 | tf_op jit(solution)/shard_map/all_to_all | solution.py:692
  37.8 2.7 all_gather.7
  40.6 5.7 %all-to-all-done.pieces_ref = bf16[16,80,128]{2,1,0:T(8,128)(2,1)S(1)} async-done(((bf16[16,80,128]{2,1,0:T(8,128)(2,1)}), bf16[16,80,128]{2,1,0:T(8,128)(2,1)S(1)}, u32[]{:S(2)}, u32[]{:S(2)}) %all-to-all-start) | async-done | bytes 327712 | tf_op jit(solution)/shard_map/all_to_all | solution.py:692
  46.3 0.7 copy-done.4
  47.0 1.7 shard_map.273
  48.7 3.5 %all-to-all-start.1 = ((bf16[16,64,128]{2,1,0:T(8,128)(2,1)}), bf16[16,64,128]{2,1,0:T(8,128)(2,1)S(1)}, u32[]{:S(2)}, u32[]{:S(2)}) async-start(bf16[16,64,128]{2,1,0:T(8,128)(2,1)} %shard_map.273), calls=%async_computation.1 | async-start | bytes 524288 | tf_op jit(solution)/shard_map/all_to_all | solution.py:699
  52.3 1.7 fusion.2.dg_ref
  54.1 4.1 %shard_map.272.within_ref = f32[256,1024]{1,0:T(8,128)} custom-call(f32[256,1280]{1,0:T(8,128)} %get-tuple-element.57.pre_ref, f32[256,128]{1,0:T(8,128)} %get-tuple-element.58.step_ref, f32[256,128]{1,0:T(8,128)} %get-tuple-element.59.cum_ref, bf16[256,128]{1,0:T(8,128)(2,1)} %get-tuple-element.60.b_ref, bf16[256,128]{1,0:T(8,128)(2,1)} %get-tuple-element.61.c_ref, ...), custom_call_target="tpu_custom_call" | custom-call | tf_op jit(solution)/shard_map/pallas_call | solution.py:53
  58.2 1.7 all-to-all-done.1
  60.6 3.9 %shard_map.274 = (f32[256,1024]{1,0:T(8,128)}, f32[256,128]{1,0:T(8,128)}) custom-call(f32[256,1024]{1,0:T(8,128)} %shard_map.272.within_ref, bf16[1024,128]{1,0:T(8,128)(2,1)} %bitcast.41, bf16[256,128]{1,0:T(8,128)(2,1)} %get-tuple-element.61.c_ref, f32[256,128]{1,0:T(8,128)} %get-tuple-element.59.cum_ref, s32[1,256]{1,0:T(1,128)} %bitcast.49, ...), custom_call_target="tpu_custom_call" | custom-call | tf_op jit(solution)/shard_map/pallas_call | solution.py:53
  64.4 2.9 collective-permute-start.1
  67.4 1.2 collective-permute-done.1.other_ref
  69.2 4.4 %shard_map.275 = (bf16[256,1024]{1,0:T(8,128)(2,1)}, f32[256,1024]{1,0:T(8,128)}, bf16[256,1024]{1,0:T(8,128)(2,1)}, f32[1,1024]{1,0:T(1,128)}, bf16[16,64,128]{2,1,0:T(8,128)(2,1)}) custom-call(f32[256,128]{1,0:T(8,128)} %get-tuple-element.64.sums_ref, f32[256,128]{1,0:T(8,128)} %copy-done.13, f32[256,1024]{1,0:T(8,128)} %get-tuple-element.65.mixed_ref, ...), custom_call_target="tpu_custom_call" | custom-call | tf_op jit(solution)/shard_map/pallas_call | solution.py:53
  73.7 3.8 %fusion.3 = f32[1024,1024]{1,0:T(8,128)} fusion(bf16[256,1024]{1,0:T(8,128)(2,1)} %get-tuple-element.66, bf16[256,1024]{1,0:T(8,128)(2,1)S(1)} %all_gather.7), kind=kOutput, calls=%fused_computation.9 | convolution fusion | flops 536870912 | bytes 5242880 | tf_op jit(solution)/shard_map/dot_general | solution.py:39
  77.5 2.8 fusion
  80.3 0.9 copy-done.12
  81.2 12.2 %all_to_all.30.grads_ref = bf16[16,64,128]{2,1,0:T(8,128)(2,1)} all-to-all(bf16[16,64,128]{2,1,0:T(8,128)(2,1)S(1)} %copy-done.12), channel_id=1, replica_groups=mesh['tensor'=2,'dp'=4,'context_0'=4,'context_1'=4] {'context_0','contex..., dimensions={0} | all-to-all | bytes 524288 | tf_op jit(solution)/shard_map/all_to_all | solution.py:721
  93.4 1.8 shard_map.276
  95.3 13.6 %all_to_all.31 = bf16[16,64,128]{2,1,0:T(8,128)(2,1)} all-to-all(bf16[16,64,128]{2,1,0:T(8,128)(2,1)} %shard_map.276), channel_id=1, replica_groups=mesh['tensor'=2,'dp'=4,'context_0'=4,'context_1'=4] {'context_0','contex..., dimensions={0} | all-to-all | bytes 524288 | tf_op jit(solution)/shard_map/all_to_all | solution.py:725
  108.8 10.6 %shard_map.277 = (bf16[256,256]{1,0:T(8,128)(2,1)}, bf16[272,1024]{1,0:T(8,128)(2,1)}, bf16[256,128]{1,0:T(8,128)(2,1)}, f32[8,1024]{1,0:T(8,128)}, f32[1,1024]{1,0:T(1,128)}, /*index=5*/f32[8,128]{1,0:T(8,128)}) custom-call(f32[256,1024]{1,0:T(8,128)} %get-tuple-element.67.d_mixed_ref, f32[256,1280]{1,0:T(8,128)} %get-tuple-element.57.pre_ref, ...), custom_call_target="tpu_custom_call" | custom-call | tf_op jit(solution)/shard_map/pallas_call | solution.py:53
  119.4 4.5 %collective-permute-start.3 = (bf16[256,256]{1,0:T(8,128)(2,1)}, bf16[256,256]{1,0:T(8,128)(2,1)S(1)}, u32[]{:S(2)}, u32[]{:S(2)}) collective-permute-start(bf16[256,256]{1,0:T(8,128)(2,1)} %get-tuple-element.77.own_ref), channel_id=1, source_target_pairs={{0,64},{64,0},{1,65},{65,1},{2,66},{66,2},{3,67},{67,3},{4,68},{68... | collective-permute-start | bytes 393224 | tf_op jit(solution)/shard_map/ppermute | solution.py:613
  124.0 1.2 collective-permute-done.3.other_ref
  125.8 3.0 shard_map.278
  128.8 5.3 %shard_map.279.terms_ref = bf16[272,1024]{1,0:T(8,128)(2,1)} custom-call(bf16[272,1024]{1,0:T(8,128)(2,1)} %get-tuple-element.75.dx_ref, bf16[256,1024]{1,0:T(8,128)(2,1)} %get-tuple-element.70.dz_ref, bf16[256,128]{1,0:T(8,128)(2,1)} %get-tuple-element.76.dst_ref, bf16[272,256]{1,0:T(8,128)(2,1)} %get-tuple-element.78.dbc_ref, bf16[1024,2048]{1,0:T(8,128)(2,1)} %bitcast.36, ...), custom_call_target="tpu_custom_call" | custom-call | tf_op jit(solution)/shard_map/pallas_call | solution.py:53
  134.4 1.8 collective-permute-done.4.other_ref
  136.2 0.8 add_convert_fusion.1
  137.0 1.3 collective-permute-start.5
  138.3 4.3 %collective-permute-done.5.returned_ref = bf16[16,1024]{1,0:T(8,128)(2,1)S(1)} collective-permute-done((bf16[16,1024]{1,0:T(8,128)(2,1)S(1)}, bf16[16,1024]{1,0:T(8,128)(2,1)S(1)}, u32[]{:S(2)}, u32[]{:S(2)}) %collective-permute-start.5) | collective-permute-done | bytes 32800 | tf_op jit(solution)/shard_map/ppermute | solution.py:775
  143.2 2.7 shard_map.280
  145.9 4.3 %shard_map.281 = bf16[1024,1280]{1,0:T(8,128)(2,1)} custom-call(bf16[272,1024]{1,0:T(8,128)(2,1)} %get-tuple-element.69.normed_ref, bf16[272,1024]{1,0:T(8,128)(2,1)} %get-tuple-element.75.dx_ref, bf16[272,256]{1,0:T(8,128)(2,1)} %get-tuple-element.78.dbc_ref, bf16[256,128]{1,0:T(8,128)(2,1)} %get-tuple-element.76.dst_ref, ...), custom_call_target="tpu_custom_call" | custom-call | tf_op jit(solution)/shard_map/pallas_call | solution.py:53
  150.2 42.3 %all_to_all.32.received_ref = bf16[64,16,1280]{2,1,0:T(8,128)(2,1)} all-to-all(bf16[64,16,1280]{2,1,0:T(8,128)(2,1)} %bitcast.37), channel_id=1, replica_groups=mesh['tensor'=2,'dp'=4,'context_0'=4,'context_1'=4] {'dp','context_0','c..., dimensions={0} | all-to-all | bytes 5242880 | tf_op jit(solution)/shard_map/all_to_all | solution.py:797
  192.6 3.7 %shard_map.282 = bf16[64,16,1280]{2,1,0:T(8,128)(2,1)} custom-call(bf16[64,16,1280]{2,1,0:T(8,128)(2,1)} %all_to_all.32.received_ref), custom_call_target="tpu_custom_call" | custom-call | tf_op jit(solution)/shard_map/pallas_call | solution.py:53
  196.3 6.3 %all-to-all-start.5 = ((bf16[64,16,1280]{2,1,0:T(8,128)(2,1)}), bf16[64,16,1280]{2,1,0:T(8,128)(2,1)}, u32[]{:S(2)}, u32[]{:S(2)}) async-start(bf16[64,16,1280]{2,1,0:T(8,128)(2,1)} %shard_map.282), calls=%async_computation.5 | async-start | bytes 5242880 | tf_op jit(solution)/shard_map/all_to_all | solution.py:801
  203.4 2.4 collective-permute-start.2
  205.8 1.2 collective-permute-done.2
  207.0 0.8 add_convert_fusion
  207.8 28.0 %all-to-all-done.5 = bf16[64,16,1280]{2,1,0:T(8,128)(2,1)} async-done(((bf16[64,16,1280]{2,1,0:T(8,128)(2,1)}), bf16[64,16,1280]{2,1,0:T(8,128)(2,1)}, u32[]{:S(2)}, u32[]{:S(2)}) %all-to-all-start.5) | async-done | bytes 2621472 | tf_op jit(solution)/shard_map/all_to_all | solution.py:801
  235.8 3.1 %shard_map.283 = (f32[512,2,128]{2,1,0:T(2,128)}, f32[1024,16]{1,0:T(8,128)}, f32[4,1024]{1,0:T(4,128)}, f32[1,1024]{1,0:T(1,128)}, f32[4,2,128]{2,1,0:T(2,128)}...) custom-call(bf16[1024,1280]{1,0:T(8,128)(2,1)} %bitcast.11.final_ref), custom_call_target="tpu_custom_call" | custom-call | tf_op jit(solution)/shard_map/pallas_call | solution.py:53
  238.9 1.8 copy.33
  240.8 44.9 %all-reduce.3.cloned.1.call-done = (f32[1024,1024]{1,0:T(8,128)}, f32[1024,1024]{1,0:T(8,128)}) async-done(((f32[1024,1024]{1,0:T(8,128)}, f32[1024,1024]{1,0:T(8,128)}), (f32[1024,1024]{1,0:T(8,128)}, f32[1024,1024]{1,0:T(8,128)})) %all-reduce.3.cloned.1.call-update) | async-done | bytes 8388624 | tf_op jit(solution)/shard_map/psum | solution.py:720
  285.6 8.0 %shard_map.284 = f32[1024,2,1024]{2,1,0:T(2,128)} custom-call(bf16[1024,1280]{1,0:T(8,128)(2,1)} %bitcast.11.final_ref, f32[1024,1024]{1,0:T(8,128)} %get-tuple-element.114.gate_ref), custom_call_target="tpu_custom_call" | custom-call | tf_op jit(solution)/shard_map/pallas_call | solution.py:53
  293.6 2.0 copy.43
  (44 shorter events, 5.1 us)
Async XLA Ops:
  7.2 45.2 %copy-start = (bf16[1024,1024]{1,0:T(8,128)(2,1)S(1)}, bf16[1024,1024]{1,0:T(8,128)(2,1)}, u32[]{:S(2)}) copy-start(bf16[1024,1024]{1,0:T(8,128)(2,1)} %param.30) | copy-start | bytes 6291460
  10.8 9.0 %copy-start.1 = (bf16[256,1024]{1,0:T(8,128)(2,1)}, bf16[256,1024]{1,0:T(8,128)(2,1)S(1)}, u32[]{:S(2)}) copy-start(bf16[256,1024]{1,0:T(8,128)(2,1)S(1)} %all_gather.6.hidden_ref) | copy-start | bytes 1572868
  10.8 11.3 %collective-permute-start = (bf16[16,1024]{1,0:T(8,128)(2,1)S(1)}, bf16[16,1024]{1,0:T(8,128)(2,1)S(1)}, u32[]{:S(2)}, u32[]{:S(2)}) collective-permute-start(bf16[16,1024]{1,0:T(8,128)(2,1)S(1)} %slice.16), channel_id=1, source_target_pairs={{0,1},{1,2},{2,3},{3,4},{4,5},{5,6},{6,7},{7,8},{8,9},{9,10},{10,1... | collective-permute-start | bytes 98312 | tf_op jit(solution)/shard_map/ppermute | solution.py:637
  14.1 5.7 %copy-start.11 = (bf16[1024,2,128]{2,1,0:T(2,128)(2,1)S(1)}, bf16[1024,2,128]{2,1,0:T(2,128)(2,1)}, u32[]{:S(2)}) copy-start(bf16[1024,2,128]{2,1,0:T(2,128)(2,1)} %param.20) | copy-start | bytes 1572868
  14.1 6.6 %copy-start.17 = (bf16[1024,16]{0,1:T(8,128)(2,1)S(1)}, bf16[1024,16]{0,1:T(8,128)(2,1)}, u32[]{:S(2)}) copy-start(bf16[1024,16]{0,1:T(8,128)(2,1)} %param.21) | copy-start | bytes 98308
  14.1 7.4 %copy-start.18 = (f32[4,2,128]{2,1,0:T(2,128)S(1)}, f32[4,2,128]{2,1,0:T(2,128)}, u32[]{:S(2)}) copy-start(f32[4,2,128]{2,1,0:T(2,128)} %param.24) | copy-start | bytes 12292
  22.1 0.6 copy-start.15
  22.7 15.1 %copy-start.9 = (bf16[256,512]{1,0:T(8,128)(2,1)S(1)}, bf16[256,512]{1,0:T(8,128)(2,1)}, u32[]{:S(2)}) copy-start(bf16[256,512]{1,0:T(8,128)(2,1)} %out_grad_ref.1) | copy-start | bytes 786436
  30.3 16.0 %all-to-all-start = ((bf16[16,80,128]{2,1,0:T(8,128)(2,1)}), bf16[16,80,128]{2,1,0:T(8,128)(2,1)S(1)}, u32[]{:S(2)}, u32[]{:S(2)}) async-start(bf16[16,80,128]{2,1,0:T(8,128)(2,1)} %get-tuple-element.62), calls=%async_computation | async-start | bytes 655360 | tf_op jit(solution)/shard_map/all_to_all | solution.py:692
  46.3 0.7 copy-start.4
  48.7 11.1 %all-to-all-start.1 = ((bf16[16,64,128]{2,1,0:T(8,128)(2,1)}), bf16[16,64,128]{2,1,0:T(8,128)(2,1)S(1)}, u32[]{:S(2)}, u32[]{:S(2)}) async-start(bf16[16,64,128]{2,1,0:T(8,128)(2,1)} %shard_map.273), calls=%async_computation.1 | async-start | bytes 524288 | tf_op jit(solution)/shard_map/all_to_all | solution.py:699
  52.3 233.3 %all-reduce.3.cloned.1.call-start = ((), (), s32[]{:S(2)}) async-start(), calls=%async_computation.6 | async-start | bytes 16777216 | tf_op jit(solution)/shard_map/psum | solution.py:720
  59.9 0.7 copy-start.5
  64.4 4.1 %collective-permute-start.1 = (f32[256,128]{1,0:T(8,128)}, f32[256,128]{1,0:T(8,128)S(1)}, u32[]{:S(2)}, u32[]{:S(2)}) collective-permute-start(f32[256,128]{1,0:T(8,128)} %get-tuple-element.64.sums_ref), channel_id=1, source_target_pairs={{0,64},{64,0},{1,65},{65,1},{2,66},{66,2},{3,67},{67,3},{4,68},{68... | collective-permute-start | bytes 393224 | tf_op jit(solution)/shard_map/ppermute | solution.py:613
  68.6 0.7 copy-start.13
  73.7 3.8 %copy-start.3 = (bf16[272,1024]{1,0:T(8,128)(2,1)S(1)}, bf16[272,1024]{1,0:T(8,128)(2,1)}, u32[]{:S(2)}) copy-start(bf16[272,1024]{1,0:T(8,128)(2,1)} %get-tuple-element.69.normed_ref) | copy-start | bytes 1671172
  73.7 3.8 %copy-start.6 = (bf16[256,1024]{1,0:T(8,128)(2,1)S(1)}, bf16[256,1024]{1,0:T(8,128)(2,1)}, u32[]{:S(2)}) copy-start(bf16[256,1024]{1,0:T(8,128)(2,1)} %get-tuple-element.70.dz_ref) | copy-start | bytes 1572868
  80.2 0.9 copy-start.12
  119.4 5.7 %collective-permute-start.3 = (bf16[256,256]{1,0:T(8,128)(2,1)}, bf16[256,256]{1,0:T(8,128)(2,1)S(1)}, u32[]{:S(2)}, u32[]{:S(2)}) collective-permute-start(bf16[256,256]{1,0:T(8,128)(2,1)} %get-tuple-element.77.own_ref), channel_id=1, source_target_pairs={{0,64},{64,0},{1,65},{65,1},{2,66},{66,2},{3,67},{67,3},{4,68},{68... | collective-permute-start | bytes 393224 | tf_op jit(solution)/shard_map/ppermute | solution.py:613
  125.2 0.7 copy-start.14
  134.0 2.2 collective-permute-start.4
  136.2 6.4 %copy-start.10 = (bf16[272,1024]{1,0:T(8,128)(2,1)}, bf16[272,1024]{1,0:T(8,128)(2,1)S(1)}, u32[]{:S(2)}) copy-start(bf16[272,1024]{1,0:T(8,128)(2,1)S(1)} %collective-permute-done.4.other_ref) | copy-start | bytes 1671172
  137.0 5.6 %collective-permute-start.5 = (bf16[16,1024]{1,0:T(8,128)(2,1)S(1)}, bf16[16,1024]{1,0:T(8,128)(2,1)S(1)}, u32[]{:S(2)}, u32[]{:S(2)}) collective-permute-start(bf16[16,1024]{1,0:T(8,128)(2,1)S(1)} %add_convert_fusion.1), channel_id=1, source_target_pairs={{1,0},{2,1},{3,2},{4,3},{5,4},{6,5},{7,6},{8,7},{9,8},{10,9},{11,1... | collective-permute-start | bytes 98312 | tf_op jit(solution)/shard_map/ppermute | solution.py:775
  142.6 0.6 copy-start.16
  196.3 6.4 %copy-start.7 = (bf16[256,1024]{1,0:T(8,128)(2,1)S(1)}, bf16[256,1024]{1,0:T(8,128)(2,1)}, u32[]{:S(2)}) copy-start(bf16[256,1024]{1,0:T(8,128)(2,1)} %get-tuple-element.66) | copy-start | bytes 1572868
  196.3 39.5 %all-to-all-start.5 = ((bf16[64,16,1280]{2,1,0:T(8,128)(2,1)}), bf16[64,16,1280]{2,1,0:T(8,128)(2,1)}, u32[]{:S(2)}, u32[]{:S(2)}) async-start(bf16[64,16,1280]{2,1,0:T(8,128)(2,1)} %shard_map.282), calls=%async_computation.5 | async-start | bytes 5242880 | tf_op jit(solution)/shard_map/all_to_all | solution.py:801
  202.6 4.3 %copy-start.8 = (bf16[256,512]{1,0:T(8,128)(2,1)S(1)}, bf16[256,512]{1,0:T(8,128)(2,1)}, u32[]{:S(2)}) copy-start(bf16[256,512]{1,0:T(8,128)(2,1)} %param.16) | copy-start | bytes 786436
  203.4 3.6 %collective-permute-start.2 = (bf16[256,512]{1,0:T(8,128)(2,1)S(1)}, bf16[256,512]{1,0:T(8,128)(2,1)S(1)}, u32[]{:S(2)}, u32[]{:S(2)}) collective-permute-start(bf16[256,512]{1,0:T(8,128)(2,1)S(1)} %constant_dynamic-slice_fusion), channel_id=1, source_target_pairs={{0,64},{64,0},{1,65},{65,1},{2,66},{66,2},{3,67},{67,3},{4,68},{68... | collective-permute-start | bytes 786440 | tf_op jit(solution)/shard_map/ppermute | solution.py:613
  285.6 8.0 %copy-start.2 = (f32[1024,1024]{1,0:T(8,128)S(1)}, f32[1024,1024]{1,0:T(8,128)}, u32[]{:S(2)}) copy-start(f32[1024,1024]{1,0:T(8,128)} %get-tuple-element.130) | copy-start | bytes 12582916
Sparse Core Ops, SparseCore 0:
  80.4 205.1 all-reduce.2
where the time goes:
time: 305 us; the launch traced here: 302 us
  waiting for transfers between devices  90 us (30%)
  blocking collectives  74.5 us (24%)
  Pallas kernels  64.2 us (21%)
  starting transfers between devices  32.2 us (11%)
  local copies, waits for them, and re-layouts  16.8 us (6%)
  between operations  14.2 us (5%)
  matrix products  9.02 us (3%)
    pallas_call x14, Pallas kernels, kernel_call(): pl.pallas_call(body, grid=(1,), out_shape=[jax.ShapeDtypeStruct(shape, ki...  64.2 us
    psum x1, waiting for transfers between devices, shards(): grad_out, grad_gate = lax.psum((grad_out, grad_gate), EVERYONE)  44.9 us
    all_to_all x1, blocking collectives, shards(): lax.all_to_all(bundle.reshape(DEVICES, 16, LOCAL + 256), EVERYONE, 0, 0,...  42.3 us
    all_to_all x1, waiting for transfers between devices, shards(): lax.all_to_all(spread, EVERYONE, 0, 0, tiled=True).reshape(D, LOCAL + 256)  28 us
    unnamed x44, local copies, waits for them, and re-layouts  16.8 us
    all_to_all x1, blocking collectives, shards(): lax.all_to_all(adjoints, CONTEXT, 0, 0, tiled=True).reshape(LOCAL, STATE)  13.6 us
    all_to_all x1, blocking collectives, shards(): received = lax.all_to_all(d_start, CONTEXT, 0, 0, tiled=True)  12.2 us
    ppermute x4, starting transfers between devices, swapped(): return lax.ppermute(values, 'tensor', [(0, 1), (1, 0)])  10.2 us
  transfers between devices with their start and end apart: 10, of which 9 were waited for; matrix products, arithmetic and copies ran while one was open for 5% of the time, Pallas kernels for 13%

commit v1 on v0

--- a/solution.py
+++ b/solution.py
@@ -22,6 +22,10 @@
 CONTEXT = ("context_0", "context_1")
 EVERYONE = ("dp", "context_0", "context_1")
 EPSILON = 1e-05
+BC_COST = 10_000_000
+TERMS_COST = 15_000_000
+HIDDEN_COST = 9_000_000
+BUNDLE_COST = 8_000_000
 f32 = jnp.float32
 bf16 = jnp.bfloat16
 HIGHEST = lax.Precision.HIGHEST
@@ -45,24 +49,21 @@
     )
 
 
-def whole(shape):
-    return pl.BlockSpec(shape, lambda i: (0,) * len(shape), pipeline_mode=pl.Buffered(1))
-
-
-def kernel_call(body, outs, args, scratch=(), flops=0, vmem=56):
+def whole(shape, index=None):
+    index = index or (0,) * len(shape)
+    return pl.BlockSpec(shape, lambda i: index, pipeline_mode=pl.Buffered(1))
+
+
+def kernel_call(body, outs, args, scratch=(), cost=0, vmem=56, blocks={}):
     return pl.pallas_call(
         body,
         grid=(1,),
         out_shape=[jax.ShapeDtypeStruct(shape, kind) for shape, kind in outs],
-        in_specs=[whole(a.shape) for a in args],
+        in_specs=[whole(*blocks.get(i, (a.shape,))) for i, a in enumerate(args)],
         out_specs=[whole(shape) for shape, _ in outs],
         scratch_shapes=list(scratch),
         compiler_params=pltpu.CompilerParams(vmem_limit_bytes=vmem * 1024 * 1024),
-        cost_estimate=pl.CostEstimate(
-            flops=flops,
-            bytes_accessed=0,
-            transcendentals=0,
-        ),
+        cost_estimate=pl.CostEstimate(flops=0, bytes_accessed=cost, transcendentals=0),
     )(*args)
 
 
@@ -139,7 +140,6 @@
     normed_ref,
     joined_ref,
     pre_ref,
-    gate_ref,
     b_ref,
     c_ref,
     step_ref,
@@ -157,15 +157,14 @@
         normed_ref[start : start + rows, :] = (values * scale * gain).astype(bf16)
     normed_ext = normed_ref[...]
     normed = normed_ref[HALO:, :]
-    joined_ref[:, :LOCAL] = mm(normed_ext, win_ref[:, :LOCAL])
+    joined_ref[:, :LOCAL] = mm(normed_ext, win_ref[...])
     joined_ref[:, LOCAL:] = mm(normed_ext, wbc_ref[...])
-    gate_ref[...] = mm(normed, win_ref[:, LOCAL:])
     wide_ref[...] = jnp.zeros_like(wide_ref)
-    wide_ref[:, :HEADS] = wst_ref[...]
+    wide_ref[:HEADS, :] = wst_ref[...]
     both = step_bias_ref[...]
     first = lax.axis_index("tensor") == 0
     local_bias = jnp.where(first, both[:, :HEADS], both[:, HEADS:])
-    raw = mm(normed, wide_ref[...]) + to_lanes(local_bias)
+    raw = nt(normed, wide_ref[...]) + to_lanes(local_bias)
     step = jnp.maximum(raw, 0.0) + jnp.log1p(jnp.exp(-jnp.abs(raw)))
     decay = step * to_lanes(-jnp.exp(decay_log_ref[...]))
     tri = (row_index((ROWS, ROWS)) >= lane_index((ROWS, ROWS))).astype(f32)
@@ -202,6 +201,10 @@
             state_ref[head, HEAD:, :] = jnp.broadcast_to(
                 gains[:, head : head + 1], (CHUNK - HEAD, STATE)
             ).astype(bf16)
+
+
+def gate_proj_body(normed_ref, win_ref, gate_ref):
+    gate_ref[...] = mm(normed_ref[HALO:, :], win_ref[...])
 
 
 def within_body(pre_ref, step_ref, cum_ref, b_ref, c_ref, seg_ref, skip_ref, within_ref):
@@ -340,12 +343,73 @@
 def back_body(
     d_mixed_ref,
     pre_ref,
+    within_ref,
+    start_ref,
+    b_ref,
+    c_ref,
+    step_ref,
+    cum_ref,
+    seg_ref,
+    skip_ref,
+    d_xs_ref,
+    d_bc_ref,
+    d_cum_ref,
+    skip_grad_ref,
+):
+    seg_row, documents = documents_of(seg_ref)
+    skips = skip_ref[...]
+    cum = cum_ref[...]
+    cum_t = cum.T
+    step = step_ref[...]
+    b_low = b_ref[...]
+    c_low = c_ref[...]
+    products = nt(c_low, b_low)
+    bias = pair_mask(documents, seg_row)
+    entry = entry_decay(cum, documents)
+    first_half = lane_index((ROWS, LANES)) < HEAD
+    d_products = jnp.zeros((ROWS, ROWS), f32)
+    d_c = jnp.zeros((ROWS, STATE), f32)
+    d_cum = jnp.zeros((ROWS, LANES), f32)
+    for pair in range(PAIRS):
+        lanes = slice(pair * LANES, (pair + 1) * LANES)
+        pre = pre_ref[:, lanes]
+        x = pre * jax.nn.sigmoid(pre)
+        xs_low = (x * spread_pair(step, pair)).astype(bf16)
+        d_mixed = d_mixed_ref[:, lanes]
+        dy_low = d_mixed.astype(bf16)
+        zero = jnp.zeros_like(dy_low)
+        parts = []
+        for side in range(2):
+            head = 2 * pair + side
+            own = jnp.where(first_half if side == 0 else ~first_half, dy_low, zero)
+            decays = decay_block(cum, cum_t, head, bias)
+            d_products = d_products + decays * nt(own, xs_low)
+            parts.append(tn((decays * products).astype(bf16), dy_low))
+        d_xs = jnp.where(first_half, parts[0], parts[1])
+        d_xs_ref[:, lanes] = d_xs
+        within = within_ref[:, lanes] - spread_pair(skips, pair) * x
+        through = dy_low.astype(f32) * within - xs_low.astype(f32) * d_xs
+        start_low = start_ref[lanes, :]
+        carried = d_mixed * spread_pair(entry, pair)
+        d_c = d_c + mm(carried.astype(bf16), start_low)
+        d_cum = d_cum + head_sums(through + carried * nt(c_low, start_low), pair)
+        skip_grad_ref[:, lanes] = jnp.sum(d_mixed * x, axis=0, keepdims=True)
+    d_products = d_products.astype(bf16)
+    d_bc_ref[:, :STATE] = tn(d_products, c_low)
+    d_bc_ref[:, STATE:] = d_c + mm(d_products, b_low)
+    d_cum_ref[...] = d_cum
+
+
+def carry_back_body(
+    d_mixed_ref,
+    pre_ref,
     joined_ref,
-    within_ref,
+    d_xs_ref,
+    d_bc_in_ref,
+    d_cum_ref,
     start_ref,
     adjoint_ref,
     b_ref,
-    c_ref,
     step_ref,
     cum_ref,
     sig_ref,
@@ -358,31 +422,22 @@
     d_ext_ref,
     d_step_ref,
     conv_ref,
-    skip_grad_ref,
     small_ref,
     ext_ref,
     pad_ref,
 ):
-    seg_row, documents = documents_of(seg_ref)
+    _, documents = documents_of(seg_ref)
     tap_masks = tap_masks_of(documents, ext_ref)
     pad_ref[...] = jnp.zeros_like(pad_ref)
     skips = skip_ref[...]
     cum = cum_ref[...]
-    cum_t = cum.T
     step = step_ref[...]
     b_low = b_ref[...]
-    c_low = c_ref[...]
-    products = nt(c_low, b_low)
-    bias = pair_mask(documents, seg_row)
     end = end_decay(cum, documents)
-    entry = entry_decay(cum, documents)
     gains = jnp.exp(cum[ROWS - 1 : ROWS, :])
-    first_half = lane_index((ROWS, LANES)) < HEAD
     lane = lane_index((1, LANES))
-    d_products = jnp.zeros((ROWS, ROWS), f32)
-    d_b = jnp.zeros((ROWS, STATE), f32)
-    d_c = jnp.zeros((ROWS, STATE), f32)
-    d_cum = jnp.zeros((ROWS, LANES), f32)
+    d_b = d_bc_in_ref[:, :STATE]
+    d_cum = d_cum_ref[...]
     d_step = jnp.zeros((ROWS, LANES), f32)
     d_last = jnp.zeros((8, LANES), f32)
     d_whole = jnp.zeros((1, LANES), f32)
@@ -393,51 +448,31 @@
         x = pre * sig
         steps = spread_pair(step, pair)
         ends = spread_pair(end, pair)
-        entries = spread_pair(entry, pair)
-        skip = spread_pair(skips, pair)
         xs = x * steps
-        xs_low = xs.astype(bf16)
-        d_mixed = d_mixed_ref[:, lanes]
-        dy_low = d_mixed.astype(bf16)
-        zero = jnp.zeros_like(dy_low)
-        parts = []
-        for side in range(2):
-            head = 2 * pair + side
-            own = jnp.where(first_half if side == 0 else ~first_half, dy_low, zero)
-            decays = decay_block(cum, cum_t, head, bias)
-            d_products = d_products + decays * nt(own, xs_low)
-            parts.append(tn((decays * products).astype(bf16), dy_low))
-        d_xs = jnp.where(first_half, parts[0], parts[1])
-        within = within_ref[:, lanes] - skip * x
-        through = dy_low.astype(f32) * within - xs_low.astype(f32) * d_xs
-        start_low = start_ref[lanes, :]
         adjoint_low = adjoint_ref[lanes, :]
         d_ended = nt(b_low, adjoint_low) * ends
         d_b = d_b + mm((xs * ends).astype(bf16), adjoint_low)
         at_end = xs * d_ended
-        carried = nt(c_low, start_low) * entries
-        d_c = d_c + mm((d_mixed * entries).astype(bf16), start_low)
-        d_cum = d_cum + head_sums(through + d_mixed * carried - at_end, pair)
-        d_xs = d_xs + d_ended
+        d_cum = d_cum - head_sums(at_end, pair)
+        d_xs = d_xs_ref[:, lanes] + d_ended
         d_step = d_step + head_sums(x * d_xs, pair)
         end_sum = jnp.sum(at_end, axis=0, keepdims=True)
         d_last = d_last + head_sums(jnp.broadcast_to(end_sum, (8, LANES)), pair)
-        meeting = start_low.astype(f32) * adjoint_low.astype(f32)
+        meeting = start_ref[lanes, :].astype(f32) * adjoint_low.astype(f32)
         for side in range(2):
-            whole = jnp.sum(
+            whole_sum = jnp.sum(
                 jnp.sum(meeting[side * HEAD : (side + 1) * HEAD, :], axis=0, keepdims=True),
                 axis=1,
                 keepdims=True,
             )
-            d_whole = d_whole + jnp.where(lane == 2 * pair + side, whole, 0.0)
-        skip_grad_ref[:, lanes] = jnp.sum(d_mixed * x, axis=0, keepdims=True)
-        d_pre = (steps * d_xs + skip * d_mixed) * (sig + x * (1.0 - sig))
+            d_whole = d_whole + jnp.where(lane == 2 * pair + side, whole_sum, 0.0)
+        d_act = steps * d_xs + spread_pair(skips, pair) * d_mixed_ref[:, lanes]
+        d_pre = d_act * (sig + x * (1.0 - sig))
         d_ext_ref[:, lanes] = conv_back(
             d_pre, joined_ref, lanes, lanes, taps_ref[:, lanes], tap_masks, pad_ref, conv_ref
         ).astype(bf16)
-    d_products = d_products.astype(bf16)
-    d_bc_ref[:, :STATE] = (d_b + tn(d_products, c_low)).astype(bf16)
-    d_bc_ref[:, STATE:] = (d_c + mm(d_products, b_low)).astype(bf16)
+    d_bc_ref[:, :STATE] = d_b.astype(bf16)
+    d_bc_ref[:, STATE:] = d_bc_in_ref[:, STATE:].astype(bf16)
     tri = (row_index((ROWS, ROWS)) <= lane_index((ROWS, ROWS))).astype(f32)
     d_decay = exact(tri, d_cum) + (d_last[0:1, :] + gains * d_whole)
     d_raw = (d_step + d_decay * to_lanes(-jnp.exp(decay_log_ref[...]))) * sig_ref[...]
@@ -478,7 +513,7 @@
     weights = jnp.where(first, wbc[:, :STATE], wbc[:, STATE:])
     both = nt(dx_ref[...], win_ref[:, :LOCAL]) + nt(half, weights)
     out_ref[:HALO, :] = both[:HALO, :].astype(bf16)
-    own = nt(dz_ref[...], win_ref[:, LOCAL:]) + nt(dst_ref[:, :HEADS], wst_ref[...])
+    own = nt(dz_ref[...], win_ref[:, LOCAL:]) + mm(dst_ref[:, :HEADS], wst_ref[...])
     out_ref[HALO:, :] = (both[HALO:, :] + own).astype(bf16)
 
 
@@ -503,9 +538,12 @@
     grad_ref[...] = (out_grad_ref[...].astype(f32) + own).astype(bf16)
 
 
+def x_grad_body(normed_ref, dx_ref, grad_ref):
+    grad_ref[...] = tn(normed_ref[...], dx_ref[...]).astype(bf16)
+
+
 def bundle_body(
     normed_ref,
-    dx_ref,
     dbc_ref,
     dst_ref,
     conv_ref,
@@ -517,14 +555,13 @@
     bundle_ref,
 ):
     half = D // 2
-    bundle_ref[:, :LOCAL] = tn(normed_ref[...], dx_ref[...]).astype(bf16)
     first = lax.axis_index("tensor") == 0
     share = jnp.where(first, normed_ref[:, :half], normed_ref[:, half:])
-    bundle_ref[:half, LOCAL:] = tn(share, dbc_ref[...]).astype(bf16)
+    bundle_ref[:half, :] = tn(share, dbc_ref[...]).astype(bf16)
     steps = tn(dst_ref[...], normed_ref[HALO:, :])
     for part in range(4):
         at = half + part * HEADS
-        bundle_ref[at : at + HEADS, LOCAL:] = steps[:HEADS, part * 256 : part * 256 + 256].astype(bf16)
+        bundle_ref[at : at + HEADS, :] = steps[:HEADS, part * 256 : part * 256 + 256].astype(bf16)
     row = half + 4 * HEADS
     pieces = []
     for part in range(4):
@@ -544,17 +581,18 @@
         )
     )
     pieces.append(jnp.zeros((8, 256), f32))
-    bundle_ref[row : row + 64, LOCAL:] = jnp.concatenate(pieces, axis=0).astype(bf16)
-    bundle_ref[row + 64 :, LOCAL:] = jnp.zeros((half - 4 * HEADS - 64, 256), bf16)
-
-
-def total_body(received_ref, out_ref):
-    total = jnp.zeros(received_ref.shape[1:], f32)
-    for k in range(DEVICES):
-        total = total + received_ref[k].astype(f32)
-    total = total.astype(bf16)
-    for k in range(DEVICES):
-        out_ref[k] = total
+    bundle_ref[row : row + 64, :] = jnp.concatenate(pieces, axis=0).astype(bf16)
+    bundle_ref[row + 64 :, :] = jnp.zeros((half - 4 * HEADS - 64, 256), bf16)
+
+
+def total_body(x_ref, few_ref, out_ref):
+    for received_ref, lanes in ((x_ref, slice(0, LOCAL)), (few_ref, slice(LOCAL, LOCAL + 256))):
+        total = jnp.zeros(received_ref.shape[1:], f32)
+        for k in range(DEVICES):
+            total = total + received_ref[k].astype(f32)
+        total = total.astype(bf16)
+        for k in range(DEVICES):
+            out_ref[k, :, lanes] = total
 
 
 def few_body(
@@ -576,9 +614,8 @@
     bc_ref[:, 0, :] = grads[:, :STATE]
     bc_ref[:, 1, :] = grads[:, STATE:]
     rest = final_ref[half : half + 128, LOCAL:].astype(f32)
-    steps = jnp.concatenate([rest[part * HEADS : (part + 1) * HEADS] for part in range(4)], axis=1)
-    steps = jnp.concatenate([steps, jnp.zeros((LANES - HEADS, D), f32)], axis=0)
-    step_ref[...] = steps.T[:, :HEADS]
+    for part in range(4):
+        step_ref[:, part * 256 : part * 256 + 256] = rest[part * HEADS : (part + 1) * HEADS]
     conv = jnp.concatenate([rest[64 + part * 8 : 72 + part * 8] for part in range(4)], axis=1)
     conv_ref[...] = conv[:4]
     conv_bias_ref[...] = conv[4:5]
@@ -604,9 +641,10 @@
     skip_ref[...] = total[:, :HEADS]
 
 
-def large_body(final_ref, gate_ref, grad_in_ref):
-    grad_in_ref[:, 0, :] = final_ref[:, :LOCAL].astype(f32)
-    grad_in_ref[:, 1, :] = gate_ref[...]
+def large_body(final_ref, gate_ref, out_ref, grad_in_ref, grad_out_ref):
+    grad_in_ref[:, 0, :] = final_ref[...].astype(f32)
+    grad_in_ref[:, 1, :] = gate_ref[...].astype(f32)
+    grad_out_ref[...] = out_ref[...].astype(f32)
 
 
 def swapped(values):
@@ -641,6 +679,7 @@
     bc_taps = bc_conv_weight.reshape(4, 2 * STATE)
     segs = segment_ids[None]
     skip = skip_gain[None]
+    step_rows = step_weight.T
     gain_row = gate_gain[None]
     dg = nt(cotangent, out_weight)
     ext_scratch = pltpu.VMEM((ROWS + 8, LANES), f32)
@@ -649,7 +688,6 @@
         normed_ext,
         joined,
         pre,
-        gate,
         b_low,
         c_low,
         step,
@@ -663,7 +701,6 @@
             ((EXT, D), bf16),
             ((EXT, LOCAL + 2 * STATE), f32),
             ((ROWS, LOCAL + 2 * STATE), f32),
-            ((ROWS, LOCAL), f32),
             ((ROWS, STATE), bf16),
             ((ROWS, STATE), bf16),
             ((ROWS, LANES), f32),
@@ -678,7 +715,7 @@
             norm_gain[None],
             win,
             wbc,
-            step_weight,
+            step_rows,
             conv_weight,
             conv_bias[None],
             bc_taps,
@@ -687,13 +724,21 @@
             step_bias[None],
             decay_log[None],
         ),
-        scratch=[ext_scratch, pltpu.VMEM((D, LANES), bf16)],
+        scratch=[ext_scratch, pltpu.VMEM((LANES, D), bf16)],
+        blocks={3: ((D, LOCAL), (0, 0))},
     )
     pieces = lax.all_to_all(state, CONTEXT, 0, 0, tiled=True)
+    (gate,) = kernel_call(
+        gate_proj_body,
+        [((ROWS, LOCAL), f32)],
+        (normed_ext, win),
+        blocks={1: ((D, LOCAL), (0, 1))},
+    )
     (within,) = kernel_call(
         within_body,
         [((ROWS, LOCAL), f32)],
         (pre, step, cum, b_low, c_low, segs, skip),
+        cost=12_000_000,
     )
     (starts,) = kernel_call(scan_body, [((16, HEAD, STATE), bf16)], (pieces,))
     start = lax.all_to_all(starts, CONTEXT, 0, 0, tiled=True).reshape(LOCAL, STATE)
@@ -714,91 +759,153 @@
         (sums, swapped(sums), mixed, gate, dg, gain_row, c_low, cum, segs),
     )
     normed = normed_ext[HALO:]
-    grad_out, grad_gate, d_start = lax.optimization_barrier(
-        (tn(gnorm, cotangent), tn(normed, d_gate), d_start)
-    )
+    grad_out = tn(gnorm, cotangent).astype(bf16)
+    grad_gate = tn(normed, d_gate).astype(bf16)
     grad_out, grad_gate = lax.psum((grad_out, grad_gate), EVERYONE)
-    received = lax.all_to_all(d_start, CONTEXT, 0, 0, tiled=True)
-    (adjoints,) = kernel_call(
-        scan_back_body, [((16, HEAD, STATE), bf16)], (pieces, received)
-    )
-    adjoint = lax.all_to_all(adjoints, CONTEXT, 0, 0, tiled=True).reshape(LOCAL, STATE)
-    out_terms = mm(gnorm, out_weight).astype(bf16)
-    kept = lax.dynamic_slice_in_dim(out_terms, side * width, width, 1)
-    given = lax.dynamic_slice_in_dim(out_terms, (1 - side) * width, width, 1)
-    hidden_out = (
-        hidden_in.astype(f32) + kept.astype(f32) + swapped(given).astype(f32)
-    ).astype(bf16)
-    d_bc, d_ext, d_step, conv_grads, skip_grads, small = kernel_call(
-        back_body,
-        [
-            ((ROWS, 2 * STATE), bf16),
-            ((EXT, LOCAL), bf16),
-            ((ROWS, LANES), bf16),
-            ((8, LOCAL), f32),
-            ((1, LOCAL), f32),
-            ((8, LANES), f32),
-        ],
-        (
-            d_mixed,
-            pre,
-            joined,
-            within,
-            start,
-            adjoint,
-            b_low,
-            c_low,
-            step,
-            cum,
-            sig,
-            decay,
-            segs,
-            decay_log[None],
-            skip,
-            conv_weight,
-        ),
-        scratch=[ext_scratch, pad_scratch],
-    )
-    d_bc_ext, bc_conv_grads = kernel_call(
-        bc_back_body,
-        [((EXT, 2 * STATE), bf16), ((8, 2 * STATE), f32)],
-        (d_bc, swapped(d_bc), pre, joined, segs, bc_taps),
-        scratch=[ext_scratch, pad_scratch],
-    )
-    (terms,) = kernel_call(
-        terms_body,
-        [((EXT, D), bf16)],
-        (d_ext, d_gate, d_step, d_bc_ext, win, step_weight, wbc),
-    )
-    other_terms = swapped(terms)
-    halo_terms = (terms[:HALO].astype(f32) + other_terms[:HALO].astype(f32)).astype(bf16)
-    returned = lax.ppermute(halo_terms, CONTEXT, [(i + 1, i) for i in range(15)])
-    hidden_grad, grad_norm = kernel_call(
-        hidden_body,
-        [((ROWS, width), bf16), ((1, width), f32)],
-        (gathered, terms, other_terms, returned, norm_gain[None], out_grad),
-    )
-    (bundle,) = kernel_call(
-        bundle_body,
-        [((D, LOCAL + 256), bf16)],
-        (
-            normed_ext,
-            d_ext,
-            d_bc_ext,
-            d_step,
-            conv_grads,
-            bc_conv_grads,
-            grad_gate_gain,
-            grad_norm,
-            skip_grads,
-            small,
-        ),
-    )
-    scattered = lax.all_to_all(
-        bundle.reshape(DEVICES, 16, LOCAL + 256), EVERYONE, 0, 0, tiled=True
-    )
-    (spread,) = kernel_call(total_body, [(scattered.shape, bf16)], (scattered,))
-    final = lax.all_to_all(spread, EVERYONE, 0, 0, tiled=True).reshape(D, LOCAL + 256)
+    def later(
+        d_start,
+        gnorm,
+        d_mixed,
+        d_gate,
+        grad_gate_gain,
+        start,
+        pieces,
+        within,
+        normed_ext,
+        joined,
+        pre,
+        gathered,
+        win,
+    ):
+        received = lax.all_to_all(d_start, CONTEXT, 0, 0, tiled=True)
+        (adjoints,) = kernel_call(
+            scan_back_body, [((16, HEAD, STATE), bf16)], (pieces, received)
+        )
+        adjoint = lax.all_to_all(adjoints, CONTEXT, 0, 0, tiled=True).reshape(LOCAL, STATE)
+        out_terms = mm(gnorm, out_weight).astype(bf16)
+        kept = lax.dynamic_slice_in_dim(out_terms, side * width, width, 1)
+        given = lax.dynamic_slice_in_dim(out_terms, (1 - side) * width, width, 1)
+        hidden_out = (
+            hidden_in.astype(f32) + kept.astype(f32) + swapped(given).astype(f32)
+        ).astype(bf16)
+        d_xs, d_bc_part, d_cum, skip_grads = kernel_call(
+            back_body,
+            [
+                ((ROWS, LOCAL), f32),
+                ((ROWS, 2 * STATE), f32),
+                ((ROWS, LANES), f32),
+                ((1, LOCAL), f32),
+            ],
+            (d_mixed, pre, within, start, b_low, c_low, step, cum, segs, skip),
+            cost=20_000_000,
+        )
+        d_bc, d_ext, d_step, conv_grads, small = kernel_call(
+            carry_back_body,
+            [
+                ((ROWS, 2 * STATE), bf16),
+                ((EXT, LOCAL), bf16),
+                ((ROWS, LANES), bf16),
+                ((8, LOCAL), f32),
+                ((8, LANES), f32),
+            ],
+            (
+                d_mixed,
+                pre,
+                joined,
+                d_xs,
+                d_bc_part,
+                d_cum,
+                start,
+                adjoint,
+                b_low,
+                step,
+                cum,
+                sig,
+                decay,
+                segs,
+                decay_log[None],
+                skip,
+                conv_weight,
+            ),
+            scratch=[ext_scratch, pad_scratch],
+        )
+        (grad_x,) = kernel_call(x_grad_body, [((D, LOCAL), bf16)], (normed_ext, d_ext))
+        scattered_x = lax.all_to_all(
+            grad_x.reshape(DEVICES, 16, LOCAL), EVERYONE, 0, 0, tiled=True
+        )
+        d_bc_ext, bc_conv_grads = kernel_call(
+            bc_back_body,
+            [((EXT, 2 * STATE), bf16), ((8, 2 * STATE), f32)],
+            (d_bc, swapped(d_bc), pre, joined, segs, bc_taps),
+            scratch=[ext_scratch, pad_scratch],
+            cost=BC_COST,
+        )
+        (terms,) = kernel_call(
+            terms_body,
+            [((EXT, D), bf16)],
+            (d_ext, d_gate, d_step, d_bc_ext, win, step_rows, wbc),
+            cost=TERMS_COST,
+        )
+        other_terms = swapped(terms)
+        halo_terms = (terms[:HALO].astype(f32) + other_terms[:HALO].astype(f32)).astype(bf16)
+        returned = lax.ppermute(halo_terms, CONTEXT, [(i + 1, i) for i in range(15)])
+        hidden_grad, grad_norm = kernel_call(
+            hidden_body,
+            [((ROWS, width), bf16), ((1, width), f32)],
+            (gathered, terms, other_terms, returned, norm_gain[None], out_grad),
+            cost=HIDDEN_COST,
+        )
+        (bundle,) = kernel_call(
+            bundle_body,
+            [((D, 256), bf16)],
+            (
+                normed_ext,
+                d_bc_ext,
+                d_step,
+                conv_grads,
+                bc_conv_grads,
+                grad_gate_gain,
+                grad_norm,
+                skip_grads,
+                small,
+            ),
+            cost=BUNDLE_COST,
+        )
+        bundle, scattered_x = lax.optimization_barrier((bundle, scattered_x))
+        scattered = lax.all_to_all(
+            bundle.reshape(DEVICES, 16, 256), EVERYONE, 0, 0, tiled=True
+        )
+        (spread,) = kernel_call(
+            total_body, [((DEVICES, 16, LOCAL + 256), bf16)], (scattered_x, scattered)
+        )
+        final = lax.all_to_all(spread, EVERYONE, 0, 0, tiled=True).reshape(D, LOCAL + 256)
+        return hidden_out, hidden_grad, final
+
+    def nothing(*_):
+        return (
+            jnp.zeros((ROWS, width), bf16),
+            jnp.zeros((ROWS, width), bf16),
+            jnp.zeros((D, LOCAL + 256), bf16),
+        )
+
+    hidden_out, hidden_grad, final = lax.cond(
+        segment_ids[0] >= 0,
+        later,
+        nothing,
+        d_start,
+        gnorm,
+        d_mixed,
+        d_gate,
+        grad_gate_gain,
+        start,
+        pieces,
+        within,
+        normed_ext,
+        joined,
+        pre,
+        gathered,
+        win,
+    )
     half = D // 2
     (
         grad_bc,
@@ -816,7 +923,7 @@
         few_body,
         [
             ((half, 2, STATE), f32),
-            ((D, HEADS), f32),
+            ((HEADS, D), f32),
             ((4, LOCAL), f32),
             ((1, LOCAL), f32),
             ((4, 2, STATE), f32),
@@ -829,14 +936,24 @@
         ],
         (final,),
     )
-    (grad_in,) = kernel_call(large_body, [((D, 2, LOCAL), f32)], (final, grad_gate))
+    rows = pl.BlockSpec((D // 8, LOCAL), lambda i: (i, 0))
+    grad_in, grad_out = pl.pallas_call(
+        large_body,
+        grid=(8,),
+        out_shape=[
+            jax.ShapeDtypeStruct((D, 2, LOCAL), f32),
+            jax.ShapeDtypeStruct((LOCAL, D), f32),
+        ],
+        in_specs=[rows] * 3,
+        out_specs=[pl.BlockSpec((D // 8, 2, LOCAL), lambda i: (i, 0, 0)), rows],
+    )(final, grad_gate, grad_out)
     return (
         hidden_out,
         hidden_grad,
         total_norm_gain[0],
         grad_in,
         grad_bc,
-        grad_step,
+        grad_step.T,
         grad_conv,
         grad_conv_bias[0],
         grad_bc_conv,

time: 305 us -> 268 us (0.88)
  blocking collectives: 74.5 us -> 48.7 us
  waiting for transfers between devices: 90 us -> 73.5 us
  starting transfers between devices: 32.2 us -> 42.7 us
  local copies, waits for them, and re-layouts: 16.8 us -> 10.3 us
    all_to_all x3 -> x2, blocking collectives: 68.1 us -> 42.5 us  [the longest x1 24.9 us: later(): lax.all_to_all(bundle.reshape(DEVICES, 16, 256), EVERYONE, 0, 0, tiled=True)]
    psum x1, waiting for transfers between devices: 44.9 us -> 29.7 us  [shards(): grad_out, grad_gate = lax.psum((grad_out, grad_gate), EVERYONE)]
    all_to_all x1 -> x3, starting transfers between devices: 6.33 us -> 18.6 us  [the longest x1 9.19 us: later(): lax.all_to_all(grad_x.reshape(DEVICES, 16, LOCAL), EVERYONE, 0, 0, tiled=...]
    unnamed x44 -> x55, local copies, waits for them, and re-layouts: 16.8 us -> 7.04 us
    pallas_call x0 -> x1, Pallas kernels: none -> 9.14 us  [shards(): pl.pallas_call(large_body, grid=(8,), out_shape=[jax.ShapeDtypeStruct((D,...]
    pallas_call x14 -> x16, Pallas kernels: 64.2 us -> 55.7 us  [kernel_call(): pl.pallas_call(body, grid=(1,), out_shape=[jax.ShapeDtypeStruct(shape, ki...]
    all_to_all x1 -> x3, waiting for transfers between devices: 28 us -> 26.5 us  [the longest x1 25.4 us: later(): lax.all_to_all(spread, EVERYONE, 0, 0, tiled=True).reshape(D, LOCAL + 256)]
  transfers between devices with their start and end apart: 10 -> 12, of which waited for: 9 -> 9; matrix products, arithmetic and copies ran while one was open for 5% -> 5% of each run, Pallas kernels for 13% -> 16%
where the time goes in v1:
time: 268 us; the launch traced here: 267 us
  waiting for transfers between devices  73.5 us (27%)
  Pallas kernels  64.9 us (24%)
  blocking collectives  48.7 us (18%)
  starting transfers between devices  42.7 us (16%)
  between operations  15 us (6%)
  local copies, waits for them, and re-layouts  10.3 us (4%)
  matrix products  9.95 us (4%)
    pallas_call x16, Pallas kernels, kernel_call(): pl.pallas_call(body, grid=(1,), out_shape=[jax.ShapeDtypeStruct(shape, ki...  55.7 us
    psum x1, waiting for transfers between devices, shards(): grad_out, grad_gate = lax.psum((grad_out, grad_gate), EVERYONE)  29.7 us
    all_to_all x1, waiting for transfers between devices, later(): lax.all_to_all(spread, EVERYONE, 0, 0, tiled=True).reshape(D, LOCAL + 256)  25.4 us
    all_to_all x1, blocking collectives, later(): lax.all_to_all(bundle.reshape(DEVICES, 16, 256), EVERYONE, 0, 0, tiled=True)  24.9 us
    all_to_all x1, blocking collectives, later(): received = lax.all_to_all(d_start, CONTEXT, 0, 0, tiled=True)  17.6 us
    all_to_all x1, starting transfers between devices, later(): lax.all_to_all(grad_x.reshape(DEVICES, 16, LOCAL), EVERYONE, 0, 0, tiled=...  9.19 us
    pallas_call x1, Pallas kernels, shards(): pl.pallas_call(large_body, grid=(8,), out_shape=[jax.ShapeDtypeStruct((D,...  9.14 us
    ppermute x4, starting transfers between devices, swapped(): return lax.ppermute(values, 'tensor', [(0, 1), (1, 0)])  7.49 us
  transfers between devices with their start and end apart: 12, of which 9 were waited for; matrix products, arithmetic and copies ran while one was open for 5% of the time, Pallas kernels for 16%

profile of v1, /device:TPU:1, one launch (start us, length us, event | category | flops | bytes accessed | tf_op | source)
XLA Modules:
  0.0 266.8 jit_solution(15228370958704725498)
XLA Ops:
  7.2 3.4 %all_gather.6.hidden_ref = bf16[256,1024]{1,0:T(8,128)(2,1)S(1)} all-gather(bf16[256,512]{1,0:T(8,128)(2,1)} %param.18), channel_id=1, replica_groups=mesh['tensor'=2,'dp'=4,'context_0'=4,'context_1'=4] {'tensor'}, dimensions={1}, use_global_device_ids=true | all-gather | bytes 786432 | tf_op jit(solution)/shard_map/all_gather | solution.py:674
  10.6 3.3 %collective-permute-start.4 = (bf16[16,1024]{1,0:T(8,128)(2,1)S(1)}, bf16[16,1024]{1,0:T(8,128)(2,1)S(1)}, u32[]{:S(2)}, u32[]{:S(2)}) collective-permute-start(bf16[16,1024]{1,0:T(8,128)(2,1)S(1)} %slice.20), channel_id=1, source_target_pairs={{0,1},{1,2},{2,3},{3,4},{4,5},{5,6},{6,7},{7,8},{8,9},{9,10},{10,1... | collective-permute-start | bytes 98312 | tf_op jit(solution)/shard_map/ppermute | solution.py:675
  14.6 1.1 copy.36
  15.8 3.8 %copy.31 = bf16[128,8,2,1024]{3,1,2,0:T(8,128)(2,1)S(1)} copy(bf16[128,8,2,1024]{3,2,1,0:T(2,128)(2,1)} %bitcast.47) | data formatting | bytes 8388608
  20.4 5.3 %shard_map.271 = (bf16[272,1024]{1,0:T(8,128)(2,1)S(1)}, f32[272,1280]{1,0:T(8,128)}, f32[256,1280]{1,0:T(8,128)S(1)}, bf16[256,128]{1,0:T(8,128)(2,1)}, bf16[25...) custom-call(bf16[256,1024]{1,0:T(8,128)(2,1)S(1)} %all_gather.6.hidd, ...), custom_call_target="tpu_custom_call" | custom-call | tf_op jit(solution)/shard_map/pallas_call | solution.py:58
  25.6 7.5 %all-to-all-start.5 = ((bf16[16,80,128]{2,1,0:T(8,128)(2,1)}), bf16[16,80,128]{2,1,0:T(8,128)(2,1)S(1)}, u32[]{:S(2)}, u32[]{:S(2)}) async-start(bf16[16,80,128]{2,1,0:T(8,128)(2,1)} %get-tuple-element.161), calls=%async_computation.5 | async-start | bytes 655360 | tf_op jit(solution)/shard_map/all_to_all | solution.py:730
  33.1 2.7 %all_gather.7 = bf16[256,1024]{1,0:T(8,128)(2,1)S(1)} all-gather(bf16[256,512]{1,0:T(8,128)(2,1)S(1)} %copy-done.18), channel_id=1, replica_groups=mesh['tensor'=2,'dp'=4,'context_0'=4,'context_1'=4] {'tensor'}, dimensions={1}, use_global_device_ids=true | all-gather | bytes 786432 | tf_op jit(solution)/shard_map/all_gather | solution.py:676
  35.9 5.7 %all-to-all-done.5.pieces_ref = bf16[16,80,128]{2,1,0:T(8,128)(2,1)S(1)} async-done(((bf16[16,80,128]{2,1,0:T(8,128)(2,1)}), bf16[16,80,128]{2,1,0:T(8,128)(2,1)S(1)}, u32[]{:S(2)}, u32[]{:S(2)}) %all-to-all-start.5) | async-done | bytes 327712 | tf_op jit(solution)/shard_map/all_to_all | solution.py:730
  42.4 4.2 %all-to-all-start.6 = ((bf16[16,64,128]{2,1,0:T(8,128)(2,1)}), bf16[16,64,128]{2,1,0:T(8,128)(2,1)}, u32[]{:S(2)}, u32[]{:S(2)}) async-start(bf16[16,64,128]{2,1,0:T(8,128)(2,1)} %shard_map.273), calls=%async_computation.6 | async-start | bytes 524288 | tf_op jit(solution)/shard_map/all_to_all | solution.py:744
  46.7 3.3 %fusion.1.dg_ref = f32[256,1024]{1,0:T(8,128)} fusion(bf16[256,1024]{1,0:T(8,128)(2,1)S(1)} %all_gather.7, bf16[1024,1024]{1,0:T(8,128)(2,1)} %param.32), kind=kOutput, calls=%fused_computation.9 | convolution fusion | flops 536870912 | bytes 3670016 | tf_op jit(solution)/shard_map/dot_general | solution.py:39
  50.1 3.3 %shard_map.274.gate_ref = f32[256,1024]{1,0:T(8,128)} custom-call(bf16[272,1024]{1,0:T(8,128)(2,1)S(1)} %get-tuple-element.162.normed_ref, bf16[1024,2048]{1,0:T(8,128)(2,1)} %bitcast.42), custom_call_target="tpu_custom_call" | custom-call | tf_op jit(solution)/shard_map/pallas_call | solution.py:58
  53.4 1.6 shard_map.272.within_ref
  55.1 3.5 %shard_map.275 = (f32[256,1024]{1,0:T(8,128)}, f32[256,128]{1,0:T(8,128)}) custom-call(f32[256,1024]{1,0:T(8,128)S(1)} %shard_map.272.within_ref, bf16[1024,128]{1,0:T(8,128)(2,1)} %bitcast.15.start_ref, bf16[256,128]{1,0:T(8,128)(2,1)S(1)} %get-tuple-element.160.c_ref, f32[256,128]{1,0:T(8,128)} %get-tuple-element.158.cum_ref, s32[1,256]{1,0:T(1,128)S(1)} %bitcast.56, ...), custom_call_target="tpu_custom_call" | custom-call | tf_op jit(solution)/shard_map/pallas_call | solution.py:58
  58.6 2.1 collective-permute-start.5
  60.7 1.2 collective-permute-done.5.other_ref
  62.5 4.3 %shard_map.276 = (bf16[256,1024]{1,0:T(8,128)(2,1)S(1)}, f32[256,1024]{1,0:T(8,128)}, bf16[256,1024]{1,0:T(8,128)(2,1)S(1)}, f32[1,1024]{1,0:T(1,128)}, bf16[16,64,128]{2,1,0:T(8,128)(2,1)}) custom-call(f32[256,128]{1,0:T(8,128)} %get-tuple-element.163.sums_ref, f32[256,128]{1,0:T(8,128)} %copy-done.27, f32[256,1024]{1,0:T(8,128)} %get-tuple-element.164.mixed_ref, ...), custom_call_target="tpu_custom_call" | custom-call | tf_op jit(solution)/shard_map/pallas_call | solution.py:58
  66.8 2.2 convolution_convert_fusion.1
  69.0 2.1 convolution_convert_fusion.2
  71.1 1.2 slice.15
  73.1 145.0 %conditional.1 = (bf16[256,512]{1,0:T(8,128)(2,1)}, bf16[256,512]{1,0:T(8,128)(2,1)}, bf16[1024,1280]{1,0:T(8,128)(2,1)}) conditional(s32[]{:T(128)} %bitcast.6, () %tuple.17, (bf16[256,512]{1,0:T(8,128)(2,1)}, bf16[256,1024]{1,0:T(8,128)(2,1)}, bf16[1024,1024]{1,0:T(8,128)(2,1)}, s32[]{:T(128)}, f32[256,1024]{1,0:T(8,128)}, ...), branch_computations={%region_0.0_spmd, %region_1.0_spmd} | conditional | flops 537985024 | bytes 108072624 | solution.py:891
  73.1 17.6 %all_to_all.30.grads_ref = bf16[16,64,128]{2,1,0:T(8,128)(2,1)} all-to-all(bf16[16,64,128]{2,1,0:T(8,128)(2,1)} %get-tuple-element.82), channel_id=1, replica_groups=mesh['tensor'=2,'dp'=4,'context_0'=4,'context_1'=4] {'context_0','contex..., dimensions={0} | all-to-all | bytes 524288 | tf_op jit(solution)/shard_map/cond/branch_1_fun/all_to_all | solution.py:780
  90.7 1.7 branch_1_fun.10
  92.4 3.8 %all-to-all-start.1 = ((bf16[16,64,128]{2,1,0:T(8,128)(2,1)}), bf16[16,64,128]{2,1,0:T(8,128)(2,1)S(1)}, u32[]{:S(2)}, u32[]{:S(2)}) async-start(bf16[16,64,128]{2,1,0:T(8,128)(2,1)} %branch_1_fun.10), calls=%async_computation.1 | async-start | bytes 524288 | tf_op jit(solution)/shard_map/cond/branch_1_fun/all_to_all | solution.py:784
  96.2 6.3 %branch_1_fun.9 = (f32[256,1024]{1,0:T(8,128)}, f32[256,256]{1,0:T(8,128)}, f32[256,128]{1,0:T(8,128)}, f32[1,1024]{1,0:T(1,128)}) custom-call(f32[256,1024]{1,0:T(8,128)} %get-tuple-element.67.d_mixed_ref, f32[256,1280]{1,0:T(8,128)S(1)} %get-tuple-element.68.pre_ref, f32[256,1024]{1,0:T(8,128)S(1)} %get-tuple-element.70.within_ref, ...), custom_call_target="tpu_custom_call" | custom-call | bytes 20000000 | tf_op jit(solution)/shard_map/cond/branch_1_fun/pallas_call | solution.py:58
  102.5 1.1 all-to-all-done.1
  104.3 6.9 %branch_1_fun.11 = (bf16[256,256]{1,0:T(8,128)(2,1)}, bf16[272,1024]{1,0:T(8,128)(2,1)}, bf16[256,128]{1,0:T(8,128)(2,1)}, f32[8,1024]{1,0:T(8,128)}, f32[8,128]{1,0:T(8,128)}) custom-call(f32[256,1024]{1,0:T(8,128)} %get-tuple-element.67.d_mixed_ref, f32[256,1280]{1,0:T(8,128)S(1)} %get-tuple-element.68.pre_ref, f32[272,1280]{1,0:T(8,128)} %get-tuple-element.69.joined_ref, ...), custom_call_target="tpu_custom_call" | custom-call | tf_op jit(solution)/shard_map/cond/branch_1_fun/pallas_call | solution.py:58
  111.2 3.7 %branch_1_fun.16 = bf16[1024,1024]{1,0:T(8,128)(2,1)} custom-call(bf16[272,1024]{1,0:T(8,128)(2,1)S(1)} %get-tuple-element.99.normed_ref, bf16[272,1024]{1,0:T(8,128)(2,1)} %get-tuple-element.87.dx_ref), custom_call_target="tpu_custom_call" | custom-call | tf_op jit(solution)/shard_map/cond/branch_1_fun/pallas_call | solution.py:58
  114.9 9.2 %all-to-all-start.2 = ((bf16[64,16,1024]{2,1,0:T(8,128)(2,1)}), bf16[64,16,1024]{2,1,0:T(8,128)(2,1)}, u32[]{:S(2)}, u32[]{:S(2)}) async-start(bf16[64,16,1024]{2,1,0:T(8,128)(2,1)} %bitcast.44), calls=%async_computation.2 | async-start | bytes 4194304 | tf_op jit(solution)/shard_map/cond/branch_1_fun/all_to_all | solution.py:833
  124.1 2.3 collective-permute-start.1
  126.4 1.0 collective-permute-done.1.other_ref
  128.1 2.1 branch_1_fun.12
  130.2 4.9 %branch_1_fun.13.terms_ref = bf16[272,1024]{1,0:T(8,128)(2,1)} custom-call(bf16[272,1024]{1,0:T(8,128)(2,1)} %get-tuple-element.87.dx_ref, bf16[256,1024]{1,0:T(8,128)(2,1)S(1)} %copy-done.12, bf16[256,128]{1,0:T(8,128)(2,1)} %get-tuple-element.89.dst_ref, bf16[272,256]{1,0:T(8,128)(2,1)} %get-tuple-element.92.dbc_ref, ...), custom_call_target="tpu_custom_call" | custom-call | bytes 15000000 | tf_op jit(solution)/shard_map/cond/branch_1_fun/pallas_call | solution.py:58
  135.5 1.8 collective-permute-done.2.other_ref
  138.1 1.6 collective-permute-start.3
  139.6 6.4 %collective-permute-done.3.returned_ref = bf16[16,1024]{1,0:T(8,128)(2,1)S(1)} collective-permute-done((bf16[16,1024]{1,0:T(8,128)(2,1)S(1)}, bf16[16,1024]{1,0:T(8,128)(2,1)S(1)}, u32[]{:S(2)}, u32[]{:S(2)}) %collective-permute-start.3) | collective-permute-done | bytes 32800 | tf_op jit(solution)/shard_map/cond/branch_1_fun/ppermute | solution.py:851
  146.6 2.5 branch_1_fun.14
  149.1 2.2 branch_1_fun.15
  151.3 24.9 %all_to_all.31.few_ref = bf16[64,16,256]{2,1,0:T(8,128)(2,1)} all-to-all(bf16[64,16,256]{2,1,0:T(8,128)(2,1)} %bitcast.48), channel_id=1, replica_groups=mesh['tensor'=2,'dp'=4,'context_0'=4,'context_1'=4] {'dp','context_0','c..., dimensions={0} | all-to-all | bytes 1048576 | tf_op jit(solution)/shard_map/cond/branch_1_fun/all_to_all | solution.py:875
  176.2 3.6 %branch_1_fun.17 = bf16[64,16,1280]{2,1,0:T(8,128)(2,1)} custom-call(bf16[64,16,1024]{2,1,0:T(8,128)(2,1)} %all-to-all-done.2.x_ref, bf16[64,16,256]{2,1,0:T(8,128)(2,1)} %all_to_all.31.few_ref), custom_call_target="tpu_custom_call" | custom-call | tf_op jit(solution)/shard_map/cond/branch_1_fun/pallas_call | solution.py:58
  179.8 5.7 %all-to-all-start.4 = ((bf16[64,16,1280]{2,1,0:T(8,128)(2,1)}), bf16[64,16,1280]{2,1,0:T(8,128)(2,1)}, u32[]{:S(2)}, u32[]{:S(2)}) async-start(bf16[64,16,1280]{2,1,0:T(8,128)(2,1)} %branch_1_fun.17), calls=%async_computation.4 | async-start | bytes 5242880 | tf_op jit(solution)/shard_map/cond/branch_1_fun/all_to_all | solution.py:881
  185.6 2.3 convolution_convert_fusion
  188.0 2.7 %collective-permute-start = (bf16[256,512]{1,0:T(8,128)(2,1)S(1)}, bf16[256,512]{1,0:T(8,128)(2,1)S(1)}, u32[]{:S(2)}, u32[]{:S(2)}) collective-permute-start(bf16[256,512]{1,0:T(8,128)(2,1)S(1)} %constant_dynamic-slice_fusion), channel_id=1, source_target_pairs={{0,64},{64,0},{1,65},{65,1},{2,66},{66,2},{3,67},{67,3},{4,68},{68... | collective-permute-start | bytes 786440 | tf_op jit(solution)/shard_map/cond/branch_1_fun/ppermute | solution.py:651
  190.7 1.2 collective-permute-done
  191.8 0.8 add_convert_fusion
  192.7 25.4 %all-to-all-done.4 = bf16[64,16,1280]{2,1,0:T(8,128)(2,1)} async-done(((bf16[64,16,1280]{2,1,0:T(8,128)(2,1)}), bf16[64,16,1280]{2,1,0:T(8,128)(2,1)}, u32[]{:S(2)}, u32[]{:S(2)}) %all-to-all-start.4) | async-done | bytes 2621472 | tf_op jit(solution)/shard_map/cond/branch_1_fun/all_to_all | solution.py:881
  218.1 3.0 %shard_map.277 = (f32[512,2,128]{2,1,0:T(2,128)}, f32[16,1024]{1,0:T(8,128)}, f32[4,1024]{1,0:T(4,128)}, f32[1,1024]{1,0:T(1,128)}, f32[4,2,128]{2,1,0:T(2,128)}...) custom-call(bf16[1024,1280]{1,0:T(8,128)(2,1)} %get-tuple-element.17, ...), custom_call_target="tpu_custom_call" | custom-call | tf_op jit(solution)/shard_map/pallas_call | solution.py:58
  221.1 29.7 %all-reduce.3.cloned.1.call-done = (bf16[1024,1024]{1,0:T(8,128)(2,1)}, bf16[1024,1024]{1,0:T(8,128)(2,1)}) async-done(((bf16[1024,1024]{1,0:T(8,128)(2,1)}, bf16[1024,1024]{1,0:T(8,128)(2,1)}), (bf16[1024,1024]{1,0:T(8,128)(2,1)}, bf16[1024,1024]{1,0:T(8,128)(2,1)})) %all-reduce.3.cloned.1.call-update) | async-done | bytes 4194320 | tf_op jit(solution)/shard_map/psum | solution.py:764
  250.8 9.1 %shard_map.278 = (f32[1024,2,1024]{2,1,0:T(2,128)}, f32[1024,1024]{1,0:T(8,128)}) custom-call(bf16[1024,1280]{1,0:T(8,128)(2,1)} %get-tuple-element.175.final_ref, bf16[1024,1024]{1,0:T(8,128)(2,1)} %get-tuple-element.189.gate_ref, bf16[1024,1024]{1,0:T(8,128)(2,1)} %get-tuple-element.190.out_ref), custom_call_target="tpu_custom_call" | custom-call | tf_op jit(solution)/shard_map/pallas_call | solution.py:940
  (93 shorter events, 6.1 us)
Async XLA Ops:
  10.6 9.0 %copy-start.2 = (bf16[256,1024]{1,0:T(8,128)(2,1)}, bf16[256,1024]{1,0:T(8,128)(2,1)S(1)}, u32[]{:S(2)}) copy-start(bf16[256,1024]{1,0:T(8,128)(2,1)S(1)} %all_gather.6.hidden_ref) | copy-start | bytes 1572868
  10.6 9.0 %collective-permute-start.4 = (bf16[16,1024]{1,0:T(8,128)(2,1)S(1)}, bf16[16,1024]{1,0:T(8,128)(2,1)S(1)}, u32[]{:S(2)}, u32[]{:S(2)}) collective-permute-start(bf16[16,1024]{1,0:T(8,128)(2,1)S(1)} %slice.20), channel_id=1, source_target_pairs={{0,1},{1,2},{2,3},{3,4},{4,5},{5,6},{6,7},{7,8},{8,9},{9,10},{10,1... | collective-permute-start | bytes 98312 | tf_op jit(solution)/shard_map/ppermute | solution.py:675
  14.6 5.1 %copy-start.33 = (f32[1,4,2,128]{3,1,2,0:T(4,128)}, f32[1,4,2,128]{3,1,2,0:T(4,128)S(1)}, u32[]{:S(2)}) copy-start(f32[1,4,2,128]{3,1,2,0:T(4,128)S(1)} %copy.37) | copy-start | bytes 12292
  15.7 4.0 %copy-start.4 = (bf16[128,8,2,128]{3,1,2,0:T(8,128)(2,1)}, bf16[128,8,2,128]{3,1,2,0:T(8,128)(2,1)S(1)}, u32[]{:S(2)}) copy-start(bf16[128,8,2,128]{3,1,2,0:T(8,128)(2,1)S(1)} %copy.36) | copy-start | bytes 1572868
  15.7 4.6 %copy-start.25 = (bf16[1024,16]{0,1:T(8,128)(2,1)S(1)}, bf16[1024,16]{0,1:T(8,128)(2,1)}, u32[]{:S(2)}) copy-start(bf16[1024,16]{0,1:T(8,128)(2,1)} %param.23) | copy-start | bytes 98308
  15.8 4.6 %copy-start.29 = (f32[4,1024]{1,0:T(4,128)S(1)}, f32[4,1024]{1,0:T(4,128)}, u32[]{:S(2)}) copy-start(f32[4,1024]{1,0:T(4,128)} %taps_ref.1) | copy-start | bytes 49156
  15.8 4.6 %copy-start.31 = (s32[256]{0:T(256)S(1)}, s32[256]{0:T(256)}, u32[]{:S(2)}) copy-start(s32[256]{0:T(256)} %param.19) | copy-start | bytes 3076
  15.8 4.5 %copy-start.36 = (f32[1024]{0:T(1024)S(1)}, f32[1024]{0:T(1024)}, u32[]{:S(2)}) copy-start(f32[1024]{0:T(1024)} %param.20) | copy-start | bytes 12292
  15.8 4.5 %copy-start.40 = (f32[16]{0:T(128)S(1)}, f32[16]{0:T(128)}, u32[]{:S(2)}) copy-start(f32[16]{0:T(128)} %param.29) | copy-start | bytes 196
  19.6 6.0 %copy-start = (bf16[128,8,2,1024]{3,1,2,0:T(8,128)(2,1)}, bf16[128,8,2,1024]{3,1,2,0:T(8,128)(2,1)S(1)}, u32[]{:S(2)}) copy-start(bf16[128,8,2,1024]{3,1,2,0:T(8,128)(2,1)S(1)} %copy.31) | copy-start | bytes 12582916
  20.3 12.8 %copy-start.18 = (bf16[256,512]{1,0:T(8,128)(2,1)S(1)}, bf16[256,512]{1,0:T(8,128)(2,1)}, u32[]{:S(2)}) copy-start(bf16[256,512]{1,0:T(8,128)(2,1)} %param.33) | copy-start | bytes 786436
  25.6 36.3 %copy-start.15 = (bf16[256,128]{1,0:T(8,128)(2,1)}, bf16[256,128]{1,0:T(8,128)(2,1)S(1)}, u32[]{:S(2)}) copy-start(bf16[256,128]{1,0:T(8,128)(2,1)S(1)} %get-tuple-element.160.c_ref) | copy-start | bytes 196612
  25.6 16.0 %all-to-all-start.5 = ((bf16[16,80,128]{2,1,0:T(8,128)(2,1)}), bf16[16,80,128]{2,1,0:T(8,128)(2,1)S(1)}, u32[]{:S(2)}, u32[]{:S(2)}) async-start(bf16[16,80,128]{2,1,0:T(8,128)(2,1)} %get-tuple-element.161), calls=%async_computation.5 | async-start | bytes 655360 | tf_op jit(solution)/shard_map/all_to_all | solution.py:730
  41.6 8.4 %copy-start.9 = (bf16[16,80,128]{2,1,0:T(8,128)(2,1)}, bf16[16,80,128]{2,1,0:T(8,128)(2,1)S(1)}, u32[]{:S(2)}) copy-start(bf16[16,80,128]{2,1,0:T(8,128)(2,1)S(1)} %all-to-all-done.5.pieces_ref) | copy-start | bytes 983044
  42.4 12.6 %all-to-all-start.6 = ((bf16[16,64,128]{2,1,0:T(8,128)(2,1)}), bf16[16,64,128]{2,1,0:T(8,128)(2,1)}, u32[]{:S(2)}, u32[]{:S(2)}) async-start(bf16[16,64,128]{2,1,0:T(8,128)(2,1)} %shard_map.273), calls=%async_computation.6 | async-start | bytes 524288 | tf_op jit(solution)/shard_map/all_to_all | solution.py:744
  46.6 204.2 %all-reduce.3.cloned.1.call-start = ((), (), s32[]{:S(2)}) async-start(), calls=%async_computation.7 | async-start | bytes 8388608 | tf_op jit(solution)/shard_map/psum | solution.py:764
  50.0 3.4 %copy-start.6 = (f32[256,128]{1,0:T(8,128)S(1)}, f32[256,128]{1,0:T(8,128)}, u32[]{:S(2)}) copy-start(f32[256,128]{1,0:T(8,128)} %get-tuple-element.158.cum_ref) | copy-start | bytes 393220
  50.0 3.4 %copy-start.13 = (f32[256,128]{1,0:T(8,128)S(1)}, f32[256,128]{1,0:T(8,128)}, u32[]{:S(2)}) copy-start(f32[256,128]{1,0:T(8,128)} %get-tuple-element.157.step_ref) | copy-start | bytes 393220
  50.0 3.4 %copy-start.21 = (bf16[256,128]{1,0:T(8,128)(2,1)S(1)}, bf16[256,128]{1,0:T(8,128)(2,1)}, u32[]{:S(2)}) copy-start(bf16[256,128]{1,0:T(8,128)(2,1)} %get-tuple-element.159.b_ref) | copy-start | bytes 196612
  50.0 3.4 %copy-start.32 = (s32[256]{0:T(256)S(1)}, s32[256]{0:T(256)}, u32[]{:S(2)}) copy-start(s32[256]{0:T(256)} %param.19) | copy-start | bytes 3076
  50.0 3.4 %copy-start.38 = (f32[16]{0:T(128)S(1)}, f32[16]{0:T(128)}, u32[]{:S(2)}) copy-start(f32[16]{0:T(128)} %param.30) | copy-start | bytes 196
  55.1 7.5 %copy-start.7 = (f32[256,128]{1,0:T(8,128)S(1)}, f32[256,128]{1,0:T(8,128)}, u32[]{:S(2)}) copy-start(f32[256,128]{1,0:T(8,128)} %get-tuple-element.158.cum_ref) | copy-start | bytes 393220
  58.6 3.3 %collective-permute-start.5 = (f32[256,128]{1,0:T(8,128)}, f32[256,128]{1,0:T(8,128)S(1)}, u32[]{:S(2)}, u32[]{:S(2)}) collective-permute-start(f32[256,128]{1,0:T(8,128)} %get-tuple-element.163.sums_ref), channel_id=1, source_target_pairs={{0,64},{64,0},{1,65},{65,1},{2,66},{66,2},{3,67},{67,3},{4,68},{68... | collective-permute-start | bytes 393224 | tf_op jit(solution)/shard_map/ppermute | solution.py:651
  66.8 2.2 copy-start.23
  66.8 2.2 copy-start.11
  71.1 1.9 copy-start.8
  71.1 2.0 copy-start.10
  71.1 2.0 copy-start.14
  71.1 2.0 copy-start.30
  92.4 11.2 %all-to-all-start.1 = ((bf16[16,64,128]{2,1,0:T(8,128)(2,1)}), bf16[16,64,128]{2,1,0:T(8,128)(2,1)S(1)}, u32[]{:S(2)}, u32[]{:S(2)}) async-start(bf16[16,64,128]{2,1,0:T(8,128)(2,1)} %branch_1_fun.10), calls=%async_computation.1 | async-start | bytes 524288 | tf_op jit(solution)/shard_map/cond/branch_1_fun/all_to_all | solution.py:784
  96.2 8.1 %copy-start.22 = (bf16[256,128]{1,0:T(8,128)(2,1)S(1)}, bf16[256,128]{1,0:T(8,128)(2,1)}, u32[]{:S(2)}) copy-start(bf16[256,128]{1,0:T(8,128)(2,1)} %get-tuple-element.72.b_ref) | copy-start | bytes 196612 | tf_op jit(solution)/shard_map/cond
  114.9 9.2 %copy-start.26 = (bf16[256,256]{1,0:T(8,128)(2,1)S(1)}, bf16[256,256]{1,0:T(8,128)(2,1)}, u32[]{:S(2)}) copy-start(bf16[256,256]{1,0:T(8,128)(2,1)} %get-tuple-element.90.own_ref) | copy-start | bytes 393220 | tf_op jit(solution)/shard_map/cond
  114.9 13.2 %copy-start.1 = (f32[272,1280]{1,0:T(8,128)S(1)}, f32[272,1280]{1,0:T(8,128)}, u32[]{:S(2)}) copy-start(f32[272,1280]{1,0:T(8,128)} %get-tuple-element.69.joined_ref) | copy-start | bytes 4177924 | tf_op jit(solution)/shard_map/cond
  114.9 36.4 %all-to-all-start.2 = ((bf16[64,16,1024]{2,1,0:T(8,128)(2,1)}), bf16[64,16,1024]{2,1,0:T(8,128)(2,1)}, u32[]{:S(2)}, u32[]{:S(2)}) async-start(bf16[64,16,1024]{2,1,0:T(8,128)(2,1)} %bitcast.44), calls=%async_computation.2 | async-start | bytes 4194304 | tf_op jit(solution)/shard_map/cond/branch_1_fun/all_to_all | solution.py:833
  124.1 6.1 %copy-start.5 = (bf16[1024,256]{1,0:T(8,128)(2,1)S(1)}, bf16[1024,256]{1,0:T(8,128)(2,1)}, u32[]{:S(2)}) copy-start(bf16[1024,256]{1,0:T(8,128)(2,1)} %get-tuple-element.95.wbc_ref) | copy-start | bytes 1572868 | tf_op jit(solution)/shard_map/cond
  124.1 6.1 %copy-start.12 = (bf16[256,1024]{1,0:T(8,128)(2,1)S(1)}, bf16[256,1024]{1,0:T(8,128)(2,1)}, u32[]{:S(2)}) copy-start(bf16[256,1024]{1,0:T(8,128)(2,1)} %get-tuple-element.88.dz_ref) | copy-start | bytes 1572868 | tf_op jit(solution)/shard_map/cond
  124.1 3.3 %collective-permute-start.1 = (bf16[256,256]{1,0:T(8,128)(2,1)S(1)}, bf16[256,256]{1,0:T(8,128)(2,1)S(1)}, u32[]{:S(2)}, u32[]{:S(2)}) collective-permute-start(bf16[256,256]{1,0:T(8,128)(2,1)S(1)} %copy-done.26), channel_id=1, source_target_pairs={{0,64},{64,0},{1,65},{65,1},{2,66},{66,2},{3,67},{67,3},{4,68},{68... | collective-permute-start | bytes 393224 | tf_op jit(solution)/shard_map/cond/branch_1_fun/ppermute | solution.py:651
  130.2 16.4 %copy-start.3 = (bf16[256,1024]{1,0:T(8,128)(2,1)S(1)}, bf16[256,1024]{1,0:T(8,128)(2,1)}, u32[]{:S(2)}) copy-start(bf16[256,1024]{1,0:T(8,128)(2,1)} %get-tuple-element.66.hidden_ref) | copy-start | bytes 1572868 | tf_op jit(solution)/shard_map/cond
  130.2 16.4 %copy-start.19 = (bf16[256,512]{1,0:T(8,128)(2,1)S(1)}, bf16[256,512]{1,0:T(8,128)(2,1)}, u32[]{:S(2)}) copy-start(bf16[256,512]{1,0:T(8,128)(2,1)} %get-tuple-element.97.out_grad_ref) | copy-start | bytes 786436 | tf_op jit(solution)/shard_map/cond
  130.2 16.4 %copy-start.37 = (f32[1024]{0:T(1024)S(1)}, f32[1024]{0:T(1024)}, u32[]{:S(2)}) copy-start(f32[1024]{0:T(1024)} %get-tuple-element.96) | copy-start | bytes 12292 | tf_op jit(solution)/shard_map/cond
  130.2 18.9 %copy-start.39 = (f32[1,1024]{1,0:T(1,128)S(1)}, f32[1,1024]{1,0:T(1,128)}, u32[]{:S(2)}) copy-start(f32[1,1024]{1,0:T(1,128)} %get-tuple-element.102.gate_gain_ref) | copy-start | bytes 12292 | tf_op jit(solution)/shard_map/cond
  135.1 2.2 collective-permute-start.2
  137.3 8.7 %copy-start.20 = (bf16[272,1024]{1,0:T(8,128)(2,1)}, bf16[272,1024]{1,0:T(8,128)(2,1)S(1)}, u32[]{:S(2)}) copy-start(bf16[272,1024]{1,0:T(8,128)(2,1)S(1)} %collective-permute-done.2.other_ref) | copy-start | bytes 1671172 | tf_op jit(solution)/shard_map/cond
  138.1 7.9 %collective-permute-start.3 = (bf16[16,1024]{1,0:T(8,128)(2,1)S(1)}, bf16[16,1024]{1,0:T(8,128)(2,1)S(1)}, u32[]{:S(2)}, u32[]{:S(2)}) collective-permute-start(bf16[16,1024]{1,0:T(8,128)(2,1)S(1)} %add_convert_fusion.1), channel_id=1, source_target_pairs={{1,0},{2,1},{3,2},{4,3},{5,4},{6,5},{7,6},{8,7},{9,8},{10,9},{11,1... | collective-permute-start | bytes 98312 | tf_op jit(solution)/shard_map/cond/branch_1_fun/ppermute | solution.py:851
  179.8 5.7 %copy-start.24 = (bf16[256,1024]{1,0:T(8,128)(2,1)S(1)}, bf16[256,1024]{1,0:T(8,128)(2,1)}, u32[]{:S(2)}) copy-start(bf16[256,1024]{1,0:T(8,128)(2,1)} %get-tuple-element.63) | copy-start | bytes 1572868 | tf_op jit(solution)/shard_map/cond
  179.8 38.2 %all-to-all-start.4 = ((bf16[64,16,1280]{2,1,0:T(8,128)(2,1)}), bf16[64,16,1280]{2,1,0:T(8,128)(2,1)}, u32[]{:S(2)}, u32[]{:S(2)}) async-start(bf16[64,16,1280]{2,1,0:T(8,128)(2,1)} %branch_1_fun.17), calls=%async_computation.4 | async-start | bytes 5242880 | tf_op jit(solution)/shard_map/cond/branch_1_fun/all_to_all | solution.py:881
  185.5 6.3 %copy-start.17 = (bf16[256,512]{1,0:T(8,128)(2,1)S(1)}, bf16[256,512]{1,0:T(8,128)(2,1)}, u32[]{:S(2)}) copy-start(bf16[256,512]{1,0:T(8,128)(2,1)} %get-tuple-element.62) | copy-start | bytes 786436 | tf_op jit(solution)/shard_map/cond
  188.0 3.9 %collective-permute-start = (bf16[256,512]{1,0:T(8,128)(2,1)S(1)}, bf16[256,512]{1,0:T(8,128)(2,1)S(1)}, u32[]{:S(2)}, u32[]{:S(2)}) collective-permute-start(bf16[256,512]{1,0:T(8,128)(2,1)S(1)} %constant_dynamic-slice_fusion), channel_id=1, source_target_pairs={{0,64},{64,0},{1,65},{65,1},{2,66},{66,2},{3,67},{67,3},{4,68},{68... | collective-permute-start | bytes 786440 | tf_op jit(solution)/shard_map/cond/branch_1_fun/ppermute | solution.py:651
  (5 other events, 3.3 us)
Sparse Core Ops, SparseCore 0:
  71.2 179.4 all-reduce.2

commit v2 on v1

--- a/solution.py
+++ b/solution.py
@@ -282,12 +282,18 @@
     c_ref,
     cum_ref,
     seg_ref,
+    cotangent_ref,
+    normed_ref,
     gnorm_ref,
     d_mixed_ref,
     d_gate_ref,
     grad_gain_ref,
     d_start_ref,
+    grad_out_ref,
+    grad_gate_ref,
 ):
+    normed_t = normed_ref[HALO:, :].T
+    cotangent = cotangent_ref[...]
     sums = sums_ref[...] + other_ref[...]
     rate = lax.rsqrt(sums[:, 0:1] / INNER + EPSILON)
     back = rate * rate * rate * sums[:, 1:2] / INNER
@@ -314,6 +320,10 @@
         d_state = tn((d_mixed * spread_pair(entry, pair)).astype(bf16), c_low).astype(bf16)
         for side in range(2):
             d_start_ref[2 * pair + side] = d_state[side * HEAD : (side + 1) * HEAD, :]
+        if pair % 2 == 1:
+            group = slice((pair - 1) * LANES, (pair + 1) * LANES)
+            grad_out_ref[group, :] = tn(gnorm_ref[:, group], cotangent).astype(bf16)
+            grad_gate_ref[:, group] = mm(normed_t, d_gate_ref[:, group]).astype(bf16)
 
 
 def head_sums(values, pair):
@@ -641,10 +651,45 @@
     skip_ref[...] = total[:, :HEADS]
 
 
-def large_body(final_ref, gate_ref, out_ref, grad_in_ref, grad_out_ref):
-    grad_in_ref[:, 0, :] = final_ref[...].astype(f32)
-    grad_in_ref[:, 1, :] = gate_ref[...].astype(f32)
-    grad_out_ref[...] = out_ref[...].astype(f32)
+PARTS = 4
+
+
+def x_rows_body(final_ref, grad_in_ref, wide_ref, sem):
+    wide_ref[...] = final_ref[...].astype(f32)
+    copy = pltpu.make_async_copy(wide_ref, grad_in_ref.at[:, 0, :], sem)
+    copy.start()
+    copy.wait()
+
+
+def early_rows_body(
+    _, gate_ref, out_ref, grad_in_ref, grad_out_ref, low_ref, wide_ref, in_sems, out_sems
+):
+    size = D // PARTS
+    loads, stores = [], []
+    for part in range(PARTS):
+        rows = slice(part * size, (part + 1) * size)
+        for which, source in enumerate((gate_ref, out_ref)):
+            loads.append(
+                pltpu.make_async_copy(
+                    source.at[rows, :], low_ref.at[which, rows, :], in_sems.at[which, part]
+                )
+            )
+    for load in loads:
+        load.start()
+    for part in range(PARTS):
+        rows = slice(part * size, (part + 1) * size)
+        for which in range(2):
+            target = grad_out_ref.at[rows, :] if which else grad_in_ref.at[rows, 1, :]
+            loads[2 * part + which].wait()
+            wide_ref[which, rows, :] = low_ref[which, rows, :].astype(f32)
+            stores.append(
+                pltpu.make_async_copy(
+                    wide_ref.at[which, rows, :], target, out_sems.at[which, part]
+                )
+            )
+            stores[-1].start()
+    for store in stores:
+        store.wait()
 
 
 def swapped(values):
@@ -673,7 +718,6 @@
     width = hidden_in.shape[1]
     gathered = lax.all_gather(hidden_in, "tensor", axis=1, tiled=True)
     halo = lax.ppermute(gathered[ROWS - HALO :], CONTEXT, [(i, i + 1) for i in range(15)])
-    cotangent = lax.all_gather(out_grad, "tensor", axis=1, tiled=True)
     win = in_weight.reshape(D, 2 * LOCAL)
     wbc = bc_weight.reshape(D, 2 * STATE)
     bc_taps = bc_conv_weight.reshape(4, 2 * STATE)
@@ -681,7 +725,6 @@
     skip = skip_gain[None]
     step_rows = step_weight.T
     gain_row = gate_gain[None]
-    dg = nt(cotangent, out_weight)
     ext_scratch = pltpu.VMEM((ROWS + 8, LANES), f32)
     pad_scratch = pltpu.VMEM((4, ROWS + 48, LANES), f32)
     (
@@ -727,6 +770,9 @@
         scratch=[ext_scratch, pltpu.VMEM((LANES, D), bf16)],
         blocks={3: ((D, LOCAL), (0, 0))},
     )
+    late_grad, state = lax.optimization_barrier((out_grad, state))
+    cotangent = lax.all_gather(late_grad, "tensor", axis=1, tiled=True)
+    dg = nt(cotangent, out_weight)
     pieces = lax.all_to_all(state, CONTEXT, 0, 0, tiled=True)
     (gate,) = kernel_call(
         gate_proj_body,
@@ -740,6 +786,7 @@
         (pre, step, cum, b_low, c_low, segs, skip),
         cost=12_000_000,
     )
+    pieces, dg = lax.optimization_barrier((pieces, dg))
     (starts,) = kernel_call(scan_body, [((16, HEAD, STATE), bf16)], (pieces,))
     start = lax.all_to_all(starts, CONTEXT, 0, 0, tiled=True).reshape(LOCAL, STATE)
     mixed, sums = kernel_call(
@@ -747,7 +794,7 @@
         [((ROWS, LOCAL), f32), ((ROWS, LANES), f32)],
         (within, start, c_low, cum, segs, gate, dg, gain_row),
     )
-    gnorm, d_mixed, d_gate, grad_gate_gain, d_start = kernel_call(
+    gnorm, d_mixed, d_gate, grad_gate_gain, d_start, grad_out, grad_gate = kernel_call(
         gate_body,
         [
             ((ROWS, LOCAL), bf16),
@@ -755,12 +802,11 @@
             ((ROWS, LOCAL), bf16),
             ((1, LOCAL), f32),
             ((HEADS, HEAD, STATE), bf16),
+            ((LOCAL, D), bf16),
+            ((D, LOCAL), bf16),
         ],
-        (sums, swapped(sums), mixed, gate, dg, gain_row, c_low, cum, segs),
-    )
-    normed = normed_ext[HALO:]
-    grad_out = tn(gnorm, cotangent).astype(bf16)
-    grad_gate = tn(normed, d_gate).astype(bf16)
+        (sums, swapped(sums), mixed, gate, dg, gain_row, c_low, cum, segs, cotangent, normed_ext),
+    )
     grad_out, grad_gate = lax.psum((grad_out, grad_gate), EVERYONE)
     def later(
         d_start,
@@ -936,17 +982,34 @@
         ],
         (final,),
     )
-    rows = pl.BlockSpec((D // 8, LOCAL), lambda i: (i, 0))
+    anywhere = pl.BlockSpec(memory_space=pl.ANY)
+    params = pltpu.CompilerParams(vmem_limit_bytes=60 * 1024 * 1024)
+    grad_in = pl.pallas_call(
+        x_rows_body,
+        grid=(1,),
+        out_shape=jax.ShapeDtypeStruct((D, 2, LOCAL), f32),
+        in_specs=[whole((D, LOCAL))],
+        out_specs=anywhere,
+        scratch_shapes=[pltpu.VMEM((D, LOCAL), f32), pltpu.SemaphoreType.DMA],
+        compiler_params=params,
+    )(final)
     grad_in, grad_out = pl.pallas_call(
-        large_body,
-        grid=(8,),
+        early_rows_body,
         out_shape=[
             jax.ShapeDtypeStruct((D, 2, LOCAL), f32),
             jax.ShapeDtypeStruct((LOCAL, D), f32),
         ],
-        in_specs=[rows] * 3,
-        out_specs=[pl.BlockSpec((D // 8, 2, LOCAL), lambda i: (i, 0, 0)), rows],
-    )(final, grad_gate, grad_out)
+        in_specs=[anywhere] * 3,
+        out_specs=[anywhere] * 2,
+        scratch_shapes=[
+            pltpu.VMEM((2, D, LOCAL), bf16),
+            pltpu.VMEM((2, D, LOCAL), f32),
+            pltpu.SemaphoreType.DMA((2, PARTS)),
+            pltpu.SemaphoreType.DMA((2, PARTS)),
+        ],
+        input_output_aliases={0: 0},
+        compiler_params=params,
+    )(grad_in, grad_gate, grad_out)
     return (
         hidden_out,
         hidden_grad,

time: 268 us -> 258 us (0.963)
  waiting for transfers between devices: 73.5 us -> 69.4 us
  matrix products: 9.95 us -> 5.91 us
    dot_general x2 -> x0, matrix products: 4.27 us -> none  [tn(): lax.dot_general(a, b, (((0,), (0,)), ((), ())), preferred_element_type=f32)]
    psum x1, waiting for transfers between devices: 29.7 us -> 25.6 us  [shards(): grad_out, grad_gate = lax.psum((grad_out, grad_gate), EVERYONE)]
    all_to_all x1, waiting for transfers between devices: 5.75 us -> 2.17 us  [shards(): pieces = lax.all_to_all(state, CONTEXT, 0, 0, tiled=True)]
    all_to_all x1, waiting for transfers between devices: 0.01 us -> 2.94 us  [shards(): lax.all_to_all(starts, CONTEXT, 0, 0, tiled=True).reshape(LOCAL, STATE)]
    pallas_call x1 -> x2, Pallas kernels: 9.14 us -> 8.44 us  [the longest x1 4.54 us: shards(): pl.pallas_call(early_rows_body, out_shape=[jax.ShapeDtypeStruct((D, 2, LO...]
    unnamed x55 -> x45, local copies, waits for them, and re-layouts: 7.04 us -> 7.03 us
  transfers between devices with their start and end apart: 12 -> 12, of which waited for: 9 -> 10; matrix products, arithmetic and copies ran while one was open for 5% -> 6% of each run, Pallas kernels for 16% -> 18%
where the time goes in v2:
time: 258 us; the launch traced here: 257 us
  waiting for transfers between devices  69.4 us (27%)
  Pallas kernels  66 us (26%)
  blocking collectives  46.5 us (18%)
  starting transfers between devices  42.6 us (17%)
  between operations  15 us (6%)
  local copies, waits for them, and re-layouts  9.57 us (4%)
  matrix products  5.91 us (2%)
    pallas_call x16, Pallas kernels, kernel_call(): pl.pallas_call(body, grid=(1,), out_shape=[jax.ShapeDtypeStruct(shape, ki...  57.6 us
    psum x1, waiting for transfers between devices, shards(): grad_out, grad_gate = lax.psum((grad_out, grad_gate), EVERYONE)  25.6 us
    all_to_all x1, waiting for transfers between devices, later(): lax.all_to_all(spread, EVERYONE, 0, 0, tiled=True).reshape(D, LOCAL + 256)  25.5 us
    all_to_all x1, blocking collectives, later(): lax.all_to_all(bundle.reshape(DEVICES, 16, 256), EVERYONE, 0, 0, tiled=True)  25.1 us
    all_to_all x1, blocking collectives, later(): received = lax.all_to_all(d_start, CONTEXT, 0, 0, tiled=True)  15.2 us
    all_to_all x1, starting transfers between devices, later(): lax.all_to_all(grad_x.reshape(DEVICES, 16, LOCAL), EVERYONE, 0, 0, tiled=...  8.93 us
    all_to_all x1, starting transfers between devices, shards(): pieces = lax.all_to_all(state, CONTEXT, 0, 0, tiled=True)  7.48 us
    unnamed x45, local copies, waits for them, and re-layouts  7.03 us
  transfers between devices with their start and end apart: 12, of which 10 were waited for; matrix products, arithmetic and copies ran while one was open for 6% of the time, Pallas kernels for 18%

profile of v2, /device:TPU:1, one launch (start us, length us, event | category | flops | bytes accessed | tf_op | source)
XLA Modules:
  0.0 256.7 jit_solution(16788651822793994088)
XLA Ops:
  7.2 3.4 %all_gather.6.hidden_ref = bf16[256,1024]{1,0:T(8,128)(2,1)S(1)} all-gather(bf16[256,512]{1,0:T(8,128)(2,1)} %param.18), channel_id=1, replica_groups=mesh['tensor'=2,'dp'=4,'context_0'=4,'context_1'=4] {'tensor'}, dimensions={1}, use_global_device_ids=true | all-gather | bytes 786432 | tf_op jit(solution)/shard_map/all_gather | solution.py:719
  10.6 3.3 %collective-permute-start.4 = (bf16[16,1024]{1,0:T(8,128)(2,1)S(1)}, bf16[16,1024]{1,0:T(8,128)(2,1)S(1)}, u32[]{:S(2)}, u32[]{:S(2)}) collective-permute-start(bf16[16,1024]{1,0:T(8,128)(2,1)S(1)} %slice.16), channel_id=1, source_target_pairs={{0,1},{1,2},{2,3},{3,4},{4,5},{5,6},{6,7},{7,8},{8,9},{9,10},{10,1... | collective-permute-start | bytes 98312 | tf_op jit(solution)/shard_map/ppermute | solution.py:720
  14.6 1.1 copy.37
  15.8 3.8 %copy.32 = bf16[128,8,2,1024]{3,1,2,0:T(8,128)(2,1)S(1)} copy(bf16[128,8,2,1024]{3,2,1,0:T(2,128)(2,1)} %bitcast.46) | data formatting | bytes 8388608
  20.4 5.2 %shard_map.271 = (bf16[272,1024]{1,0:T(8,128)(2,1)S(1)}, f32[272,1280]{1,0:T(8,128)}, f32[256,1280]{1,0:T(8,128)S(1)}, bf16[256,128]{1,0:T(8,128)(2,1)}, bf16[25...) custom-call(bf16[256,1024]{1,0:T(8,128)(2,1)S(1)} %all_gather.6.hidd, ...), custom_call_target="tpu_custom_call" | custom-call | tf_op jit(solution)/shard_map/pallas_call | solution.py:58
  25.6 7.5 %all-to-all-start.5 = ((bf16[16,80,128]{2,1,0:T(8,128)(2,1)}), bf16[16,80,128]{2,1,0:T(8,128)(2,1)S(1)}, u32[]{:S(2)}, u32[]{:S(2)}) async-start(bf16[16,80,128]{2,1,0:T(8,128)(2,1)} %get-tuple-element.168), calls=%async_computation.5 | async-start | bytes 655360 | tf_op jit(solution)/shard_map/all_to_all | solution.py:776
  33.1 2.7 %all_gather.7.cotangent_ref = bf16[256,1024]{1,0:T(8,128)(2,1)S(1)} all-gather(bf16[256,512]{1,0:T(8,128)(2,1)S(1)} %copy-done.12), channel_id=1, replica_groups=mesh['tensor'=2,'dp'=4,'context_0'=4,'context_1'=4] {'tensor'}, dimensions={1}, use_global_device_ids=true | all-gather | bytes 786432 | tf_op jit(solution)/shard_map/all_gather | solution.py:774
  35.8 3.6 %fusion.dg_ref = f32[256,1024]{1,0:T(8,128)} fusion(bf16[256,1024]{1,0:T(8,128)(2,1)S(1)} %all_gather.7.cotangent_ref, bf16[1024,1024]{1,0:T(8,128)(2,1)} %param.32), kind=kOutput, calls=%fused_computation.6 | convolution fusion | flops 536870912 | bytes 3670016 | tf_op jit(solution)/shard_map/dot_general | solution.py:39
  39.4 2.2 all-to-all-done.5.pieces_ref
  42.4 4.8 %all-to-all-start.6 = ((bf16[16,64,128]{2,1,0:T(8,128)(2,1)}), bf16[16,64,128]{2,1,0:T(8,128)(2,1)S(1)}, u32[]{:S(2)}, u32[]{:S(2)}) async-start(bf16[16,64,128]{2,1,0:T(8,128)(2,1)} %shard_map.273), calls=%async_computation.6 | async-start | bytes 524288 | tf_op jit(solution)/shard_map/all_to_all | solution.py:791
  47.3 3.4 %shard_map.274.gate_ref = f32[256,1024]{1,0:T(8,128)} custom-call(bf16[272,1024]{1,0:T(8,128)(2,1)S(1)} %get-tuple-element.171.normed_ref, bf16[1024,2048]{1,0:T(8,128)(2,1)} %bitcast.39), custom_call_target="tpu_custom_call" | custom-call | tf_op jit(solution)/shard_map/pallas_call | solution.py:58
  50.7 1.6 shard_map.272.within_ref
  52.4 2.9 %all-to-all-done.6 = bf16[16,64,128]{2,1,0:T(8,128)(2,1)S(1)} async-done(((bf16[16,64,128]{2,1,0:T(8,128)(2,1)}), bf16[16,64,128]{2,1,0:T(8,128)(2,1)S(1)}, u32[]{:S(2)}, u32[]{:S(2)}) %all-to-all-start.6) | async-done | bytes 262176 | tf_op jit(solution)/shard_map/all_to_all | solution.py:791
  55.3 3.3 %shard_map.275 = (f32[256,1024]{1,0:T(8,128)}, f32[256,128]{1,0:T(8,128)}) custom-call(f32[256,1024]{1,0:T(8,128)S(1)} %shard_map.272.within_ref, bf16[1024,128]{1,0:T(8,128)(2,1)S(1)} %bitcast.44, bf16[256,128]{1,0:T(8,128)(2,1)S(1)} %copy-done.10, f32[256,128]{1,0:T(8,128)S(1)} %copy-done.7, s32[1,256]{1,0:T(1,128)S(1)} %bitcast.54, ...), custom_call_target="tpu_custom_call" | custom-call | tf_op jit(solution)/shard_map/pallas_call | solution.py:58
  58.6 1.5 collective-permute-start.5
  60.1 1.2 collective-permute-done.5.other_ref
  62.0 6.4 %shard_map.276 = (bf16[256,1024]{1,0:T(8,128)(2,1)}, f32[256,1024]{1,0:T(8,128)}, bf16[256,1024]{1,0:T(8,128)(2,1)}, f32[1,1024]{1,0:T(1,128)}, bf16[16,64,128]{...) custom-call(f32[256,128]{1,0:T(8,128)} %get-tuple-element.173.sums_ref, ...), custom_call_target="tpu_custom_call" | custom-call | tf_op jit(solution)/shard_map/pallas_call | solution.py:58
  68.4 1.2 slice.12
  70.2 142.5 %conditional.1 = (bf16[256,512]{1,0:T(8,128)(2,1)}, bf16[256,512]{1,0:T(8,128)(2,1)}, bf16[1024,1280]{1,0:T(8,128)(2,1)}) conditional(s32[]{:T(128)} %bitcast.6, () %tuple.19, (bf16[256,512]{1,0:T(8,128)(2,1)}, bf16[256,1024]{1,0:T(8,128)(2,1)}, bf16[1024,1024]{1,0:T(8,128)(2,1)}, s32[]{:T(128)}, f32[256,1024]{1,0:T(8,128)}, ...), branch_computations={%region_0.0_spmd, %region_1.0_spmd} | conditional | flops 537985024 | bytes 106761856 | solution.py:937
  70.3 15.2 %all_to_all.30.grads_ref = bf16[16,64,128]{2,1,0:T(8,128)(2,1)} all-to-all(bf16[16,64,128]{2,1,0:T(8,128)(2,1)} %get-tuple-element.82), channel_id=1, replica_groups=mesh['tensor'=2,'dp'=4,'context_0'=4,'context_1'=4] {'context_0','contex..., dimensions={0} | all-to-all | bytes 524288 | tf_op jit(solution)/shard_map/cond/branch_1_fun/all_to_all | solution.py:826
  85.5 1.8 branch_1_fun.10
  87.3 4.2 %all-to-all-start.1 = ((bf16[16,64,128]{2,1,0:T(8,128)(2,1)}), bf16[16,64,128]{2,1,0:T(8,128)(2,1)}, u32[]{:S(2)}, u32[]{:S(2)}) async-start(bf16[16,64,128]{2,1,0:T(8,128)(2,1)} %branch_1_fun.10), calls=%async_computation.1 | async-start | bytes 524288 | tf_op jit(solution)/shard_map/cond/branch_1_fun/all_to_all | solution.py:830
  91.5 6.2 %branch_1_fun.9 = (f32[256,1024]{1,0:T(8,128)}, f32[256,256]{1,0:T(8,128)}, f32[256,128]{1,0:T(8,128)}, f32[1,1024]{1,0:T(1,128)}) custom-call(f32[256,1024]{1,0:T(8,128)} %get-tuple-element.67.d_mixed_ref, f32[256,1280]{1,0:T(8,128)S(1)} %get-tuple-element.68.pre_ref, f32[256,1024]{1,0:T(8,128)S(1)} %get-tuple-element.70.within_ref, ...), custom_call_target="tpu_custom_call" | custom-call | bytes 20000000 | tf_op jit(solution)/shard_map/cond/branch_1_fun/pallas_call | solution.py:58
  97.8 1.4 all-to-all-done.1
  99.1 6.9 %branch_1_fun.11 = (bf16[256,256]{1,0:T(8,128)(2,1)}, bf16[272,1024]{1,0:T(8,128)(2,1)}, bf16[256,128]{1,0:T(8,128)(2,1)}, f32[8,1024]{1,0:T(8,128)}, f32[8,128]{1,0:T(8,128)}) custom-call(f32[256,1024]{1,0:T(8,128)} %get-tuple-element.67.d_mixed_ref, f32[256,1280]{1,0:T(8,128)S(1)} %get-tuple-element.68.pre_ref, f32[272,1280]{1,0:T(8,128)} %get-tuple-element.69.joined_ref, ...), custom_call_target="tpu_custom_call" | custom-call | tf_op jit(solution)/shard_map/cond/branch_1_fun/pallas_call | solution.py:58
  106.0 3.7 %branch_1_fun.16 = bf16[1024,1024]{1,0:T(8,128)(2,1)} custom-call(bf16[272,1024]{1,0:T(8,128)(2,1)S(1)} %get-tuple-element.99.normed_ref, bf16[272,1024]{1,0:T(8,128)(2,1)} %get-tuple-element.87.dx_ref), custom_call_target="tpu_custom_call" | custom-call | tf_op jit(solution)/shard_map/cond/branch_1_fun/pallas_call | solution.py:58
  109.7 8.9 %all-to-all-start.2 = ((bf16[64,16,1024]{2,1,0:T(8,128)(2,1)}), bf16[64,16,1024]{2,1,0:T(8,128)(2,1)}, u32[]{:S(2)}, u32[]{:S(2)}) async-start(bf16[64,16,1024]{2,1,0:T(8,128)(2,1)} %bitcast.41), calls=%async_computation.2 | async-start | bytes 4194304 | tf_op jit(solution)/shard_map/cond/branch_1_fun/all_to_all | solution.py:879
  118.6 2.3 collective-permute-start.1
  120.9 1.0 collective-permute-done.1.other_ref
  122.6 2.1 branch_1_fun.12
  124.7 4.9 %branch_1_fun.13.terms_ref = bf16[272,1024]{1,0:T(8,128)(2,1)} custom-call(bf16[272,1024]{1,0:T(8,128)(2,1)} %get-tuple-element.87.dx_ref, bf16[256,1024]{1,0:T(8,128)(2,1)S(1)} %copy-done.16, bf16[256,128]{1,0:T(8,128)(2,1)} %get-tuple-element.89.dst_ref, bf16[272,256]{1,0:T(8,128)(2,1)} %get-tuple-element.92.dbc_ref, ...), custom_call_target="tpu_custom_call" | custom-call | bytes 15000000 | tf_op jit(solution)/shard_map/cond/branch_1_fun/pallas_call | solution.py:58
  130.0 1.8 collective-permute-done.2.other_ref
  132.5 1.3 collective-permute-start.3
  133.8 6.6 %collective-permute-done.3.returned_ref = bf16[16,1024]{1,0:T(8,128)(2,1)S(1)} collective-permute-done((bf16[16,1024]{1,0:T(8,128)(2,1)S(1)}, bf16[16,1024]{1,0:T(8,128)(2,1)S(1)}, u32[]{:S(2)}, u32[]{:S(2)}) %collective-permute-start.3) | collective-permute-done | bytes 32800 | tf_op jit(solution)/shard_map/cond/branch_1_fun/ppermute | solution.py:897
  141.1 2.5 branch_1_fun.14
  143.6 2.2 branch_1_fun.15
  145.8 25.1 %all_to_all.31.few_ref = bf16[64,16,256]{2,1,0:T(8,128)(2,1)} all-to-all(bf16[64,16,256]{2,1,0:T(8,128)(2,1)} %bitcast.47), channel_id=1, replica_groups=mesh['tensor'=2,'dp'=4,'context_0'=4,'context_1'=4] {'dp','context_0','c..., dimensions={0} | all-to-all | bytes 1048576 | tf_op jit(solution)/shard_map/cond/branch_1_fun/all_to_all | solution.py:921
  170.9 3.6 %branch_1_fun.17 = bf16[64,16,1280]{2,1,0:T(8,128)(2,1)} custom-call(bf16[64,16,1024]{2,1,0:T(8,128)(2,1)} %all-to-all-done.2.x_ref, bf16[64,16,256]{2,1,0:T(8,128)(2,1)} %all_to_all.31.few_ref), custom_call_target="tpu_custom_call" | custom-call | tf_op jit(solution)/shard_map/cond/branch_1_fun/pallas_call | solution.py:58
  174.5 5.7 %all-to-all-start.4 = ((bf16[64,16,1280]{2,1,0:T(8,128)(2,1)}), bf16[64,16,1280]{2,1,0:T(8,128)(2,1)}, u32[]{:S(2)}, u32[]{:S(2)}) async-start(bf16[64,16,1280]{2,1,0:T(8,128)(2,1)} %branch_1_fun.17), calls=%async_computation.4 | async-start | bytes 5242880 | tf_op jit(solution)/shard_map/cond/branch_1_fun/all_to_all | solution.py:927
  180.2 2.3 convolution_convert_fusion
  182.6 2.7 %collective-permute-start = (bf16[256,512]{1,0:T(8,128)(2,1)S(1)}, bf16[256,512]{1,0:T(8,128)(2,1)S(1)}, u32[]{:S(2)}, u32[]{:S(2)}) collective-permute-start(bf16[256,512]{1,0:T(8,128)(2,1)S(1)} %constant_dynamic-slice_fusion), channel_id=1, source_target_pairs={{0,64},{64,0},{1,65},{65,1},{2,66},{66,2},{3,67},{67,3},{4,68},{68... | collective-permute-start | bytes 786440 | tf_op jit(solution)/shard_map/cond/branch_1_fun/ppermute | solution.py:696
  185.3 1.2 collective-permute-done
  186.5 0.8 add_convert_fusion
  187.3 25.5 %all-to-all-done.4 = bf16[64,16,1280]{2,1,0:T(8,128)(2,1)} async-done(((bf16[64,16,1280]{2,1,0:T(8,128)(2,1)}), bf16[64,16,1280]{2,1,0:T(8,128)(2,1)}, u32[]{:S(2)}, u32[]{:S(2)}) %all-to-all-start.4) | async-done | bytes 2621472 | tf_op jit(solution)/shard_map/cond/branch_1_fun/all_to_all | solution.py:927
  212.8 3.0 %shard_map.277 = (f32[512,2,128]{2,1,0:T(2,128)}, f32[16,1024]{1,0:T(8,128)}, f32[4,1024]{1,0:T(4,128)}, f32[1,1024]{1,0:T(1,128)}, f32[4,2,128]{2,1,0:T(2,128)}...) custom-call(bf16[1024,1280]{1,0:T(8,128)(2,1)} %get-tuple-element.18, ...), custom_call_target="tpu_custom_call" | custom-call | tf_op jit(solution)/shard_map/pallas_call | solution.py:58
  215.8 3.9 %shard_map.278._ = f32[1024,2,1024]{2,1,0:T(2,128)} custom-call(bf16[1024,1280]{1,0:T(8,128)(2,1)} %get-tuple-element.185.final_ref), custom_call_target="tpu_custom_call" | custom-call | tf_op jit(solution)/shard_map/pallas_call | solution.py:987
  219.7 25.6 %all-reduce.3.cloned.1.call-done = (bf16[1024,1024]{1,0:T(8,128)(2,1)}, bf16[1024,1024]{1,0:T(8,128)(2,1)}) async-done(((bf16[1024,1024]{1,0:T(8,128)(2,1)}, bf16[1024,1024]{1,0:T(8,128)(2,1)}), (bf16[1024,1024]{1,0:T(8,128)(2,1)}, bf16[1024,1024]{1,0:T(8,128)(2,1)})) %all-reduce.3.cloned.1.call-update) | async-done | bytes 4194320 | tf_op jit(solution)/shard_map/psum | solution.py:810
  245.3 4.5 %shard_map.279 = (f32[1024,2,1024]{2,1,0:T(2,128)}, f32[1024,1024]{1,0:T(8,128)}) custom-call(f32[1024,2,1024]{2,1,0:T(2,128)} %shard_map.278._, bf16[1024,1024]{1,0:T(8,128)(2,1)} %get-tuple-element.201.gate_ref, bf16[1024,1024]{1,0:T(8,128)(2,1)} %get-tuple-element.202.out_ref), custom_call_target="tpu_custom_call", output_to_operand_aliasing={{0}: (0, {})} | custom-call | tf_op jit(solution)/shard_map/pallas_call | solution.py:996
  (78 shorter events, 5.4 us)
Async XLA Ops:
  10.6 9.0 %copy-start.2 = (bf16[256,1024]{1,0:T(8,128)(2,1)}, bf16[256,1024]{1,0:T(8,128)(2,1)S(1)}, u32[]{:S(2)}) copy-start(bf16[256,1024]{1,0:T(8,128)(2,1)S(1)} %all_gather.6.hidden_ref) | copy-start | bytes 1572868
  10.6 9.0 %collective-permute-start.4 = (bf16[16,1024]{1,0:T(8,128)(2,1)S(1)}, bf16[16,1024]{1,0:T(8,128)(2,1)S(1)}, u32[]{:S(2)}, u32[]{:S(2)}) collective-permute-start(bf16[16,1024]{1,0:T(8,128)(2,1)S(1)} %slice.16), channel_id=1, source_target_pairs={{0,1},{1,2},{2,3},{3,4},{4,5},{5,6},{6,7},{7,8},{8,9},{9,10},{10,1... | collective-permute-start | bytes 98312 | tf_op jit(solution)/shard_map/ppermute | solution.py:720
  14.6 5.1 %copy-start.25 = (f32[1,4,2,128]{3,1,2,0:T(4,128)}, f32[1,4,2,128]{3,1,2,0:T(4,128)S(1)}, u32[]{:S(2)}) copy-start(f32[1,4,2,128]{3,1,2,0:T(4,128)S(1)} %copy.38) | copy-start | bytes 12292
  15.7 4.0 %copy-start.4 = (bf16[128,8,2,128]{3,1,2,0:T(8,128)(2,1)}, bf16[128,8,2,128]{3,1,2,0:T(8,128)(2,1)S(1)}, u32[]{:S(2)}) copy-start(bf16[128,8,2,128]{3,1,2,0:T(8,128)(2,1)S(1)} %copy.37) | copy-start | bytes 1572868
  15.7 4.6 %copy-start.17 = (bf16[1024,16]{0,1:T(8,128)(2,1)S(1)}, bf16[1024,16]{0,1:T(8,128)(2,1)}, u32[]{:S(2)}) copy-start(bf16[1024,16]{0,1:T(8,128)(2,1)} %param.23) | copy-start | bytes 98308
  15.8 4.6 %copy-start.21 = (f32[4,1024]{1,0:T(4,128)S(1)}, f32[4,1024]{1,0:T(4,128)}, u32[]{:S(2)}) copy-start(f32[4,1024]{1,0:T(4,128)} %taps_ref.1) | copy-start | bytes 49156
  15.8 4.6 %copy-start.23 = (s32[256]{0:T(256)S(1)}, s32[256]{0:T(256)}, u32[]{:S(2)}) copy-start(s32[256]{0:T(256)} %param.19) | copy-start | bytes 3076
  15.8 4.5 %copy-start.28 = (f32[1024]{0:T(1024)S(1)}, f32[1024]{0:T(1024)}, u32[]{:S(2)}) copy-start(f32[1024]{0:T(1024)} %param.20) | copy-start | bytes 12292
  15.8 4.5 %copy-start.32 = (f32[16]{0:T(128)S(1)}, f32[16]{0:T(128)}, u32[]{:S(2)}) copy-start(f32[16]{0:T(128)} %param.29) | copy-start | bytes 196
  19.6 6.0 %copy-start = (bf16[128,8,2,1024]{3,1,2,0:T(8,128)(2,1)}, bf16[128,8,2,1024]{3,1,2,0:T(8,128)(2,1)S(1)}, u32[]{:S(2)}) copy-start(bf16[128,8,2,1024]{3,1,2,0:T(8,128)(2,1)S(1)} %copy.32) | copy-start | bytes 12582916
  19.7 0.7 copy-start.26
  20.3 12.7 %copy-start.12 = (bf16[256,512]{1,0:T(8,128)(2,1)S(1)}, bf16[256,512]{1,0:T(8,128)(2,1)}, u32[]{:S(2)}) copy-start(bf16[256,512]{1,0:T(8,128)(2,1)} %param.33) | copy-start | bytes 786436
  25.6 16.0 %all-to-all-start.5 = ((bf16[16,80,128]{2,1,0:T(8,128)(2,1)}), bf16[16,80,128]{2,1,0:T(8,128)(2,1)S(1)}, u32[]{:S(2)}, u32[]{:S(2)}) async-start(bf16[16,80,128]{2,1,0:T(8,128)(2,1)} %get-tuple-element.168), calls=%async_computation.5 | async-start | bytes 655360 | tf_op jit(solution)/shard_map/all_to_all | solution.py:776
  35.8 6.6 %copy-start.6 = (bf16[256,1024]{1,0:T(8,128)(2,1)}, bf16[256,1024]{1,0:T(8,128)(2,1)S(1)}, u32[]{:S(2)}) copy-start(bf16[256,1024]{1,0:T(8,128)(2,1)S(1)} %all_gather.7.cotangent_ref) | copy-start | bytes 1572868
  41.6 9.1 %copy-start.8 = (bf16[16,80,128]{2,1,0:T(8,128)(2,1)}, bf16[16,80,128]{2,1,0:T(8,128)(2,1)S(1)}, u32[]{:S(2)}) copy-start(bf16[16,80,128]{2,1,0:T(8,128)(2,1)S(1)} %all-to-all-done.5.pieces_ref) | copy-start | bytes 983044
  42.4 12.9 %all-to-all-start.6 = ((bf16[16,64,128]{2,1,0:T(8,128)(2,1)}), bf16[16,64,128]{2,1,0:T(8,128)(2,1)S(1)}, u32[]{:S(2)}, u32[]{:S(2)}) async-start(bf16[16,64,128]{2,1,0:T(8,128)(2,1)} %shard_map.273), calls=%async_computation.6 | async-start | bytes 524288 | tf_op jit(solution)/shard_map/all_to_all | solution.py:791
  47.2 198.1 %all-reduce.3.cloned.1.call-start = ((), (), s32[]{:S(2)}) async-start(), calls=%async_computation.7 | async-start | bytes 8388608 | tf_op jit(solution)/shard_map/psum | solution.py:810
  47.2 3.4 %copy-start.7 = (f32[256,128]{1,0:T(8,128)S(1)}, f32[256,128]{1,0:T(8,128)}, u32[]{:S(2)}) copy-start(f32[256,128]{1,0:T(8,128)} %get-tuple-element.164.cum_ref) | copy-start | bytes 393220
  47.2 3.4 %copy-start.9 = (f32[256,128]{1,0:T(8,128)S(1)}, f32[256,128]{1,0:T(8,128)}, u32[]{:S(2)}) copy-start(f32[256,128]{1,0:T(8,128)} %get-tuple-element.163.step_ref) | copy-start | bytes 393220
  47.2 3.4 %copy-start.10 = (bf16[256,128]{1,0:T(8,128)(2,1)S(1)}, bf16[256,128]{1,0:T(8,128)(2,1)}, u32[]{:S(2)}) copy-start(bf16[256,128]{1,0:T(8,128)(2,1)} %get-tuple-element.166.c_ref) | copy-start | bytes 196612
  47.3 3.4 %copy-start.15 = (bf16[256,128]{1,0:T(8,128)(2,1)S(1)}, bf16[256,128]{1,0:T(8,128)(2,1)}, u32[]{:S(2)}) copy-start(bf16[256,128]{1,0:T(8,128)(2,1)} %get-tuple-element.165.b_ref) | copy-start | bytes 196612
  47.3 3.4 %copy-start.24 = (s32[256]{0:T(256)S(1)}, s32[256]{0:T(256)}, u32[]{:S(2)}) copy-start(s32[256]{0:T(256)} %param.19) | copy-start | bytes 3076
  47.3 3.4 %copy-start.30 = (f32[16]{0:T(128)S(1)}, f32[16]{0:T(128)}, u32[]{:S(2)}) copy-start(f32[16]{0:T(128)} %param.30) | copy-start | bytes 196
  58.6 2.7 %collective-permute-start.5 = (f32[256,128]{1,0:T(8,128)}, f32[256,128]{1,0:T(8,128)S(1)}, u32[]{:S(2)}, u32[]{:S(2)}) collective-permute-start(f32[256,128]{1,0:T(8,128)} %get-tuple-element.173.sums_ref), channel_id=1, source_target_pairs={{0,64},{64,0},{1,65},{65,1},{2,66},{66,2},{3,67},{67,3},{4,68},{68... | collective-permute-start | bytes 393224 | tf_op jit(solution)/shard_map/ppermute | solution.py:696
  61.3 0.7 copy-start.19
  68.4 1.9 copy-start.22
  87.3 11.8 %all-to-all-start.1 = ((bf16[16,64,128]{2,1,0:T(8,128)(2,1)}), bf16[16,64,128]{2,1,0:T(8,128)(2,1)}, u32[]{:S(2)}, u32[]{:S(2)}) async-start(bf16[16,64,128]{2,1,0:T(8,128)(2,1)} %branch_1_fun.10), calls=%async_computation.1 | async-start | bytes 524288 | tf_op jit(solution)/shard_map/cond/branch_1_fun/all_to_all | solution.py:830
  109.7 9.0 %copy-start.18 = (bf16[256,256]{1,0:T(8,128)(2,1)S(1)}, bf16[256,256]{1,0:T(8,128)(2,1)}, u32[]{:S(2)}) copy-start(bf16[256,256]{1,0:T(8,128)(2,1)} %get-tuple-element.90.own_ref) | copy-start | bytes 393220 | tf_op jit(solution)/shard_map/cond
  109.7 12.9 %copy-start.1 = (f32[272,1280]{1,0:T(8,128)S(1)}, f32[272,1280]{1,0:T(8,128)}, u32[]{:S(2)}) copy-start(f32[272,1280]{1,0:T(8,128)} %get-tuple-element.69.joined_ref) | copy-start | bytes 4177924 | tf_op jit(solution)/shard_map/cond
  109.7 36.1 %all-to-all-start.2 = ((bf16[64,16,1024]{2,1,0:T(8,128)(2,1)}), bf16[64,16,1024]{2,1,0:T(8,128)(2,1)}, u32[]{:S(2)}, u32[]{:S(2)}) async-start(bf16[64,16,1024]{2,1,0:T(8,128)(2,1)} %bitcast.41), calls=%async_computation.2 | async-start | bytes 4194304 | tf_op jit(solution)/shard_map/cond/branch_1_fun/all_to_all | solution.py:879
  118.6 6.1 %copy-start.5 = (bf16[1024,256]{1,0:T(8,128)(2,1)S(1)}, bf16[1024,256]{1,0:T(8,128)(2,1)}, u32[]{:S(2)}) copy-start(bf16[1024,256]{1,0:T(8,128)(2,1)} %get-tuple-element.95.wbc_ref) | copy-start | bytes 1572868 | tf_op jit(solution)/shard_map/cond
  118.6 6.1 %copy-start.16 = (bf16[256,1024]{1,0:T(8,128)(2,1)S(1)}, bf16[256,1024]{1,0:T(8,128)(2,1)}, u32[]{:S(2)}) copy-start(bf16[256,1024]{1,0:T(8,128)(2,1)} %get-tuple-element.88.dz_ref) | copy-start | bytes 1572868 | tf_op jit(solution)/shard_map/cond
  118.6 3.3 %collective-permute-start.1 = (bf16[256,256]{1,0:T(8,128)(2,1)S(1)}, bf16[256,256]{1,0:T(8,128)(2,1)S(1)}, u32[]{:S(2)}, u32[]{:S(2)}) collective-permute-start(bf16[256,256]{1,0:T(8,128)(2,1)S(1)} %copy-done.18), channel_id=1, source_target_pairs={{0,64},{64,0},{1,65},{65,1},{2,66},{66,2},{3,67},{67,3},{4,68},{68... | collective-permute-start | bytes 393224 | tf_op jit(solution)/shard_map/cond/branch_1_fun/ppermute | solution.py:696
  121.9 0.7 copy-start.20
  124.7 16.4 %copy-start.3 = (bf16[256,1024]{1,0:T(8,128)(2,1)S(1)}, bf16[256,1024]{1,0:T(8,128)(2,1)}, u32[]{:S(2)}) copy-start(bf16[256,1024]{1,0:T(8,128)(2,1)} %get-tuple-element.66.hidden_ref) | copy-start | bytes 1572868 | tf_op jit(solution)/shard_map/cond
  124.7 16.4 %copy-start.13 = (bf16[256,512]{1,0:T(8,128)(2,1)S(1)}, bf16[256,512]{1,0:T(8,128)(2,1)}, u32[]{:S(2)}) copy-start(bf16[256,512]{1,0:T(8,128)(2,1)} %get-tuple-element.97.out_grad_ref) | copy-start | bytes 786436 | tf_op jit(solution)/shard_map/cond
  124.7 16.4 %copy-start.29 = (f32[1024]{0:T(1024)S(1)}, f32[1024]{0:T(1024)}, u32[]{:S(2)}) copy-start(f32[1024]{0:T(1024)} %get-tuple-element.96) | copy-start | bytes 12292 | tf_op jit(solution)/shard_map/cond
  124.7 18.9 %copy-start.31 = (f32[1,1024]{1,0:T(1,128)S(1)}, f32[1,1024]{1,0:T(1,128)}, u32[]{:S(2)}) copy-start(f32[1,1024]{1,0:T(1,128)} %get-tuple-element.102.gate_gain_ref) | copy-start | bytes 12292 | tf_op jit(solution)/shard_map/cond
  129.6 2.2 collective-permute-start.2
  131.8 8.7 %copy-start.14 = (bf16[272,1024]{1,0:T(8,128)(2,1)}, bf16[272,1024]{1,0:T(8,128)(2,1)S(1)}, u32[]{:S(2)}) copy-start(bf16[272,1024]{1,0:T(8,128)(2,1)S(1)} %collective-permute-done.2.other_ref) | copy-start | bytes 1671172 | tf_op jit(solution)/shard_map/cond
  132.5 7.9 %collective-permute-start.3 = (bf16[16,1024]{1,0:T(8,128)(2,1)S(1)}, bf16[16,1024]{1,0:T(8,128)(2,1)S(1)}, u32[]{:S(2)}, u32[]{:S(2)}) collective-permute-start(bf16[16,1024]{1,0:T(8,128)(2,1)S(1)} %add_convert_fusion.1), channel_id=1, source_target_pairs={{1,0},{2,1},{3,2},{4,3},{5,4},{6,5},{7,6},{8,7},{9,8},{10,9},{11,1... | collective-permute-start | bytes 98312 | tf_op jit(solution)/shard_map/cond/branch_1_fun/ppermute | solution.py:897
  140.5 0.6 copy-start.27
  174.5 5.7 %copy-start.33 = (bf16[256,1024]{1,0:T(8,128)(2,1)S(1)}, bf16[256,1024]{1,0:T(8,128)(2,1)}, u32[]{:S(2)}) copy-start(bf16[256,1024]{1,0:T(8,128)(2,1)} %get-tuple-element.63) | copy-start | bytes 1572868 | tf_op jit(solution)/shard_map/cond
  174.5 38.3 %all-to-all-start.4 = ((bf16[64,16,1280]{2,1,0:T(8,128)(2,1)}), bf16[64,16,1280]{2,1,0:T(8,128)(2,1)}, u32[]{:S(2)}, u32[]{:S(2)}) async-start(bf16[64,16,1280]{2,1,0:T(8,128)(2,1)} %branch_1_fun.17), calls=%async_computation.4 | async-start | bytes 5242880 | tf_op jit(solution)/shard_map/cond/branch_1_fun/all_to_all | solution.py:927
  180.2 6.3 %copy-start.11 = (bf16[256,512]{1,0:T(8,128)(2,1)S(1)}, bf16[256,512]{1,0:T(8,128)(2,1)}, u32[]{:S(2)}) copy-start(bf16[256,512]{1,0:T(8,128)(2,1)} %get-tuple-element.62) | copy-start | bytes 786436 | tf_op jit(solution)/shard_map/cond
  182.6 3.9 %collective-permute-start = (bf16[256,512]{1,0:T(8,128)(2,1)S(1)}, bf16[256,512]{1,0:T(8,128)(2,1)S(1)}, u32[]{:S(2)}, u32[]{:S(2)}) collective-permute-start(bf16[256,512]{1,0:T(8,128)(2,1)S(1)} %constant_dynamic-slice_fusion), channel_id=1, source_target_pairs={{0,64},{64,0},{1,65},{65,1},{2,66},{66,2},{3,67},{67,3},{4,68},{68... | collective-permute-start | bytes 786440 | tf_op jit(solution)/shard_map/cond/branch_1_fun/ppermute | solution.py:696
Sparse Core Ops, SparseCore 0:
  68.5 176.7 all-reduce.2

commit v3 on v2

--- a/solution.py
+++ b/solution.py
@@ -54,7 +54,7 @@
     return pl.BlockSpec(shape, lambda i: index, pipeline_mode=pl.Buffered(1))
 
 
-def kernel_call(body, outs, args, scratch=(), cost=0, vmem=56, blocks={}):
+def kernel_call(body, outs, args, scratch=(), cost=0, vmem=24, blocks={}):
     return pl.pallas_call(
         body,
         grid=(1,),

time: 258 us -> 256 us (level)
  waiting for transfers between devices: 69.4 us -> 93.2 us
  Pallas kernels: 66 us -> 50.1 us
  blocking collectives: 46.5 us -> 40.8 us
  matrix products: 5.91 us -> 3.04 us
    psum x1, waiting for transfers between devices: 25.6 us -> 41.8 us  [shards(): grad_out, grad_gate = lax.psum((grad_out, grad_gate), EVERYONE)]
    pallas_call x16, Pallas kernels: 57.6 us -> 41.6 us  [kernel_call(): pl.pallas_call(body, grid=(1,), out_shape=[jax.ShapeDtypeStruct(shape, ki...]
    all_to_all x1, blocking collectives: 15.2 us -> 12.3 us  [later(): received = lax.all_to_all(d_start, CONTEXT, 0, 0, tiled=True)]
    ppermute x4, starting transfers between devices: 6.91 us -> 9.83 us  [swapped(): return lax.ppermute(values, 'tensor', [(0, 1), (1, 0)])]
    all_to_all x1, blocking collectives: 25.1 us -> 22.3 us  [later(): lax.all_to_all(bundle.reshape(DEVICES, 16, 256), EVERYONE, 0, 0, tiled=True)]
    all_to_all x1, starting transfers between devices: 8.93 us -> 6.27 us  [later(): lax.all_to_all(grad_x.reshape(DEVICES, 16, LOCAL), EVERYONE, 0, 0, tiled=...]
    unnamed x45 -> x53, local copies, waits for them, and re-layouts: 7.03 us -> 8.69 us
  transfers between devices with their start and end apart: 12 -> 12, of which waited for: 10 -> 11; matrix products, arithmetic and copies ran while one was open for 6% -> 4% of each run, Pallas kernels for 18% -> 14%
where the time goes in v3:
time: 256 us; the launch traced here: 255 us
  waiting for transfers between devices  93.2 us (36%)
  Pallas kernels  50.1 us (20%)
  starting transfers between devices  41.1 us (16%)
  blocking collectives  40.8 us (16%)
  between operations  15.1 us (6%)
  local copies, waits for them, and re-layouts  10.6 us (4%)
  matrix products  3.04 us (1%)
    psum x1, waiting for transfers between devices, shards(): grad_out, grad_gate = lax.psum((grad_out, grad_gate), EVERYONE)  41.8 us
    pallas_call x16, Pallas kernels, kernel_call(): pl.pallas_call(body, grid=(1,), out_shape=[jax.ShapeDtypeStruct(shape, ki...  41.6 us
    all_to_all x1, waiting for transfers between devices, later(): lax.all_to_all(spread, EVERYONE, 0, 0, tiled=True).reshape(D, LOCAL + 256)  27.1 us
    all_to_all x1, blocking collectives, later(): lax.all_to_all(bundle.reshape(DEVICES, 16, 256), EVERYONE, 0, 0, tiled=True)  22.3 us
    all_to_all x1, blocking collectives, later(): received = lax.all_to_all(d_start, CONTEXT, 0, 0, tiled=True)  12.3 us
    ppermute x4, starting transfers between devices, swapped(): return lax.ppermute(values, 'tensor', [(0, 1), (1, 0)])  9.83 us
    unnamed x53, local copies, waits for them, and re-layouts  8.69 us
    ppermute x1, waiting for transfers between devices, later(): lax.ppermute(halo_terms, CONTEXT, [(i + 1, i) for i in range(15)])  8.64 us
  transfers between devices with their start and end apart: 12, of which 11 were waited for; matrix products, arithmetic and copies ran while one was open for 4% of the time, Pallas kernels for 14%

profile of v3, /device:TPU:1, one launch (start us, length us, event | category | flops | bytes accessed | tf_op | source)
XLA Modules:
  0.0 255.0 jit_solution(7333351501315548754)
XLA Ops:
  7.2 3.4 %all_gather.6.hidden_ref = bf16[256,1024]{1,0:T(8,128)(2,1)S(1)} all-gather(bf16[256,512]{1,0:T(8,128)(2,1)} %param.18), channel_id=1, replica_groups=mesh['tensor'=2,'dp'=4,'context_0'=4,'context_1'=4] {'tensor'}, dimensions={1}, use_global_device_ids=true | all-gather | bytes 786432 | tf_op jit(solution)/shard_map/all_gather | solution.py:719
  10.6 3.3 %collective-permute-start.4 = (bf16[16,1024]{1,0:T(8,128)(2,1)S(1)}, bf16[16,1024]{1,0:T(8,128)(2,1)S(1)}, u32[]{:S(2)}, u32[]{:S(2)}) collective-permute-start(bf16[16,1024]{1,0:T(8,128)(2,1)S(1)} %slice.16), channel_id=1, source_target_pairs={{0,1},{1,2},{2,3},{3,4},{4,5},{5,6},{6,7},{7,8},{8,9},{9,10},{10,1... | collective-permute-start | bytes 98312 | tf_op jit(solution)/shard_map/ppermute | solution.py:720
  14.6 1.1 copy.37
  15.8 3.8 %copy.32 = bf16[128,8,2,1024]{3,1,2,0:T(8,128)(2,1)S(1)} copy(bf16[128,8,2,1024]{3,2,1,0:T(2,128)(2,1)} %bitcast.53) | data formatting | bytes 8388608
  19.8 4.3 %shard_map.271 = (bf16[272,1024]{1,0:T(8,128)(2,1)S(1)}, f32[272,1280]{1,0:T(8,128)}, f32[256,1280]{1,0:T(8,128)}, bf16[256,128]{1,0:T(8,128)(2,1)}, bf16[256,12...) custom-call(bf16[256,1024]{1,0:T(8,128)(2,1)S(1)} %all_gather.6.hidd, ...), custom_call_target="tpu_custom_call" | custom-call | tf_op jit(solution)/shard_map/pallas_call | solution.py:58
  24.1 7.5 %all-to-all-start.5 = ((bf16[16,80,128]{2,1,0:T(8,128)(2,1)}), bf16[16,80,128]{2,1,0:T(8,128)(2,1)S(1)}, u32[]{:S(2)}, u32[]{:S(2)}) async-start(bf16[16,80,128]{2,1,0:T(8,128)(2,1)} %get-tuple-element.168), calls=%async_computation.5 | async-start | bytes 655360 | tf_op jit(solution)/shard_map/all_to_all | solution.py:776
  31.6 2.7 %all_gather.7.cotangent_ref = bf16[256,1024]{1,0:T(8,128)(2,1)S(1)} all-gather(bf16[256,512]{1,0:T(8,128)(2,1)S(1)} %copy-done.25), channel_id=1, replica_groups=mesh['tensor'=2,'dp'=4,'context_0'=4,'context_1'=4] {'tensor'}, dimensions={1}, use_global_device_ids=true | all-gather | bytes 786432 | tf_op jit(solution)/shard_map/all_gather | solution.py:774
  34.3 2.3 fusion.dg_ref
  36.7 3.4 %all-to-all-done.5.pieces_ref = bf16[16,80,128]{2,1,0:T(8,128)(2,1)S(1)} async-done(((bf16[16,80,128]{2,1,0:T(8,128)(2,1)}), bf16[16,80,128]{2,1,0:T(8,128)(2,1)S(1)}, u32[]{:S(2)}, u32[]{:S(2)}) %all-to-all-start.5) | async-done | bytes 327712 | tf_op jit(solution)/shard_map/all_to_all | solution.py:776
  40.9 3.6 %all-to-all-start.6 = ((bf16[16,64,128]{2,1,0:T(8,128)(2,1)}), bf16[16,64,128]{2,1,0:T(8,128)(2,1)S(1)}, u32[]{:S(2)}, u32[]{:S(2)}) async-start(bf16[16,64,128]{2,1,0:T(8,128)(2,1)} %shard_map.273), calls=%async_computation.6 | async-start | bytes 524288 | tf_op jit(solution)/shard_map/all_to_all | solution.py:791
  44.5 2.4 shard_map.274.gate_ref
  47.0 2.6 %shard_map.272.within_ref = f32[256,1024]{1,0:T(8,128)} custom-call(f32[256,1280]{1,0:T(8,128)S(1)} %copy-done.8, f32[256,128]{1,0:T(8,128)S(1)} %copy-done.23, f32[256,128]{1,0:T(8,128)S(1)} %copy-done.18, bf16[256,128]{1,0:T(8,128)(2,1)S(1)} %copy-done.27, bf16[256,128]{1,0:T(8,128)(2,1)S(1)} %get-tuple-element.166.c_ref, s32[1,256]{1,0:T(1,128)S(1)} %bitcast.58, ...), custom_call_target="tpu_custom_call" | custom-call | bytes 12000000 | tf_op jit(solution)/shard_map/pallas_call | solution.py:58
  49.6 2.5 all-to-all-done.6
  52.1 2.2 shard_map.275
  54.3 3.1 %collective-permute-start.5 = (f32[256,128]{1,0:T(8,128)S(1)}, f32[256,128]{1,0:T(8,128)S(1)}, u32[]{:S(2)}, u32[]{:S(2)}) collective-permute-start(f32[256,128]{1,0:T(8,128)S(1)} %get-tuple-element.173.sums_ref), channel_id=1, source_target_pairs={{0,64},{64,0},{1,65},{65,1},{2,66},{66,2},{3,67},{67,3},{4,68},{68... | collective-permute-start | bytes 393224 | tf_op jit(solution)/shard_map/ppermute | solution.py:696
  57.4 1.0 collective-permute-done.5.other_ref
  58.4 2.7 %shard_map.276 = (bf16[256,1024]{1,0:T(8,128)(2,1)}, f32[256,1024]{1,0:T(8,128)}, bf16[256,1024]{1,0:T(8,128)(2,1)}, f32[1,1024]{1,0:T(1,128)}, bf16[16,64,128]{...) custom-call(f32[256,128]{1,0:T(8,128)S(1)} %get-tuple-element.173.sums_ref, ...), custom_call_target="tpu_custom_call" | custom-call | tf_op jit(solution)/shard_map/pallas_call | solution.py:58
  61.0 1.3 copy-done.1
  62.4 1.4 copy-done.2
  65.2 129.7 %conditional.1 = (bf16[256,512]{1,0:T(8,128)(2,1)}, bf16[256,512]{1,0:T(8,128)(2,1)}, bf16[1024,1280]{1,0:T(8,128)(2,1)}) conditional(s32[]{:T(128)} %bitcast.6, () %tuple.19, (bf16[256,512]{1,0:T(8,128)(2,1)}, bf16[256,1024]{1,0:T(8,128)(2,1)}, bf16[1024,1024]{1,0:T(8,128)(2,1)}, s32[]{:T(128)}, f32[256,1024]{1,0:T(8,128)}, ...), branch_computations={%region_0.0_spmd, %region_1.0_spmd} | conditional | flops 537985024 | bytes 126471808 | solution.py:937
  65.2 12.3 %all_to_all.30.grads_ref = bf16[16,64,128]{2,1,0:T(8,128)(2,1)S(1)} all-to-all(bf16[16,64,128]{2,1,0:T(8,128)(2,1)S(1)} %get-tuple-element.82), channel_id=1, replica_groups=mesh['tensor'=2,'dp'=4,'context_0'=4,'context_1'=4] {'context_0','contex..., dimensions={0} | all-to-all | bytes 524288 | tf_op jit(solution)/shard_map/cond/branch_1_fun/all_to_all | solution.py:826
  78.3 3.5 %all-to-all-start.1 = ((bf16[16,64,128]{2,1,0:T(8,128)(2,1)}), bf16[16,64,128]{2,1,0:T(8,128)(2,1)S(1)}, u32[]{:S(2)}, u32[]{:S(2)}) async-start(bf16[16,64,128]{2,1,0:T(8,128)(2,1)} %branch_1_fun.10), calls=%async_computation.1 | async-start | bytes 524288 | tf_op jit(solution)/shard_map/cond/branch_1_fun/all_to_all | solution.py:830
  81.8 5.8 %branch_1_fun.9 = (f32[256,1024]{1,0:T(8,128)S(1)}, f32[256,256]{1,0:T(8,128)S(1)}, f32[256,128]{1,0:T(8,128)S(1)}, f32[1,1024]{1,0:T(1,128)S(1)}) custom-call(f32[256,1024]{1,0:T(8,128)} %get-tuple-element.67.d_mixed_ref, f32[256,1280]{1,0:T(8,128)S(1)} %get-tuple-element.68.pre_ref, f32[256,1024]{1,0:T(8,128)} %get-tuple-element.70.within_ref, ...), custom_call_target="tpu_custom_call" | custom-call | bytes 20000000 | tf_op jit(solution)/shard_map/cond/branch_1_fun/pallas_call | solution.py:58
  87.6 3.6 %all-to-all-done.1 = bf16[16,64,128]{2,1,0:T(8,128)(2,1)S(1)} async-done(((bf16[16,64,128]{2,1,0:T(8,128)(2,1)}), bf16[16,64,128]{2,1,0:T(8,128)(2,1)S(1)}, u32[]{:S(2)}, u32[]{:S(2)}) %all-to-all-start.1) | async-done | bytes 262176 | tf_op jit(solution)/shard_map/cond/branch_1_fun/all_to_all | solution.py:830
  91.2 6.1 %branch_1_fun.11 = (bf16[256,256]{1,0:T(8,128)(2,1)S(1)}, bf16[272,1024]{1,0:T(8,128)(2,1)S(1)}, bf16[256,128]{1,0:T(8,128)(2,1)S(1)}, f32[8,1024]{1,0:T(8,128)S(1)}, f32[8,128]{1,0:T(8,128)S(1)}) custom-call(f32[256,1024]{1,0:T(8,128)} %get-tuple-element.67.d_mixed_ref, f32[256,1280]{1,0:T(8,128)} %copy-done.10, f32[272,1280]{1,0:T(8,128)} %get-tuple-element.69.joined_ref, ...), custom_call_target="tpu_custom_call" | custom-call | tf_op jit(solution)/shard_map/cond/branch_1_fun/pallas_call | solution.py:58
  97.4 1.3 branch_1_fun.16
  98.7 1.3 copy-done
  100.0 6.3 %all-to-all-start.2 = ((bf16[64,16,1024]{2,1,0:T(8,128)(2,1)}), bf16[64,16,1024]{2,1,0:T(8,128)(2,1)S(1)}, u32[]{:S(2)}, u32[]{:S(2)}) async-start(bf16[64,16,1024]{2,1,0:T(8,128)(2,1)} %bitcast.38), calls=%async_computation.2 | async-start | bytes 4194304 | tf_op jit(solution)/shard_map/cond/branch_1_fun/all_to_all | solution.py:879
  106.3 4.0 %collective-permute-start.1 = (bf16[256,256]{1,0:T(8,128)(2,1)S(1)}, bf16[256,256]{1,0:T(8,128)(2,1)S(1)}, u32[]{:S(2)}, u32[]{:S(2)}) collective-permute-start(bf16[256,256]{1,0:T(8,128)(2,1)S(1)} %get-tuple-element.90.own_ref), channel_id=1, source_target_pairs={{0,64},{64,0},{1,65},{65,1},{2,66},{66,2},{3,67},{67,3},{4,68},{68... | collective-permute-start | bytes 393224 | tf_op jit(solution)/shard_map/cond/branch_1_fun/ppermute | solution.py:696
  110.4 1.0 collective-permute-done.1.other_ref
  111.3 2.2 branch_1_fun.12
  113.6 3.9 %branch_1_fun.13.terms_ref = bf16[272,1024]{1,0:T(8,128)(2,1)S(1)} custom-call(bf16[272,1024]{1,0:T(8,128)(2,1)S(1)} %get-tuple-element.87.dx_ref, bf16[256,1024]{1,0:T(8,128)(2,1)S(1)} %copy-done.28, bf16[256,128]{1,0:T(8,128)(2,1)S(1)} %get-tuple-element.89.dst_ref, bf16[272,256]{1,0:T(8,128)(2,1)S(1)} %get-tuple-element.92.dbc_ref, ...), custom_call_target="tpu_custom_call" | custom-call | bytes 15000000 | tf_op jit(solution)/shard_map/cond/branch_1_fun/pallas_call | solution.py:58
  118.0 1.6 collective-permute-done.2.other_ref
  119.6 1.3 collective-permute-start.3
  120.9 8.6 %collective-permute-done.3.returned_ref = bf16[16,1024]{1,0:T(8,128)(2,1)S(1)} collective-permute-done((bf16[16,1024]{1,0:T(8,128)(2,1)S(1)}, bf16[16,1024]{1,0:T(8,128)(2,1)S(1)}, u32[]{:S(2)}, u32[]{:S(2)}) %collective-permute-start.3) | collective-permute-done | bytes 32800 | tf_op jit(solution)/shard_map/cond/branch_1_fun/ppermute | solution.py:897
  129.5 1.3 branch_1_fun.14
  131.3 1.5 all-to-all-done.2.x_ref
  132.8 22.3 %all_to_all.31.few_ref = bf16[64,16,256]{2,1,0:T(8,128)(2,1)S(1)} all-to-all(bf16[64,16,256]{2,1,0:T(8,128)(2,1)S(1)} %bitcast.39), channel_id=1, replica_groups=mesh['tensor'=2,'dp'=4,'context_0'=4,'context_1'=4] {'dp','context_0','c..., dimensions={0} | all-to-all | bytes 1048576 | tf_op jit(solution)/shard_map/cond/branch_1_fun/all_to_all | solution.py:921
  155.1 1.9 branch_1_fun.17
  157.0 5.8 %all-to-all-start.4 = ((bf16[64,16,1280]{2,1,0:T(8,128)(2,1)}), bf16[64,16,1280]{2,1,0:T(8,128)(2,1)}, u32[]{:S(2)}, u32[]{:S(2)}) async-start(bf16[64,16,1280]{2,1,0:T(8,128)(2,1)} %branch_1_fun.17), calls=%async_computation.4 | async-start | bytes 5242880 | tf_op jit(solution)/shard_map/cond/branch_1_fun/all_to_all | solution.py:927
  163.7 2.2 collective-permute-start
  165.9 1.2 collective-permute-done
  167.0 0.8 add_convert_fusion
  167.9 27.1 %all-to-all-done.4 = bf16[64,16,1280]{2,1,0:T(8,128)(2,1)} async-done(((bf16[64,16,1280]{2,1,0:T(8,128)(2,1)}), bf16[64,16,1280]{2,1,0:T(8,128)(2,1)}, u32[]{:S(2)}, u32[]{:S(2)}) %all-to-all-start.4) | async-done | bytes 2621472 | tf_op jit(solution)/shard_map/cond/branch_1_fun/all_to_all | solution.py:927
  194.9 2.9 %shard_map.277 = (f32[512,2,128]{2,1,0:T(2,128)}, f32[16,1024]{1,0:T(8,128)}, f32[4,1024]{1,0:T(4,128)}, f32[1,1024]{1,0:T(1,128)}, f32[4,2,128]{2,1,0:T(2,128)}...) custom-call(bf16[1024,1280]{1,0:T(8,128)(2,1)} %get-tuple-element.18, ...), custom_call_target="tpu_custom_call" | custom-call | tf_op jit(solution)/shard_map/pallas_call | solution.py:58
  197.9 3.9 %shard_map.278._ = f32[1024,2,1024]{2,1,0:T(2,128)} custom-call(bf16[1024,1280]{1,0:T(8,128)(2,1)} %get-tuple-element.185.final_ref), custom_call_target="tpu_custom_call" | custom-call | tf_op jit(solution)/shard_map/pallas_call | solution.py:987
  201.8 41.8 %all-reduce.3.cloned.1.call-done = (bf16[1024,1024]{1,0:T(8,128)(2,1)}, bf16[1024,1024]{1,0:T(8,128)(2,1)}) async-done(((bf16[1024,1024]{1,0:T(8,128)(2,1)}, bf16[1024,1024]{1,0:T(8,128)(2,1)}), (bf16[1024,1024]{1,0:T(8,128)(2,1)}, bf16[1024,1024]{1,0:T(8,128)(2,1)})) %all-reduce.3.cloned.1.call-update) | async-done | bytes 4194320 | tf_op jit(solution)/shard_map/psum | solution.py:810
  243.6 4.5 %shard_map.279 = (f32[1024,2,1024]{2,1,0:T(2,128)}, f32[1024,1024]{1,0:T(8,128)}) custom-call(f32[1024,2,1024]{2,1,0:T(2,128)} %shard_map.278._, bf16[1024,1024]{1,0:T(8,128)(2,1)} %get-tuple-element.201.gate_ref, bf16[1024,1024]{1,0:T(8,128)(2,1)} %get-tuple-element.202.out_ref), custom_call_target="tpu_custom_call", output_to_operand_aliasing={{0}: (0, {})} | custom-call | tf_op jit(solution)/shard_map/pallas_call | solution.py:996
  (86 shorter events, 4.9 us)
Async XLA Ops:
  10.6 9.1 %copy-start.14 = (bf16[256,1024]{1,0:T(8,128)(2,1)}, bf16[256,1024]{1,0:T(8,128)(2,1)S(1)}, u32[]{:S(2)}) copy-start(bf16[256,1024]{1,0:T(8,128)(2,1)S(1)} %all_gather.6.hidden_ref) | copy-start | bytes 1572868
  10.6 9.1 %collective-permute-start.4 = (bf16[16,1024]{1,0:T(8,128)(2,1)S(1)}, bf16[16,1024]{1,0:T(8,128)(2,1)S(1)}, u32[]{:S(2)}, u32[]{:S(2)}) collective-permute-start(bf16[16,1024]{1,0:T(8,128)(2,1)S(1)} %slice.16), channel_id=1, source_target_pairs={{0,1},{1,2},{2,3},{3,4},{4,5},{5,6},{6,7},{7,8},{8,9},{9,10},{10,1... | collective-permute-start | bytes 98312 | tf_op jit(solution)/shard_map/ppermute | solution.py:720
  15.7 4.0 %copy-start.16 = (bf16[128,8,2,128]{3,1,2,0:T(8,128)(2,1)}, bf16[128,8,2,128]{3,1,2,0:T(8,128)(2,1)S(1)}, u32[]{:S(2)}) copy-start(bf16[128,8,2,128]{3,1,2,0:T(8,128)(2,1)S(1)} %copy.37) | copy-start | bytes 1572868
  15.7 4.0 %copy-start.4 = (f32[1024]{0:T(1024)S(1)}, f32[1024]{0:T(1024)}, u32[]{:S(2)}) copy-start(f32[1024]{0:T(1024)} %param.25) | copy-start | bytes 12292
  15.7 4.0 %copy-start.5 = (f32[2,128]{1,0:T(2,128)S(1)}, f32[2,128]{1,0:T(2,128)}, u32[]{:S(2)}) copy-start(f32[2,128]{1,0:T(2,128)} %param.27) | copy-start | bytes 3076
  15.8 4.0 %copy-start.6 = (f32[32]{0:T(128)S(1)}, f32[32]{0:T(128)}, u32[]{:S(2)}) copy-start(f32[32]{0:T(128)} %param.28) | copy-start | bytes 388
  15.8 4.0 %copy-start.30 = (bf16[1024,16]{0,1:T(8,128)(2,1)S(1)}, bf16[1024,16]{0,1:T(8,128)(2,1)}, u32[]{:S(2)}) copy-start(bf16[1024,16]{0,1:T(8,128)(2,1)} %param.23) | copy-start | bytes 98308
  15.8 4.0 %copy-start.31 = (f32[4,1024]{1,0:T(4,128)S(1)}, f32[4,1024]{1,0:T(4,128)}, u32[]{:S(2)}) copy-start(f32[4,1024]{1,0:T(4,128)} %taps_ref.1) | copy-start | bytes 49156
  15.8 4.0 %copy-start.32 = (s32[256]{0:T(256)S(1)}, s32[256]{0:T(256)}, u32[]{:S(2)}) copy-start(s32[256]{0:T(256)} %param.19) | copy-start | bytes 3076
  15.8 4.0 %copy-start.33 = (f32[1024]{0:T(1024)S(1)}, f32[1024]{0:T(1024)}, u32[]{:S(2)}) copy-start(f32[1024]{0:T(1024)} %param.20) | copy-start | bytes 12292
  15.8 4.0 %copy-start.36 = (f32[16]{0:T(128)S(1)}, f32[16]{0:T(128)}, u32[]{:S(2)}) copy-start(f32[16]{0:T(128)} %param.29) | copy-start | bytes 196
  19.7 4.4 %copy-start.7 = (bf16[128,8,2,1024]{3,1,2,0:T(8,128)(2,1)}, bf16[128,8,2,1024]{3,1,2,0:T(8,128)(2,1)S(1)}, u32[]{:S(2)}) copy-start(bf16[128,8,2,1024]{3,1,2,0:T(8,128)(2,1)S(1)} %copy.32) | copy-start | bytes 12582916
  19.8 11.8 %copy-start.25 = (bf16[256,512]{1,0:T(8,128)(2,1)S(1)}, bf16[256,512]{1,0:T(8,128)(2,1)}, u32[]{:S(2)}) copy-start(bf16[256,512]{1,0:T(8,128)(2,1)} %param.33) | copy-start | bytes 786436
  24.1 16.0 %all-to-all-start.5 = ((bf16[16,80,128]{2,1,0:T(8,128)(2,1)}), bf16[16,80,128]{2,1,0:T(8,128)(2,1)S(1)}, u32[]{:S(2)}, u32[]{:S(2)}) async-start(bf16[16,80,128]{2,1,0:T(8,128)(2,1)} %get-tuple-element.168), calls=%async_computation.5 | async-start | bytes 655360 | tf_op jit(solution)/shard_map/all_to_all | solution.py:776
  40.0 4.4 %copy-start.20 = (bf16[16,80,128]{2,1,0:T(8,128)(2,1)}, bf16[16,80,128]{2,1,0:T(8,128)(2,1)S(1)}, u32[]{:S(2)}) copy-start(bf16[16,80,128]{2,1,0:T(8,128)(2,1)S(1)} %all-to-all-done.5.pieces_ref) | copy-start | bytes 983044
  40.9 11.2 %all-to-all-start.6 = ((bf16[16,64,128]{2,1,0:T(8,128)(2,1)}), bf16[16,64,128]{2,1,0:T(8,128)(2,1)S(1)}, u32[]{:S(2)}, u32[]{:S(2)}) async-start(bf16[16,64,128]{2,1,0:T(8,128)(2,1)} %shard_map.273), calls=%async_computation.6 | async-start | bytes 524288 | tf_op jit(solution)/shard_map/all_to_all | solution.py:791
  44.4 199.2 %all-reduce.3.cloned.1.call-start = ((), (), s32[]{:S(2)}) async-start(), calls=%async_computation.7 | async-start | bytes 8388608 | tf_op jit(solution)/shard_map/psum | solution.py:810
  44.5 2.5 copy-start.8
  44.5 2.5 copy-start.18
  44.5 2.5 copy-start.23
  44.5 2.5 copy-start.27
  44.5 2.5 copy-start.34
  47.0 5.1 %copy-start.3 = (f32[1024]{0:T(1024)S(1)}, f32[1024]{0:T(1024)}, u32[]{:S(2)}) copy-start(f32[1024]{0:T(1024)} %param.31) | copy-start | bytes 12292
  52.1 6.3 %copy-start.19 = (f32[256,128]{1,0:T(8,128)S(1)}, f32[256,128]{1,0:T(8,128)}, u32[]{:S(2)}) copy-start(f32[256,128]{1,0:T(8,128)} %get-tuple-element.164.cum_ref) | copy-start | bytes 393220
  54.3 4.1 %collective-permute-start.5 = (f32[256,128]{1,0:T(8,128)S(1)}, f32[256,128]{1,0:T(8,128)S(1)}, u32[]{:S(2)}, u32[]{:S(2)}) collective-permute-start(f32[256,128]{1,0:T(8,128)S(1)} %get-tuple-element.173.sums_ref), channel_id=1, source_target_pairs={{0,64},{64,0},{1,65},{65,1},{2,66},{66,2},{3,67},{67,3},{4,68},{68... | collective-permute-start | bytes 393224 | tf_op jit(solution)/shard_map/ppermute | solution.py:696
  62.3 1.4 copy-start.2
  63.8 1.4 copy-start.21
  63.8 1.4 copy-start.29
  65.2 16.6 %copy-start.11 = (bf16[272,1024]{1,0:T(8,128)(2,1)}, bf16[272,1024]{1,0:T(8,128)(2,1)S(1)}, u32[]{:S(2)}) copy-start(bf16[272,1024]{1,0:T(8,128)(2,1)S(1)} %get-tuple-element.99.normed_ref) | copy-start | bytes 1671172 | tf_op jit(solution)/shard_map/cond
  65.2 22.4 %copy-start.10 = (f32[256,1280]{1,0:T(8,128)}, f32[256,1280]{1,0:T(8,128)S(1)}, u32[]{:S(2)}) copy-start(f32[256,1280]{1,0:T(8,128)S(1)} %get-tuple-element.68.pre_ref) | copy-start | bytes 3932164 | tf_op jit(solution)/shard_map/cond
  78.3 13.0 %all-to-all-start.1 = ((bf16[16,64,128]{2,1,0:T(8,128)(2,1)}), bf16[16,64,128]{2,1,0:T(8,128)(2,1)S(1)}, u32[]{:S(2)}, u32[]{:S(2)}) async-start(bf16[16,64,128]{2,1,0:T(8,128)(2,1)} %branch_1_fun.10), calls=%async_computation.1 | async-start | bytes 524288 | tf_op jit(solution)/shard_map/cond/branch_1_fun/all_to_all | solution.py:830
  91.2 6.1 %copy-start.12 = (bf16[272,1024]{1,0:T(8,128)(2,1)S(1)}, bf16[272,1024]{1,0:T(8,128)(2,1)}, u32[]{:S(2)}) copy-start(bf16[272,1024]{1,0:T(8,128)(2,1)} %copy-done.11) | copy-start | bytes 1671172 | tf_op jit(solution)/shard_map/cond
  98.7 1.3 copy-start
  100.0 32.8 %all-to-all-start.2 = ((bf16[64,16,1024]{2,1,0:T(8,128)(2,1)}), bf16[64,16,1024]{2,1,0:T(8,128)(2,1)S(1)}, u32[]{:S(2)}, u32[]{:S(2)}) async-start(bf16[64,16,1024]{2,1,0:T(8,128)(2,1)} %bitcast.38), calls=%async_computation.2 | async-start | bytes 4194304 | tf_op jit(solution)/shard_map/cond/branch_1_fun/all_to_all | solution.py:879
  106.3 7.3 %copy-start.17 = (bf16[1024,256]{1,0:T(8,128)(2,1)S(1)}, bf16[1024,256]{1,0:T(8,128)(2,1)}, u32[]{:S(2)}) copy-start(bf16[1024,256]{1,0:T(8,128)(2,1)} %get-tuple-element.95.wbc_ref) | copy-start | bytes 1572868 | tf_op jit(solution)/shard_map/cond
  106.3 7.3 %copy-start.28 = (bf16[256,1024]{1,0:T(8,128)(2,1)S(1)}, bf16[256,1024]{1,0:T(8,128)(2,1)}, u32[]{:S(2)}) copy-start(bf16[256,1024]{1,0:T(8,128)(2,1)} %get-tuple-element.88.dz_ref) | copy-start | bytes 1572868 | tf_op jit(solution)/shard_map/cond
  106.3 5.0 %collective-permute-start.1 = (bf16[256,256]{1,0:T(8,128)(2,1)S(1)}, bf16[256,256]{1,0:T(8,128)(2,1)S(1)}, u32[]{:S(2)}, u32[]{:S(2)}) collective-permute-start(bf16[256,256]{1,0:T(8,128)(2,1)S(1)} %get-tuple-element.90.own_ref), channel_id=1, source_target_pairs={{0,64},{64,0},{1,65},{65,1},{2,66},{66,2},{3,67},{67,3},{4,68},{68... | collective-permute-start | bytes 393224 | tf_op jit(solution)/shard_map/cond/branch_1_fun/ppermute | solution.py:696
  113.6 16.0 %copy-start.15 = (bf16[256,1024]{1,0:T(8,128)(2,1)S(1)}, bf16[256,1024]{1,0:T(8,128)(2,1)}, u32[]{:S(2)}) copy-start(bf16[256,1024]{1,0:T(8,128)(2,1)} %get-tuple-element.66.hidden_ref) | copy-start | bytes 1572868 | tf_op jit(solution)/shard_map/cond
  113.6 15.9 %copy-start.26 = (bf16[256,512]{1,0:T(8,128)(2,1)S(1)}, bf16[256,512]{1,0:T(8,128)(2,1)}, u32[]{:S(2)}) copy-start(bf16[256,512]{1,0:T(8,128)(2,1)} %get-tuple-element.97.out_grad_ref) | copy-start | bytes 786436 | tf_op jit(solution)/shard_map/cond
  113.6 17.3 %copy-start.35 = (f32[1,1024]{1,0:T(1,128)S(1)}, f32[1,1024]{1,0:T(1,128)}, u32[]{:S(2)}) copy-start(f32[1,1024]{1,0:T(1,128)} %get-tuple-element.102.gate_gain_ref) | copy-start | bytes 12292 | tf_op jit(solution)/shard_map/cond
  117.5 13.4 %copy-start.13 = (bf16[272,1024]{1,0:T(8,128)(2,1)S(1)}, bf16[272,1024]{1,0:T(8,128)(2,1)}, u32[]{:S(2)}) copy-start(bf16[272,1024]{1,0:T(8,128)(2,1)} %copy-done.11) | copy-start | bytes 1671172 | tf_op jit(solution)/shard_map/cond
  117.5 2.1 collective-permute-start.2
  119.6 9.9 %collective-permute-start.3 = (bf16[16,1024]{1,0:T(8,128)(2,1)S(1)}, bf16[16,1024]{1,0:T(8,128)(2,1)S(1)}, u32[]{:S(2)}, u32[]{:S(2)}) collective-permute-start(bf16[16,1024]{1,0:T(8,128)(2,1)S(1)} %add_convert_fusion.1), channel_id=1, source_target_pairs={{1,0},{2,1},{3,2},{4,3},{5,4},{6,5},{7,6},{8,7},{9,8},{10,9},{11,1... | collective-permute-start | bytes 98312 | tf_op jit(solution)/shard_map/cond/branch_1_fun/ppermute | solution.py:897
  157.0 5.8 %copy-start.22 = (bf16[1024,1024]{1,0:T(8,128)(2,1)S(1)}, bf16[1024,1024]{1,0:T(8,128)(2,1)}, u32[]{:S(2)}) copy-start(bf16[1024,1024]{1,0:T(8,128)(2,1)} %get-tuple-element.64) | copy-start | bytes 6291460 | tf_op jit(solution)/shard_map/cond
  157.0 5.9 %copy-start.37 = (bf16[256,1024]{1,0:T(8,128)(2,1)S(1)}, bf16[256,1024]{1,0:T(8,128)(2,1)}, u32[]{:S(2)}) copy-start(bf16[256,1024]{1,0:T(8,128)(2,1)} %get-tuple-element.63) | copy-start | bytes 1572868 | tf_op jit(solution)/shard_map/cond
  157.0 37.9 %all-to-all-start.4 = ((bf16[64,16,1280]{2,1,0:T(8,128)(2,1)}), bf16[64,16,1280]{2,1,0:T(8,128)(2,1)}, u32[]{:S(2)}, u32[]{:S(2)}) async-start(bf16[64,16,1280]{2,1,0:T(8,128)(2,1)} %branch_1_fun.17), calls=%async_computation.4 | async-start | bytes 5242880 | tf_op jit(solution)/shard_map/cond/branch_1_fun/all_to_all | solution.py:927
  162.9 4.2 %copy-start.24 = (bf16[256,512]{1,0:T(8,128)(2,1)S(1)}, bf16[256,512]{1,0:T(8,128)(2,1)}, u32[]{:S(2)}) copy-start(bf16[256,512]{1,0:T(8,128)(2,1)} %get-tuple-element.62) | copy-start | bytes 786436 | tf_op jit(solution)/shard_map/cond
  163.7 3.4 %collective-permute-start = (bf16[256,512]{1,0:T(8,128)(2,1)S(1)}, bf16[256,512]{1,0:T(8,128)(2,1)S(1)}, u32[]{:S(2)}, u32[]{:S(2)}) collective-permute-start(bf16[256,512]{1,0:T(8,128)(2,1)S(1)} %constant_dynamic-slice_fusion), channel_id=1, source_target_pairs={{0,64},{64,0},{1,65},{65,1},{2,66},{66,2},{3,67},{67,3},{4,68},{68... | collective-permute-start | bytes 786440 | tf_op jit(solution)/shard_map/cond/branch_1_fun/ppermute | solution.py:696
  (2 other events, 2.6 us)
Sparse Core Ops, SparseCore 0:
  63.9 179.6 all-reduce.2

commit v4 on v3

--- a/solution.py
+++ b/solution.py
@@ -283,16 +283,13 @@
     cum_ref,
     seg_ref,
     cotangent_ref,
-    normed_ref,
     gnorm_ref,
     d_mixed_ref,
     d_gate_ref,
     grad_gain_ref,
     d_start_ref,
     grad_out_ref,
-    grad_gate_ref,
 ):
-    normed_t = normed_ref[HALO:, :].T
     cotangent = cotangent_ref[...]
     sums = sums_ref[...] + other_ref[...]
     rate = lax.rsqrt(sums[:, 0:1] / INNER + EPSILON)
@@ -323,7 +320,10 @@
         if pair % 2 == 1:
             group = slice((pair - 1) * LANES, (pair + 1) * LANES)
             grad_out_ref[group, :] = tn(gnorm_ref[:, group], cotangent).astype(bf16)
-            grad_gate_ref[:, group] = mm(normed_t, d_gate_ref[:, group]).astype(bf16)
+
+
+def gate_grad_body(normed_ref, d_gate_ref, grad_ref):
+    grad_ref[...] = tn(normed_ref[HALO:, :], d_gate_ref[...]).astype(bf16)
 
 
 def head_sums(values, pair):
@@ -651,7 +651,7 @@
     skip_ref[...] = total[:, :HEADS]
 
 
-PARTS = 4
+PARTS = 8
 
 
 def x_rows_body(final_ref, grad_in_ref, wide_ref, sem):
@@ -794,7 +794,7 @@
         [((ROWS, LOCAL), f32), ((ROWS, LANES), f32)],
         (within, start, c_low, cum, segs, gate, dg, gain_row),
     )
-    gnorm, d_mixed, d_gate, grad_gate_gain, d_start, grad_out, grad_gate = kernel_call(
+    gnorm, d_mixed, d_gate, grad_gate_gain, d_start, grad_out = kernel_call(
         gate_body,
         [
             ((ROWS, LOCAL), bf16),
@@ -803,10 +803,10 @@
             ((1, LOCAL), f32),
             ((HEADS, HEAD, STATE), bf16),
             ((LOCAL, D), bf16),
-            ((D, LOCAL), bf16),
         ],
-        (sums, swapped(sums), mixed, gate, dg, gain_row, c_low, cum, segs, cotangent, normed_ext),
-    )
+        (sums, swapped(sums), mixed, gate, dg, gain_row, c_low, cum, segs, cotangent),
+    )
+    (grad_gate,) = kernel_call(gate_grad_body, [((D, LOCAL), bf16)], (normed_ext, d_gate))
     grad_out, grad_gate = lax.psum((grad_out, grad_gate), EVERYONE)
     def later(
         d_start,

time: 256 us -> 257 us (level)
  Pallas kernels: 50.1 us -> 52.8 us
    pallas_call x16 -> x17, Pallas kernels: 41.6 us -> 44.4 us  [kernel_call(): pl.pallas_call(body, grid=(1,), out_shape=[jax.ShapeDtypeStruct(shape, ki...]
    unnamed x53 -> x51, local copies, waits for them, and re-layouts: 8.69 us -> 6.76 us
where the time goes in v4:
time: 257 us; the launch traced here: 256 us
  waiting for transfers between devices  93.2 us (36%)
  Pallas kernels  52.8 us (21%)
  starting transfers between devices  41.1 us (16%)
  blocking collectives  40.8 us (16%)
  between operations  15.1 us (6%)
  local copies, waits for them, and re-layouts  8.67 us (3%)
  matrix products  3.04 us (1%)
    pallas_call x17, Pallas kernels, kernel_call(): pl.pallas_call(body, grid=(1,), out_shape=[jax.ShapeDtypeStruct(shape, ki...  44.4 us
    psum x1, waiting for transfers between devices, shards(): grad_out, grad_gate = lax.psum((grad_out, grad_gate), EVERYONE)  41.8 us
    all_to_all x1, waiting for transfers between devices, later(): lax.all_to_all(spread, EVERYONE, 0, 0, tiled=True).reshape(D, LOCAL + 256)  27.1 us
    all_to_all x1, blocking collectives, later(): lax.all_to_all(bundle.reshape(DEVICES, 16, 256), EVERYONE, 0, 0, tiled=True)  22.3 us
    all_to_all x1, blocking collectives, later(): received = lax.all_to_all(d_start, CONTEXT, 0, 0, tiled=True)  12.3 us
    ppermute x4, starting transfers between devices, swapped(): return lax.ppermute(values, 'tensor', [(0, 1), (1, 0)])  9.84 us
    ppermute x1, waiting for transfers between devices, later(): lax.ppermute(halo_terms, CONTEXT, [(i + 1, i) for i in range(15)])  8.63 us
    all_to_all x1, starting transfers between devices, shards(): pieces = lax.all_to_all(state, CONTEXT, 0, 0, tiled=True)  7.48 us
  transfers between devices with their start and end apart: 12, of which 11 were waited for; matrix products, arithmetic and copies ran while one was open for 4% of the time, Pallas kernels for 14%

profile of v4, /device:TPU:1, one launch (start us, length us, event | category | flops | bytes accessed | tf_op | source)
XLA Modules:
  0.0 255.8 jit_solution(10599865447908010955)
XLA Ops:
  7.2 3.4 %all_gather.6.hidden_ref = bf16[256,1024]{1,0:T(8,128)(2,1)S(1)} all-gather(bf16[256,512]{1,0:T(8,128)(2,1)} %param.18), channel_id=1, replica_groups=mesh['tensor'=2,'dp'=4,'context_0'=4,'context_1'=4] {'tensor'}, dimensions={1}, use_global_device_ids=true | all-gather | bytes 786432 | tf_op jit(solution)/shard_map/all_gather | solution.py:719
  10.6 3.3 %collective-permute-start.4 = (bf16[16,1024]{1,0:T(8,128)(2,1)S(1)}, bf16[16,1024]{1,0:T(8,128)(2,1)S(1)}, u32[]{:S(2)}, u32[]{:S(2)}) collective-permute-start(bf16[16,1024]{1,0:T(8,128)(2,1)S(1)} %slice.16), channel_id=1, source_target_pairs={{0,1},{1,2},{2,3},{3,4},{4,5},{5,6},{6,7},{7,8},{8,9},{9,10},{10,1... | collective-permute-start | bytes 98312 | tf_op jit(solution)/shard_map/ppermute | solution.py:720
  14.6 1.1 copy.37
  15.8 3.8 %copy.32 = bf16[128,8,2,1024]{3,1,2,0:T(8,128)(2,1)S(1)} copy(bf16[128,8,2,1024]{3,2,1,0:T(2,128)(2,1)} %bitcast.53) | data formatting | bytes 8388608
  19.8 4.3 %shard_map.271 = (bf16[272,1024]{1,0:T(8,128)(2,1)S(1)}, f32[272,1280]{1,0:T(8,128)}, f32[256,1280]{1,0:T(8,128)}, bf16[256,128]{1,0:T(8,128)(2,1)}, bf16[256,12...) custom-call(bf16[256,1024]{1,0:T(8,128)(2,1)S(1)} %all_gather.6.hidd, ...), custom_call_target="tpu_custom_call" | custom-call | tf_op jit(solution)/shard_map/pallas_call | solution.py:58
  24.1 7.5 %all-to-all-start.5 = ((bf16[16,80,128]{2,1,0:T(8,128)(2,1)}), bf16[16,80,128]{2,1,0:T(8,128)(2,1)S(1)}, u32[]{:S(2)}, u32[]{:S(2)}) async-start(bf16[16,80,128]{2,1,0:T(8,128)(2,1)} %get-tuple-element.167), calls=%async_computation.5 | async-start | bytes 655360 | tf_op jit(solution)/shard_map/all_to_all | solution.py:776
  31.6 2.7 %all_gather.7.cotangent_ref = bf16[256,1024]{1,0:T(8,128)(2,1)S(1)} all-gather(bf16[256,512]{1,0:T(8,128)(2,1)S(1)} %copy-done.25), channel_id=1, replica_groups=mesh['tensor'=2,'dp'=4,'context_0'=4,'context_1'=4] {'tensor'}, dimensions={1}, use_global_device_ids=true | all-gather | bytes 786432 | tf_op jit(solution)/shard_map/all_gather | solution.py:774
  34.3 2.3 fusion.dg_ref
  36.7 3.4 %all-to-all-done.5.pieces_ref = bf16[16,80,128]{2,1,0:T(8,128)(2,1)S(1)} async-done(((bf16[16,80,128]{2,1,0:T(8,128)(2,1)}), bf16[16,80,128]{2,1,0:T(8,128)(2,1)S(1)}, u32[]{:S(2)}, u32[]{:S(2)}) %all-to-all-start.5) | async-done | bytes 327712 | tf_op jit(solution)/shard_map/all_to_all | solution.py:776
  40.1 0.8 shard_map.273
  40.9 3.6 %all-to-all-start.6 = ((bf16[16,64,128]{2,1,0:T(8,128)(2,1)}), bf16[16,64,128]{2,1,0:T(8,128)(2,1)S(1)}, u32[]{:S(2)}, u32[]{:S(2)}) async-start(bf16[16,64,128]{2,1,0:T(8,128)(2,1)} %shard_map.273), calls=%async_computation.6 | async-start | bytes 524288 | tf_op jit(solution)/shard_map/all_to_all | solution.py:791
  44.5 2.4 shard_map.274.gate_ref
  47.0 2.6 %shard_map.272.within_ref = f32[256,1024]{1,0:T(8,128)} custom-call(f32[256,1280]{1,0:T(8,128)S(1)} %copy-done.6, f32[256,128]{1,0:T(8,128)S(1)} %copy-done.23, f32[256,128]{1,0:T(8,128)S(1)} %copy-done.16, bf16[256,128]{1,0:T(8,128)(2,1)S(1)} %copy-done.27, bf16[256,128]{1,0:T(8,128)(2,1)S(1)} %get-tuple-element.165.c_ref, s32[1,256]{1,0:T(1,128)S(1)} %bitcast.58, ...), custom_call_target="tpu_custom_call" | custom-call | bytes 12000000 | tf_op jit(solution)/shard_map/pallas_call | solution.py:58
  49.6 2.5 all-to-all-done.6
  52.1 2.2 shard_map.275
  54.3 3.1 %collective-permute-start.5 = (f32[256,128]{1,0:T(8,128)S(1)}, f32[256,128]{1,0:T(8,128)S(1)}, u32[]{:S(2)}, u32[]{:S(2)}) collective-permute-start(f32[256,128]{1,0:T(8,128)S(1)} %get-tuple-element.172.sums_ref), channel_id=1, source_target_pairs={{0,64},{64,0},{1,65},{65,1},{2,66},{66,2},{3,67},{67,3},{4,68},{68... | collective-permute-start | bytes 393224 | tf_op jit(solution)/shard_map/ppermute | solution.py:696
  57.4 1.0 collective-permute-done.5.other_ref
  58.4 3.4 %shard_map.276 = (bf16[256,1024]{1,0:T(8,128)(2,1)}, f32[256,1024]{1,0:T(8,128)}, bf16[256,1024]{1,0:T(8,128)(2,1)S(1)}, f32[1,1024]{1,0:T(1,128)}, bf16[16,64,1...) custom-call(f32[256,128]{1,0:T(8,128)S(1)} %get-tuple-element.172.sums_ref, ...), custom_call_target="tpu_custom_call" | custom-call | tf_op jit(solution)/shard_map/pallas_call | solution.py:58
  62.5 2.1 shard_map.279
  66.1 129.7 %conditional.1 = (bf16[256,512]{1,0:T(8,128)(2,1)}, bf16[256,512]{1,0:T(8,128)(2,1)}, bf16[1024,1280]{1,0:T(8,128)(2,1)}) conditional(s32[]{:T(128)} %bitcast.6, () %tuple.19, (bf16[256,512]{1,0:T(8,128)(2,1)}, bf16[256,1024]{1,0:T(8,128)(2,1)}, bf16[1024,1024]{1,0:T(8,128)(2,1)}, s32[]{:T(128)}, f32[256,1024]{1,0:T(8,128)}, ...), branch_computations={%region_0.0_spmd, %region_1.0_spmd} | conditional | flops 537985024 | bytes 126471808 | solution.py:937
  66.1 12.3 %all_to_all.30.grads_ref = bf16[16,64,128]{2,1,0:T(8,128)(2,1)S(1)} all-to-all(bf16[16,64,128]{2,1,0:T(8,128)(2,1)S(1)} %get-tuple-element.82), channel_id=1, replica_groups=mesh['tensor'=2,'dp'=4,'context_0'=4,'context_1'=4] {'context_0','contex..., dimensions={0} | all-to-all | bytes 524288 | tf_op jit(solution)/shard_map/cond/branch_1_fun/all_to_all | solution.py:826
  79.1 3.5 %all-to-all-start.1 = ((bf16[16,64,128]{2,1,0:T(8,128)(2,1)}), bf16[16,64,128]{2,1,0:T(8,128)(2,1)S(1)}, u32[]{:S(2)}, u32[]{:S(2)}) async-start(bf16[16,64,128]{2,1,0:T(8,128)(2,1)} %branch_1_fun.10), calls=%async_computation.1 | async-start | bytes 524288 | tf_op jit(solution)/shard_map/cond/branch_1_fun/all_to_all | solution.py:830
  82.7 5.7 %branch_1_fun.9 = (f32[256,1024]{1,0:T(8,128)S(1)}, f32[256,256]{1,0:T(8,128)S(1)}, f32[256,128]{1,0:T(8,128)S(1)}, f32[1,1024]{1,0:T(1,128)S(1)}) custom-call(f32[256,1024]{1,0:T(8,128)} %get-tuple-element.67.d_mixed_ref, f32[256,1280]{1,0:T(8,128)S(1)} %get-tuple-element.68.pre_ref, f32[256,1024]{1,0:T(8,128)} %get-tuple-element.70.within_ref, ...), custom_call_target="tpu_custom_call" | custom-call | bytes 20000000 | tf_op jit(solution)/shard_map/cond/branch_1_fun/pallas_call | solution.py:58
  88.5 3.6 %all-to-all-done.1 = bf16[16,64,128]{2,1,0:T(8,128)(2,1)S(1)} async-done(((bf16[16,64,128]{2,1,0:T(8,128)(2,1)}), bf16[16,64,128]{2,1,0:T(8,128)(2,1)S(1)}, u32[]{:S(2)}, u32[]{:S(2)}) %all-to-all-start.1) | async-done | bytes 262176 | tf_op jit(solution)/shard_map/cond/branch_1_fun/all_to_all | solution.py:830
  92.1 6.1 %branch_1_fun.11 = (bf16[256,256]{1,0:T(8,128)(2,1)S(1)}, bf16[272,1024]{1,0:T(8,128)(2,1)S(1)}, bf16[256,128]{1,0:T(8,128)(2,1)S(1)}, f32[8,1024]{1,0:T(8,128)S(1)}, f32[8,128]{1,0:T(8,128)S(1)}) custom-call(f32[256,1024]{1,0:T(8,128)} %get-tuple-element.67.d_mixed_ref, f32[256,1280]{1,0:T(8,128)} %copy-done.8, f32[272,1280]{1,0:T(8,128)} %get-tuple-element.69.joined_ref, ...), custom_call_target="tpu_custom_call" | custom-call | tf_op jit(solution)/shard_map/cond/branch_1_fun/pallas_call | solution.py:58
  98.3 1.3 branch_1_fun.16
  99.6 1.3 copy-done
  100.9 6.3 %all-to-all-start.2 = ((bf16[64,16,1024]{2,1,0:T(8,128)(2,1)}), bf16[64,16,1024]{2,1,0:T(8,128)(2,1)S(1)}, u32[]{:S(2)}, u32[]{:S(2)}) async-start(bf16[64,16,1024]{2,1,0:T(8,128)(2,1)} %bitcast.38), calls=%async_computation.2 | async-start | bytes 4194304 | tf_op jit(solution)/shard_map/cond/branch_1_fun/all_to_all | solution.py:879
  107.2 4.0 %collective-permute-start.1 = (bf16[256,256]{1,0:T(8,128)(2,1)S(1)}, bf16[256,256]{1,0:T(8,128)(2,1)S(1)}, u32[]{:S(2)}, u32[]{:S(2)}) collective-permute-start(bf16[256,256]{1,0:T(8,128)(2,1)S(1)} %get-tuple-element.90.own_ref), channel_id=1, source_target_pairs={{0,64},{64,0},{1,65},{65,1},{2,66},{66,2},{3,67},{67,3},{4,68},{68... | collective-permute-start | bytes 393224 | tf_op jit(solution)/shard_map/cond/branch_1_fun/ppermute | solution.py:696
  111.2 1.0 collective-permute-done.1.other_ref
  112.2 2.2 branch_1_fun.12
  114.5 3.9 %branch_1_fun.13.terms_ref = bf16[272,1024]{1,0:T(8,128)(2,1)S(1)} custom-call(bf16[272,1024]{1,0:T(8,128)(2,1)S(1)} %get-tuple-element.87.dx_ref, bf16[256,1024]{1,0:T(8,128)(2,1)S(1)} %copy-done.21, bf16[256,128]{1,0:T(8,128)(2,1)S(1)} %get-tuple-element.89.dst_ref, bf16[272,256]{1,0:T(8,128)(2,1)S(1)} %get-tuple-element.92.dbc_ref, ...), custom_call_target="tpu_custom_call" | custom-call | bytes 15000000 | tf_op jit(solution)/shard_map/cond/branch_1_fun/pallas_call | solution.py:58
  118.9 1.6 collective-permute-done.2.other_ref
  120.5 1.3 collective-permute-start.3
  121.8 8.6 %collective-permute-done.3.returned_ref = bf16[16,1024]{1,0:T(8,128)(2,1)S(1)} collective-permute-done((bf16[16,1024]{1,0:T(8,128)(2,1)S(1)}, bf16[16,1024]{1,0:T(8,128)(2,1)S(1)}, u32[]{:S(2)}, u32[]{:S(2)}) %collective-permute-start.3) | collective-permute-done | bytes 32800 | tf_op jit(solution)/shard_map/cond/branch_1_fun/ppermute | solution.py:897
  130.4 1.3 branch_1_fun.14
  132.2 1.5 all-to-all-done.2.x_ref
  133.7 22.3 %all_to_all.31.few_ref = bf16[64,16,256]{2,1,0:T(8,128)(2,1)S(1)} all-to-all(bf16[64,16,256]{2,1,0:T(8,128)(2,1)S(1)} %bitcast.39), channel_id=1, replica_groups=mesh['tensor'=2,'dp'=4,'context_0'=4,'context_1'=4] {'dp','context_0','c..., dimensions={0} | all-to-all | bytes 1048576 | tf_op jit(solution)/shard_map/cond/branch_1_fun/all_to_all | solution.py:921
  156.0 1.9 branch_1_fun.17
  157.9 5.8 %all-to-all-start.4 = ((bf16[64,16,1280]{2,1,0:T(8,128)(2,1)}), bf16[64,16,1280]{2,1,0:T(8,128)(2,1)}, u32[]{:S(2)}, u32[]{:S(2)}) async-start(bf16[64,16,1280]{2,1,0:T(8,128)(2,1)} %branch_1_fun.17), calls=%async_computation.4 | async-start | bytes 5242880 | tf_op jit(solution)/shard_map/cond/branch_1_fun/all_to_all | solution.py:927
  164.5 2.2 collective-permute-start
  166.7 1.2 collective-permute-done
  167.9 0.8 add_convert_fusion
  168.7 27.1 %all-to-all-done.4 = bf16[64,16,1280]{2,1,0:T(8,128)(2,1)} async-done(((bf16[64,16,1280]{2,1,0:T(8,128)(2,1)}), bf16[64,16,1280]{2,1,0:T(8,128)(2,1)}, u32[]{:S(2)}, u32[]{:S(2)}) %all-to-all-start.4) | async-done | bytes 2621472 | tf_op jit(solution)/shard_map/cond/branch_1_fun/all_to_all | solution.py:927
  195.8 2.9 %shard_map.277 = (f32[512,2,128]{2,1,0:T(2,128)}, f32[16,1024]{1,0:T(8,128)}, f32[4,1024]{1,0:T(4,128)}, f32[1,1024]{1,0:T(1,128)}, f32[4,2,128]{2,1,0:T(2,128)}...) custom-call(bf16[1024,1280]{1,0:T(8,128)(2,1)} %get-tuple-element.18, ...), custom_call_target="tpu_custom_call" | custom-call | tf_op jit(solution)/shard_map/pallas_call | solution.py:58
  198.7 3.9 %shard_map.278._ = f32[1024,2,1024]{2,1,0:T(2,128)} custom-call(bf16[1024,1280]{1,0:T(8,128)(2,1)} %get-tuple-element.184.final_ref), custom_call_target="tpu_custom_call" | custom-call | tf_op jit(solution)/shard_map/pallas_call | solution.py:987
  202.6 41.8 %all-reduce.3.cloned.1.call-done = (bf16[1024,1024]{1,0:T(8,128)(2,1)}, bf16[1024,1024]{1,0:T(8,128)(2,1)}) async-done(((bf16[1024,1024]{1,0:T(8,128)(2,1)}, bf16[1024,1024]{1,0:T(8,128)(2,1)}), (bf16[1024,1024]{1,0:T(8,128)(2,1)}, bf16[1024,1024]{1,0:T(8,128)(2,1)})) %all-reduce.3.cloned.1.call-update) | async-done | bytes 4194320 | tf_op jit(solution)/shard_map/psum | solution.py:810
  244.4 4.5 %shard_map.280 = (f32[1024,2,1024]{2,1,0:T(2,128)}, f32[1024,1024]{1,0:T(8,128)}) custom-call(f32[1024,2,1024]{2,1,0:T(2,128)} %shard_map.278._, bf16[1024,1024]{1,0:T(8,128)(2,1)} %get-tuple-element.199.gate_ref, bf16[1024,1024]{1,0:T(8,128)(2,1)} %get-tuple-element.200.out_ref), custom_call_target="tpu_custom_call", output_to_operand_aliasing={{0}: (0, {})} | custom-call | tf_op jit(solution)/shard_map/pallas_call | solution.py:996
  (85 shorter events, 4.9 us)
Async XLA Ops:
  10.6 9.1 %copy-start.12 = (bf16[256,1024]{1,0:T(8,128)(2,1)}, bf16[256,1024]{1,0:T(8,128)(2,1)S(1)}, u32[]{:S(2)}) copy-start(bf16[256,1024]{1,0:T(8,128)(2,1)S(1)} %all_gather.6.hidden_ref) | copy-start | bytes 1572868
  10.6 9.1 %collective-permute-start.4 = (bf16[16,1024]{1,0:T(8,128)(2,1)S(1)}, bf16[16,1024]{1,0:T(8,128)(2,1)S(1)}, u32[]{:S(2)}, u32[]{:S(2)}) collective-permute-start(bf16[16,1024]{1,0:T(8,128)(2,1)S(1)} %slice.16), channel_id=1, source_target_pairs={{0,1},{1,2},{2,3},{3,4},{4,5},{5,6},{6,7},{7,8},{8,9},{9,10},{10,1... | collective-permute-start | bytes 98312 | tf_op jit(solution)/shard_map/ppermute | solution.py:720
  15.7 4.0 %copy-start.14 = (bf16[128,8,2,128]{3,1,2,0:T(8,128)(2,1)}, bf16[128,8,2,128]{3,1,2,0:T(8,128)(2,1)S(1)}, u32[]{:S(2)}) copy-start(bf16[128,8,2,128]{3,1,2,0:T(8,128)(2,1)S(1)} %copy.37) | copy-start | bytes 1572868
  15.7 4.0 %copy-start.2 = (f32[1024]{0:T(1024)S(1)}, f32[1024]{0:T(1024)}, u32[]{:S(2)}) copy-start(f32[1024]{0:T(1024)} %param.25) | copy-start | bytes 12292
  15.7 4.0 %copy-start.3 = (f32[2,128]{1,0:T(2,128)S(1)}, f32[2,128]{1,0:T(2,128)}, u32[]{:S(2)}) copy-start(f32[2,128]{1,0:T(2,128)} %param.27) | copy-start | bytes 3076
  15.8 4.0 %copy-start.4 = (f32[32]{0:T(128)S(1)}, f32[32]{0:T(128)}, u32[]{:S(2)}) copy-start(f32[32]{0:T(128)} %param.28) | copy-start | bytes 388
  15.8 4.0 %copy-start.29 = (bf16[1024,16]{0,1:T(8,128)(2,1)S(1)}, bf16[1024,16]{0,1:T(8,128)(2,1)}, u32[]{:S(2)}) copy-start(bf16[1024,16]{0,1:T(8,128)(2,1)} %param.23) | copy-start | bytes 98308
  15.8 4.0 %copy-start.30 = (f32[4,1024]{1,0:T(4,128)S(1)}, f32[4,1024]{1,0:T(4,128)}, u32[]{:S(2)}) copy-start(f32[4,1024]{1,0:T(4,128)} %taps_ref.1) | copy-start | bytes 49156
  15.8 4.0 %copy-start.31 = (s32[256]{0:T(256)S(1)}, s32[256]{0:T(256)}, u32[]{:S(2)}) copy-start(s32[256]{0:T(256)} %param.19) | copy-start | bytes 3076
  15.8 4.0 %copy-start.32 = (f32[1024]{0:T(1024)S(1)}, f32[1024]{0:T(1024)}, u32[]{:S(2)}) copy-start(f32[1024]{0:T(1024)} %param.20) | copy-start | bytes 12292
  15.8 4.0 %copy-start.35 = (f32[16]{0:T(128)S(1)}, f32[16]{0:T(128)}, u32[]{:S(2)}) copy-start(f32[16]{0:T(128)} %param.29) | copy-start | bytes 196
  19.7 4.4 %copy-start.5 = (bf16[128,8,2,1024]{3,1,2,0:T(8,128)(2,1)}, bf16[128,8,2,1024]{3,1,2,0:T(8,128)(2,1)S(1)}, u32[]{:S(2)}) copy-start(bf16[128,8,2,1024]{3,1,2,0:T(8,128)(2,1)S(1)} %copy.32) | copy-start | bytes 12582916
  19.8 11.8 %copy-start.25 = (bf16[256,512]{1,0:T(8,128)(2,1)S(1)}, bf16[256,512]{1,0:T(8,128)(2,1)}, u32[]{:S(2)}) copy-start(bf16[256,512]{1,0:T(8,128)(2,1)} %param.33) | copy-start | bytes 786436
  24.1 16.0 %all-to-all-start.5 = ((bf16[16,80,128]{2,1,0:T(8,128)(2,1)}), bf16[16,80,128]{2,1,0:T(8,128)(2,1)S(1)}, u32[]{:S(2)}, u32[]{:S(2)}) async-start(bf16[16,80,128]{2,1,0:T(8,128)(2,1)} %get-tuple-element.167), calls=%async_computation.5 | async-start | bytes 655360 | tf_op jit(solution)/shard_map/all_to_all | solution.py:776
  40.0 4.4 %copy-start.18 = (bf16[16,80,128]{2,1,0:T(8,128)(2,1)}, bf16[16,80,128]{2,1,0:T(8,128)(2,1)S(1)}, u32[]{:S(2)}) copy-start(bf16[16,80,128]{2,1,0:T(8,128)(2,1)S(1)} %all-to-all-done.5.pieces_ref) | copy-start | bytes 983044
  40.9 11.2 %all-to-all-start.6 = ((bf16[16,64,128]{2,1,0:T(8,128)(2,1)}), bf16[16,64,128]{2,1,0:T(8,128)(2,1)S(1)}, u32[]{:S(2)}, u32[]{:S(2)}) async-start(bf16[16,64,128]{2,1,0:T(8,128)(2,1)} %shard_map.273), calls=%async_computation.6 | async-start | bytes 524288 | tf_op jit(solution)/shard_map/all_to_all | solution.py:791
  44.4 200.0 %all-reduce.3.cloned.1.call-start = ((), (), s32[]{:S(2)}) async-start(), calls=%async_computation.7 | async-start | bytes 8388608 | tf_op jit(solution)/shard_map/psum | solution.py:810
  44.5 2.5 copy-start.6
  44.5 2.5 copy-start.16
  44.5 2.5 copy-start.23
  44.5 2.5 copy-start.27
  44.5 2.5 copy-start.33
  47.0 5.1 %copy-start.1 = (f32[1024]{0:T(1024)S(1)}, f32[1024]{0:T(1024)}, u32[]{:S(2)}) copy-start(f32[1024]{0:T(1024)} %param.31) | copy-start | bytes 12292
  52.1 6.3 %copy-start.17 = (f32[256,128]{1,0:T(8,128)S(1)}, f32[256,128]{1,0:T(8,128)}, u32[]{:S(2)}) copy-start(f32[256,128]{1,0:T(8,128)} %get-tuple-element.163.cum_ref) | copy-start | bytes 393220
  54.3 4.1 %collective-permute-start.5 = (f32[256,128]{1,0:T(8,128)S(1)}, f32[256,128]{1,0:T(8,128)S(1)}, u32[]{:S(2)}, u32[]{:S(2)}) collective-permute-start(f32[256,128]{1,0:T(8,128)S(1)} %get-tuple-element.172.sums_ref), channel_id=1, source_target_pairs={{0,64},{64,0},{1,65},{65,1},{2,66},{66,2},{3,67},{67,3},{4,68},{68... | collective-permute-start | bytes 393224 | tf_op jit(solution)/shard_map/ppermute | solution.py:696
  64.6 1.3 copy-start.7
  64.6 1.4 copy-start.19
  64.6 1.4 copy-start.28
  66.1 16.6 %copy-start.9 = (bf16[272,1024]{1,0:T(8,128)(2,1)}, bf16[272,1024]{1,0:T(8,128)(2,1)S(1)}, u32[]{:S(2)}) copy-start(bf16[272,1024]{1,0:T(8,128)(2,1)S(1)} %get-tuple-element.99.normed_ref) | copy-start | bytes 1671172 | tf_op jit(solution)/shard_map/cond
  66.1 22.4 %copy-start.8 = (f32[256,1280]{1,0:T(8,128)}, f32[256,1280]{1,0:T(8,128)S(1)}, u32[]{:S(2)}) copy-start(f32[256,1280]{1,0:T(8,128)S(1)} %get-tuple-element.68.pre_ref) | copy-start | bytes 3932164 | tf_op jit(solution)/shard_map/cond
  79.1 13.0 %all-to-all-start.1 = ((bf16[16,64,128]{2,1,0:T(8,128)(2,1)}), bf16[16,64,128]{2,1,0:T(8,128)(2,1)S(1)}, u32[]{:S(2)}, u32[]{:S(2)}) async-start(bf16[16,64,128]{2,1,0:T(8,128)(2,1)} %branch_1_fun.10), calls=%async_computation.1 | async-start | bytes 524288 | tf_op jit(solution)/shard_map/cond/branch_1_fun/all_to_all | solution.py:830
  92.1 6.1 %copy-start.10 = (bf16[272,1024]{1,0:T(8,128)(2,1)S(1)}, bf16[272,1024]{1,0:T(8,128)(2,1)}, u32[]{:S(2)}) copy-start(bf16[272,1024]{1,0:T(8,128)(2,1)} %copy-done.9) | copy-start | bytes 1671172 | tf_op jit(solution)/shard_map/cond
  99.6 1.3 copy-start
  100.9 32.8 %all-to-all-start.2 = ((bf16[64,16,1024]{2,1,0:T(8,128)(2,1)}), bf16[64,16,1024]{2,1,0:T(8,128)(2,1)S(1)}, u32[]{:S(2)}, u32[]{:S(2)}) async-start(bf16[64,16,1024]{2,1,0:T(8,128)(2,1)} %bitcast.38), calls=%async_computation.2 | async-start | bytes 4194304 | tf_op jit(solution)/shard_map/cond/branch_1_fun/all_to_all | solution.py:879
  107.1 7.3 %copy-start.15 = (bf16[1024,256]{1,0:T(8,128)(2,1)S(1)}, bf16[1024,256]{1,0:T(8,128)(2,1)}, u32[]{:S(2)}) copy-start(bf16[1024,256]{1,0:T(8,128)(2,1)} %get-tuple-element.95.wbc_ref) | copy-start | bytes 1572868 | tf_op jit(solution)/shard_map/cond
  107.2 7.3 %copy-start.21 = (bf16[256,1024]{1,0:T(8,128)(2,1)S(1)}, bf16[256,1024]{1,0:T(8,128)(2,1)}, u32[]{:S(2)}) copy-start(bf16[256,1024]{1,0:T(8,128)(2,1)} %get-tuple-element.88.dz_ref) | copy-start | bytes 1572868 | tf_op jit(solution)/shard_map/cond
  107.2 5.0 %collective-permute-start.1 = (bf16[256,256]{1,0:T(8,128)(2,1)S(1)}, bf16[256,256]{1,0:T(8,128)(2,1)S(1)}, u32[]{:S(2)}, u32[]{:S(2)}) collective-permute-start(bf16[256,256]{1,0:T(8,128)(2,1)S(1)} %get-tuple-element.90.own_ref), channel_id=1, source_target_pairs={{0,64},{64,0},{1,65},{65,1},{2,66},{66,2},{3,67},{67,3},{4,68},{68... | collective-permute-start | bytes 393224 | tf_op jit(solution)/shard_map/cond/branch_1_fun/ppermute | solution.py:696
  114.5 15.9 %copy-start.13 = (bf16[256,1024]{1,0:T(8,128)(2,1)S(1)}, bf16[256,1024]{1,0:T(8,128)(2,1)}, u32[]{:S(2)}) copy-start(bf16[256,1024]{1,0:T(8,128)(2,1)} %get-tuple-element.66.hidden_ref) | copy-start | bytes 1572868 | tf_op jit(solution)/shard_map/cond
  114.5 15.9 %copy-start.26 = (bf16[256,512]{1,0:T(8,128)(2,1)S(1)}, bf16[256,512]{1,0:T(8,128)(2,1)}, u32[]{:S(2)}) copy-start(bf16[256,512]{1,0:T(8,128)(2,1)} %get-tuple-element.97.out_grad_ref) | copy-start | bytes 786436 | tf_op jit(solution)/shard_map/cond
  114.5 17.3 %copy-start.34 = (f32[1,1024]{1,0:T(1,128)S(1)}, f32[1,1024]{1,0:T(1,128)}, u32[]{:S(2)}) copy-start(f32[1,1024]{1,0:T(1,128)} %get-tuple-element.102.gate_gain_ref) | copy-start | bytes 12292 | tf_op jit(solution)/shard_map/cond
  118.4 13.4 %copy-start.11 = (bf16[272,1024]{1,0:T(8,128)(2,1)S(1)}, bf16[272,1024]{1,0:T(8,128)(2,1)}, u32[]{:S(2)}) copy-start(bf16[272,1024]{1,0:T(8,128)(2,1)} %copy-done.9) | copy-start | bytes 1671172 | tf_op jit(solution)/shard_map/cond
  118.4 2.1 collective-permute-start.2
  120.5 9.9 %collective-permute-start.3 = (bf16[16,1024]{1,0:T(8,128)(2,1)S(1)}, bf16[16,1024]{1,0:T(8,128)(2,1)S(1)}, u32[]{:S(2)}, u32[]{:S(2)}) collective-permute-start(bf16[16,1024]{1,0:T(8,128)(2,1)S(1)} %add_convert_fusion.1), channel_id=1, source_target_pairs={{1,0},{2,1},{3,2},{4,3},{5,4},{6,5},{7,6},{8,7},{9,8},{10,9},{11,1... | collective-permute-start | bytes 98312 | tf_op jit(solution)/shard_map/cond/branch_1_fun/ppermute | solution.py:897
  157.9 5.9 %copy-start.22 = (bf16[1024,1024]{1,0:T(8,128)(2,1)S(1)}, bf16[1024,1024]{1,0:T(8,128)(2,1)}, u32[]{:S(2)}) copy-start(bf16[1024,1024]{1,0:T(8,128)(2,1)} %get-tuple-element.64) | copy-start | bytes 6291460 | tf_op jit(solution)/shard_map/cond
  157.9 5.9 %copy-start.36 = (bf16[256,1024]{1,0:T(8,128)(2,1)S(1)}, bf16[256,1024]{1,0:T(8,128)(2,1)}, u32[]{:S(2)}) copy-start(bf16[256,1024]{1,0:T(8,128)(2,1)} %get-tuple-element.63) | copy-start | bytes 1572868 | tf_op jit(solution)/shard_map/cond
  157.9 37.9 %all-to-all-start.4 = ((bf16[64,16,1280]{2,1,0:T(8,128)(2,1)}), bf16[64,16,1280]{2,1,0:T(8,128)(2,1)}, u32[]{:S(2)}, u32[]{:S(2)}) async-start(bf16[64,16,1280]{2,1,0:T(8,128)(2,1)} %branch_1_fun.17), calls=%async_computation.4 | async-start | bytes 5242880 | tf_op jit(solution)/shard_map/cond/branch_1_fun/all_to_all | solution.py:927
  163.7 4.2 %copy-start.24 = (bf16[256,512]{1,0:T(8,128)(2,1)S(1)}, bf16[256,512]{1,0:T(8,128)(2,1)}, u32[]{:S(2)}) copy-start(bf16[256,512]{1,0:T(8,128)(2,1)} %get-tuple-element.62) | copy-start | bytes 786436 | tf_op jit(solution)/shard_map/cond
  164.5 3.4 %collective-permute-start = (bf16[256,512]{1,0:T(8,128)(2,1)S(1)}, bf16[256,512]{1,0:T(8,128)(2,1)S(1)}, u32[]{:S(2)}, u32[]{:S(2)}) collective-permute-start(bf16[256,512]{1,0:T(8,128)(2,1)S(1)} %constant_dynamic-slice_fusion), channel_id=1, source_target_pairs={{0,64},{64,0},{1,65},{65,1},{2,66},{66,2},{3,67},{67,3},{4,68},{68... | collective-permute-start | bytes 786440 | tf_op jit(solution)/shard_map/cond/branch_1_fun/ppermute | solution.py:696
  (1 other events, 0.8 us)
Sparse Core Ops, SparseCore 0:
  64.8 179.6 all-reduce.2
